TPU v7x, 256 devices: a whole 4x4x8 slice. The times are simulated.
256 devices in a mesh: dp: 8 (over z_lo, y), tensor: 32 (over x, z_hi, core).
Axes of the slice: x: 4, y: 4, z: 8 (z_hi: 4, z_lo: 2; z = z_hi * 2 + z_lo), core: 2. Of those that a mesh axis runs over, the one named last changes fastest.
Arguments:
- tokens: bfloat16 [1024, 8192], P('dp', 'tensor'), may hold values from -20 to 20
- out_grads: bfloat16 [1024, 16384], P('dp', 'tensor'), may hold values from -20 to 20
- basis_act: bfloat16 [8192, 8192], P('dp', 'tensor'), may hold values from -0.0625 to 0.0625
- basis_grad: bfloat16 [16384, 16384], P('dp', 'tensor'), may hold values from -0.046875 to 0.046875
Outputs:
- cov_act: float32 [8192, 8192], P('tensor', 'dp')
- cov_grad: float32 [16384, 16384], P('tensor', 'dp')
- correction: float32 [8192, 16384], P('dp', 'tensor')
All inputs are finite; a program needn't handle non-finite values.
Results may differ from a plain program's by a relative error of at most 0.0009.
Values may be sent and summed in bfloat16 or wider, within the bound.
No kernel may reach another device: no remote copies, remote signals or barrier semaphores. Data moves between devices by JAX's collectives and lax.ppermute only.
A program may use at most 64 MiB of HBM per device.

v0:
```python
import itertools

import jax
import jax.numpy as jnp
from jax import lax
from jax.experimental import pallas as pl
from jax.experimental.pallas import tpu as pltpu
from jax.sharding import Mesh, PartitionSpec as P

AXES = ("zl", "y", "x", "zh", "c")
SIZES = (2, 4, 4, 4, 2)
ZL, Y, X, ZH, C = range(5)
STEPS = (0, 1, -1, 2)
ANY = pl.BlockSpec(memory_space=pl.ANY)
SCALARS = pl.BlockSpec(memory_space=pltpu.SMEM)
PARAMS = pltpu.CompilerParams(vmem_limit_bytes=48 * 1024 * 1024)


def device_index(q):
    index = 0
    for size, value in zip(SIZES, q):
        index = index * size + value
    return index


def permutation(target):
    every = itertools.product(*(range(size) for size in SIZES))
    return [(device_index(q), device_index(target(*q))) for q in every]


def shifted(value, axis, step):
    def target(*q):
        q = list(q)
        q[axis] = (q[axis] + step) % SIZES[axis]
        return q

    return lax.ppermute(value, AXES, permutation(target))


def folded(value):
    def target(zl, y, x, zh, c):
        return zl, y, (x - 1 + 2 * c) % SIZES[X], zh, c

    return lax.ppermute(value, AXES, permutation(target))


def to_group(zl, y, x, zh, c):
    row = (x & 1) * 2 + (zh >> 1)
    flip = zl ^ (x >> 1)
    return x >> 1, row, x ^ y ^ row, ((zh >> 1) ^ flip) * 2 + ((zh & 1) ^ flip), c


def x_slot(where, step):
    return ((where[X] - step) & 3) ^ (where[ZL] * 2 + (where[Y] >> 1)) ^ where[Y]


def y_slot(where, step):
    return (where[Y] - step) & 3


def z_slot(where, step):
    slot = (where[ZH] - step) & 3
    flip = (slot >> 1) ^ (where[Y] & 1)
    return flip ^ where[ZL], (slot & 1) ^ flip


def near_kernel(turned, where, *refs):
    *pieces, near, sems = refs
    copies = []
    for i, (step, piece) in enumerate(zip(STEPS, pieces)):
        zl, h = z_slot(where, step)
        tokens = piece.shape[1 if turned else 0]
        span = pl.ds(pl.multiple_of(zl * tokens, tokens), tokens)
        target = near.at[h, :, span] if turned else near.at[h, span, :]
        copies.append(pltpu.make_async_copy(piece, target, sems.at[i]))
        copies[-1].start()
    for copy in copies:
        copy.wait()


def gather_group(block, where, turned):
    block = lax.ppermute(block, AXES, permutation(to_group))
    pieces = [block if step == 0 else shifted(block, ZH, step) for step in STEPS]
    rows, columns = block.shape
    shape = (2, rows, 2 * columns) if turned else (2, 2 * rows, columns)
    near = pl.pallas_call(
        lambda *refs: near_kernel(turned, *refs),
        out_shape=jax.ShapeDtypeStruct(shape, block.dtype),
        in_specs=[SCALARS] + [ANY] * 4,
        out_specs=ANY,
        scratch_shapes=[pltpu.SemaphoreType.DMA((4,))],
        compiler_params=PARAMS,
    )(where, *pieces)
    left = shifted(near, X, 1)
    right = shifted(near, X, -1)
    far = folded(jnp.where(where[C] == 0, right, left))
    own = [near, left, right, far]
    return own + [shifted(piece, C, 1) for piece in own]


def fetch(where, pieces, panel, sems):
    copies = []
    for i, step in enumerate(STEPS):
        for j in range(2):
            copies.append(
                pltpu.make_async_copy(
                    pieces[i + 4 * j],
                    panel.at[where[C] ^ j, x_slot(where, step)],
                    sems.at[i, j],
                )
            )
            copies[-1].start()
    return copies


def dot(a, b):
    return jnp.dot(a, b, preferred_element_type=jnp.float32)


def rotate_kernel(where, *refs):
    pieces, (basis_act, basis_grad), outs = refs[:8], refs[8:10], refs[10:14]
    panel, act, grad, parts, in_sems, basis_sems, out_sems = refs[14:]
    n = act.shape[1]
    first = pltpu.make_async_copy(basis_act, act, basis_sems.at[0])
    second = pltpu.make_async_copy(basis_grad, grad, basis_sems.at[1])
    first.start()
    second.start()
    copies = fetch(where, pieces, panel, in_sems)
    first.wait()
    second.wait()
    for i, step in enumerate(STEPS):
        copies[2 * i].wait()
        copies[2 * i + 1].wait()
        slot = x_slot(where, step)
        for basis, low, k in ((act, 0, n), (grad, n, 2 * n)):
            total = None
            for h in range(2):
                for c in range(2):
                    rows = basis[(2 * h + c) * k:(2 * h + c + 1) * k, :]
                    term = dot(panel[c, slot, h, :, low:low + k], rows)
                    total = term if total is None else total + term
            parts[i, :, low:low + k] = total
        for j, y_step in enumerate(STEPS):
            @pl.when(slot == ((where[Y] + y_step) & 3))
            def _():
                pltpu.make_async_copy(parts.at[i], outs[j], out_sems.at[i]).start()
    for i in range(4):
        pltpu.make_async_copy(parts.at[i], outs[0], out_sems.at[i]).wait()


def rotate(where, pieces, basis_act, basis_grad):
    rows, k = pieces[0].shape[1:]
    f32, bf16 = jnp.float32, jnp.bfloat16
    return pl.pallas_call(
        rotate_kernel,
        out_shape=[jax.ShapeDtypeStruct((rows, k), f32)] * 4,
        in_specs=[SCALARS] + [ANY] * 10,
        out_specs=[ANY] * 4,
        scratch_shapes=[
            pltpu.VMEM((2, 4, 2, rows, k), bf16),
            pltpu.VMEM(basis_act.shape, bf16),
            pltpu.VMEM(basis_grad.shape, bf16),
            pltpu.VMEM((4, rows, k), f32),
            pltpu.SemaphoreType.DMA((4, 2)),
            pltpu.SemaphoreType.DMA((2,)),
            pltpu.SemaphoreType.DMA((4,)),
        ],
        compiler_params=PARAMS,
        cost_estimate=pl.CostEstimate(flops=3 * 10**9, bytes_accessed=12 * 10**6, transcendentals=0),
    )(where, *pieces, basis_act, basis_grad)


def covariance_kernel(where, *refs):
    pieces, mine, outs = refs[:8], refs[8:12], refs[12:14]
    panel, own, act, grad, in_sems, own_sems, out_sems = refs[14:]
    n = act.shape[1]
    tokens = mine[0].shape[1]
    copies = []
    for i, step in enumerate(STEPS):
        span = pl.ds(pl.multiple_of(y_slot(where, step) * tokens, tokens), tokens)
        copies.append(pltpu.make_async_copy(mine[i], own.at[:, span], own_sems.at[i]))
        copies[-1].start()
    copies += fetch(where, pieces, panel, in_sems)
    for copy in copies:
        copy.wait()
    scale = 1.0 / (4 * tokens)
    waits = []
    for h in range(2):
        for c in range(2):
            block = 2 * h + c
            for j, (held, out, low, k) in enumerate(((act, outs[0], 0, n), (grad, outs[1], n, 2 * n))):
                total = None
                for y in range(4):
                    term = dot(
                        own[low:low + k, y * tokens:(y + 1) * tokens],
                        panel[c, y, h, :, low:low + k],
                    )
                    total = term if total is None else total + term
                held[block] = total * scale
                waits.append(
                    pltpu.make_async_copy(
                        held.at[block], out.at[:, block * k:(block + 1) * k], out_sems.at[block, j]
                    )
                )
                waits[-1].start()
    for copy in waits:
        copy.wait()


def covariance(where, pieces, mine):
    rows, k = pieces[0].shape[1:]
    n = k // 3
    f32, bf16 = jnp.float32, jnp.bfloat16
    return pl.pallas_call(
        covariance_kernel,
        out_shape=[
            jax.ShapeDtypeStruct((n, 4 * n), f32),
            jax.ShapeDtypeStruct((2 * n, 8 * n), f32),
        ],
        in_specs=[SCALARS] + [ANY] * 12,
        out_specs=[ANY] * 2,
        scratch_shapes=[
            pltpu.VMEM((2, 4, 2, rows, k), bf16),
            pltpu.VMEM((k, 4 * rows), bf16),
            pltpu.VMEM((4, n, n), f32),
            pltpu.VMEM((4, 2 * n, 2 * n), f32),
            pltpu.SemaphoreType.DMA((4, 2)),
            pltpu.SemaphoreType.DMA((4,)),
            pltpu.SemaphoreType.DMA((4, 2)),
        ],
        compiler_params=PARAMS,
        cost_estimate=pl.CostEstimate(flops=3 * 10**9, bytes_accessed=14 * 10**6, transcendentals=0),
    )(where, *pieces, *mine)


def correction_kernel(where, *refs):
    pieces, squares, out = refs[:8], refs[8:12], refs[12]
    panel, grad, held, in_sems, grad_sems, out_sems = refs[13:]
    rows, tokens = panel.shape[3:]
    copies = fetch(where, pieces, panel, in_sems)
    for i, step in enumerate(STEPS):
        copies.append(
            pltpu.make_async_copy(squares[i], grad.at[y_slot(where, step)], grad_sems.at[i])
        )
        copies[-1].start()
    for copy in copies:
        copy.wait()
    scale = 1.0 / (4 * tokens)
    waits = []
    for h in range(2):
        for c in range(2):
            block = 2 * h + c
            total = None
            for y in range(4):
                term = dot(panel[c, y, h], grad[y])
                total = term if total is None else total + term
            held[block] = total * scale
            waits.append(
                pltpu.make_async_copy(
                    held.at[block], out.at[block * rows:(block + 1) * rows, :], out_sems.at[block]
                )
            )
            waits[-1].start()
    for copy in waits:
        copy.wait()


def correct(where, pieces, squares):
    rows, tokens = pieces[0].shape[1:]
    n = squares[0].shape[1]
    f32, bf16 = jnp.float32, jnp.bfloat16
    return pl.pallas_call(
        correction_kernel,
        out_shape=jax.ShapeDtypeStruct((4 * rows, n), f32),
        in_specs=[SCALARS] + [ANY] * 12,
        out_specs=ANY,
        scratch_shapes=[
            pltpu.VMEM((2, 4, 2, rows, tokens), bf16),
            pltpu.VMEM((4, tokens, n), bf16),
            pltpu.VMEM((4, rows, n), f32),
            pltpu.SemaphoreType.DMA((4, 2)),
            pltpu.SemaphoreType.DMA((4,)),
            pltpu.SemaphoreType.DMA((4,)),
        ],
        compiler_params=PARAMS,
        cost_estimate=pl.CostEstimate(flops=10**9, bytes_accessed=5 * 10**6, transcendentals=0),
    )(where, *pieces, *squares)


def square_kernel(part_ref, arrived_ref, act_ref, grad_ref):
    n = act_ref.shape[0]
    total = part_ref[...] + arrived_ref[...]
    square = total * total
    act_ref[...] = square[:, :n].T.astype(jnp.bfloat16)
    grad_ref[...] = square[:, n:].astype(jnp.bfloat16)


def pair_up(block, where, axis):
    other = shifted(block, ZL, 1)
    low = where[ZL] == 0
    return jnp.concatenate([jnp.where(low, block, other), jnp.where(low, other, block)], axis=axis)


def body(tokens, out_grads, basis_act, basis_grad):
    where = jnp.stack([lax.axis_index(axis) for axis in AXES]).astype(jnp.int32)
    n = tokens.shape[1]
    mine = jnp.concatenate([tokens, out_grads], axis=1)
    panel = gather_group(mine, where, False)
    turned = pair_up(mine.T, where, 1)
    own = [turned if step == 0 else shifted(turned, Y, step) for step in STEPS]
    parts = rotate(where, panel, basis_act, basis_grad)
    cov_act, cov_grad = covariance(where, panel, own)
    parts = [part.reshape(2, -1, 3 * n) for part in parts]
    parts = [part if step == 0 else shifted(part, Y, step) for step, part in zip(STEPS, parts)]

    def half(which):
        return sum(lax.dynamic_index_in_dim(part, which, 0, False) for part in parts)

    arrived = shifted(half(1 - where[ZL]), ZL, 1)
    kept = half(where[ZL])
    sq_act, sq_grad = pl.pallas_call(
        square_kernel,
        out_shape=[
            jax.ShapeDtypeStruct((n, kept.shape[0]), jnp.bfloat16),
            jax.ShapeDtypeStruct((kept.shape[0], 2 * n), jnp.bfloat16),
        ],
    )(kept, arrived)
    squares = gather_group(sq_act, where, True)
    pair = pair_up(sq_grad, where, 0)
    square_own = [pair if step == 0 else shifted(pair, Y, step) for step in STEPS]
    correction = correct(where, squares, square_own)
    return (cov_act, cov_grad, correction)


def solution(mesh):
    fine = Mesh(mesh.devices.reshape(SIZES), AXES)
    dp, tensor = ("zl", "y"), ("x", "zh", "c")
    placed = P(dp, tensor)
    return jax.shard_map(
        body,
        mesh=fine,
        in_specs=(placed,) * 4,
        out_specs=(P(tensor, dp), P(tensor, dp), placed),
        check_vma=False,
    )
```

profile of v0, /device:TPU:1, one launch (start us, length us, event | category | flops | bytes accessed | tf_op | source)
XLA Modules:
  0.0 203.6 jit_solution(3394453760108856818)
XLA Ops:
  3.4 3.9 %collective-permute-start.1 = (bf16[128,768]{0,1:T(8,128)(2,1)S(1)}, bf16[128,768]{0,1:T(8,128)(2,1)S(1)}, u32[]{:S(2)}, u32[]{:S(2)}) collective-permute-start(bf16[128,768]{0,1:T(8,128)(2,1)S(1)} %collective-permute-done), channel_id=1, source_target_pairs={{0,2},{1,3},{2,4},{3,5},{4,6},{5,7},{6,0},{7,1},{8,10},{9,11},{10,... | collective-permute-start | bytes 589832 | tf_op jit(solution)/shard_map/ppermute | solution.py:37
  7.3 12.9 %collective-permute-start.2 = (bf16[128,768]{0,1:T(8,128)(2,1)S(1)}, bf16[128,768]{0,1:T(8,128)(2,1)S(1)}, u32[]{:S(2)}, u32[]{:S(2)}) collective-permute-start(bf16[128,768]{0,1:T(8,128)(2,1)S(1)} %collective-permute-done), channel_id=1, source_target_pairs={{0,6},{1,7},{2,0},{3,1},{4,2},{5,3},{6,4},{7,5},{8,14},{9,15},{10,... | collective-permute-start | bytes 589832 | tf_op jit(solution)/shard_map/ppermute | solution.py:37
  20.2 2.7 %collective-permute-start.3 = (bf16[128,768]{0,1:T(8,128)(2,1)S(1)}, bf16[128,768]{0,1:T(8,128)(2,1)S(1)}, u32[]{:S(2)}, u32[]{:S(2)}) collective-permute-start(bf16[128,768]{0,1:T(8,128)(2,1)S(1)} %collective-permute-done), channel_id=1, source_target_pairs={{0,4},{1,5},{2,6},{3,7},{4,0},{5,1},{6,2},{7,3},{8,12},{9,13},{10,... | collective-permute-start | bytes 589832 | tf_op jit(solution)/shard_map/ppermute | solution.py:37
  24.2 6.5 %collective-permute-done.3 = bf16[128,768]{0,1:T(8,128)(2,1)S(1)} collective-permute-done((bf16[128,768]{0,1:T(8,128)(2,1)S(1)}, bf16[128,768]{0,1:T(8,128)(2,1)S(1)}, u32[]{:S(2)}, u32[]{:S(2)}) %collective-permute-start.3) | collective-permute-done | bytes 196640 | tf_op jit(solution)/shard_map/ppermute | solution.py:37
  32.4 7.7 %collective-permute-start.4 = (bf16[2,256,768]{2,1,0:T(8,128)(2,1)S(1)}, bf16[2,256,768]{2,1,0:T(8,128)(2,1)S(1)}, u32[]{:S(2)}, u32[]{:S(2)}) collective-permute-start(bf16[2,256,768]{2,1,0:T(8,128)(2,1)S(1)} %shard_map.67.refs_0_), channel_id=1, source_target_pairs={{0,8},{1,9},{2,10},{3,11},{4,12},{5,13},{6,14},{7,15},{8,16},{9,17... | collective-permute-start | bytes 2359304 | tf_op jit(solution)/shard_map/ppermute | solution.py:37
  40.1 7.5 %collective-permute-start.5 = (bf16[2,256,768]{2,1,0:T(8,128)(2,1)S(1)}, bf16[2,256,768]{2,1,0:T(8,128)(2,1)S(1)}, u32[]{:S(2)}, u32[]{:S(2)}) collective-permute-start(bf16[2,256,768]{2,1,0:T(8,128)(2,1)S(1)} %shard_map.67.refs_0_), channel_id=1, source_target_pairs={{0,24},{1,25},{2,26},{3,27},{4,28},{5,29},{6,30},{7,31},{8,0},{9,1... | collective-permute-start | bytes 2359304 | tf_op jit(solution)/shard_map/ppermute | solution.py:37
  47.6 16.8 %collective-permute-done.4.refs_1_ = bf16[2,256,768]{2,1,0:T(8,128)(2,1)S(1)} collective-permute-done((bf16[2,256,768]{2,1,0:T(8,128)(2,1)S(1)}, bf16[2,256,768]{2,1,0:T(8,128)(2,1)S(1)}, u32[]{:S(2)}, u32[]{:S(2)}) %collective-permute-start.4) | collective-permute-done | bytes 786464 | tf_op jit(solution)/shard_map/ppermute | solution.py:37
  65.2 4.1 %collective-permute-start.7 = (bf16[2,256,768]{2,1,0:T(8,128)(2,1)S(1)}, bf16[2,256,768]{2,1,0:T(8,128)(2,1)S(1)}, u32[]{:S(2)}, u32[]{:S(2)}) collective-permute-start(bf16[2,256,768]{2,1,0:T(8,128)(2,1)S(1)} %shard_map.67.refs_0_), channel_id=1, source_target_pairs={{0,1},{1,0},{2,3},{3,2},{4,5},{5,4},{6,7},{7,6},{8,9},{9,8},{10,11... | collective-permute-start | bytes 2359304 | tf_op jit(solution)/shard_map/ppermute | solution.py:37
  69.8 6.9 %collective-permute-done.6.refs_3_ = bf16[2,256,768]{2,1,0:T(8,128)(2,1)S(1)} collective-permute-done((bf16[2,256,768]{2,1,0:T(8,128)(2,1)S(1)}, bf16[2,256,768]{2,1,0:T(8,128)(2,1)S(1)}, u32[]{:S(2)}, u32[]{:S(2)}) %collective-permute-start.6) | collective-permute-done | bytes 786464 | tf_op jit(solution)/shard_map/ppermute | solution.py:44
  82.6 9.4 %shard_map.69 = (f32[256,768]{1,0:T(8,128)S(1)}, f32[256,768]{1,0:T(8,128)}, f32[256,768]{1,0:T(8,128)}, f32[256,768]{1,0:T(8,128)}) custom-call(s32[5]{0:T(128)S(1)} %stack.23.refs_0_.where, bf16[2,256,768]{2,1,0:T(8,128)(2,1)S(1)} %shard_map.67.refs_0_, bf16[2,256,768]{2,1,0:T(8,128)(2,1)S(1)} %collective-permute-done.4.refs_1_, ...), custom_call_target="tpu_custom_call" | custom-call | flops 3000000000 | bytes 12000000 | tf_op jit(solution)/shard_map/pallas_call | solution.py:154
  93.9 18.9 %collective-permute-done.17 = f32[2,128,768]{2,1,0:T(8,128)} collective-permute-done((f32[2,128,768]{2,1,0:T(8,128)}, f32[2,128,768]{2,1,0:T(8,128)}, u32[]{:S(2)}, u32[]{:S(2)}) %collective-permute-start.17) | collective-permute-done | bytes 786464 | tf_op jit(solution)/shard_map/ppermute | solution.py:37
  112.7 12.2 %collective-permute-done.16 = f32[2,128,768]{2,1,0:T(8,128)} collective-permute-done((f32[2,128,768]{2,1,0:T(8,128)}, f32[2,128,768]{2,1,0:T(8,128)}, u32[]{:S(2)}, u32[]{:S(2)}) %collective-permute-start.16) | collective-permute-done | bytes 786464 | tf_op jit(solution)/shard_map/ppermute | solution.py:37
  125.0 5.3 %collective-permute-done.15 = f32[2,128,768]{2,1,0:T(8,128)} collective-permute-done((f32[2,128,768]{2,1,0:T(8,128)}, f32[2,128,768]{2,1,0:T(8,128)}, u32[]{:S(2)}, u32[]{:S(2)}) %collective-permute-start.15) | collective-permute-done | bytes 786464 | tf_op jit(solution)/shard_map/ppermute | solution.py:37
  130.3 2.7 %add_bitcast_fusion = (f32[128,768]{1,0:T(8,128)}, f32[128,768]{1,0:T(8,128)}) fusion(f32[2,128,768]{2,1,0:T(8,128)} %collective-permute-done.17, s32[]{:T(128)S(6)} %select_n.59, f32[2,128,768]{2,1,0:T(8,128)} %collective-permute-done.16, f32[2,128,768]{2,1,0:T(8,128)} %collective-permute-done.15, f32[2,128,768]{2,1,0:T(8,128)S(1)} %bitcast.17, s32[]{:T(128)S(6)} %select_n.58), kind=kLoop, calls=%fused_computation.2 | loop fusion | flops 589824 | bytes 3932168 | tf_op jit(solution)/shard_map/add | solution.py:317
  134.9 9.2 %collective-permute-done.18.arrived_ref = f32[128,768]{1,0:T(8,128)S(1)} collective-permute-done((f32[128,768]{1,0:T(8,128)}, f32[128,768]{1,0:T(8,128)S(1)}, u32[]{:S(2)}, u32[]{:S(2)}) %collective-permute-start.18) | collective-permute-done | bytes 393248 | tf_op jit(solution)/shard_map/ppermute | solution.py:37
  151.4 3.8 %collective-permute-start.21 = (bf16[256,128]{1,0:T(8,128)(2,1)S(1)}, bf16[256,128]{1,0:T(8,128)(2,1)S(1)}, u32[]{:S(2)}, u32[]{:S(2)}) collective-permute-start(bf16[256,128]{1,0:T(8,128)(2,1)S(1)} %collective-permute-done.19.refs_1_), channel_id=1, source_target_pairs={{0,6},{1,7},{2,0},{3,1},{4,2},{5,3},{6,4},{7,5},{8,14},{9,15},{10,... | collective-permute-start | bytes 196616 | tf_op jit(solution)/shard_map/ppermute | solution.py:37
  155.2 3.5 %collective-permute-start.22 = (bf16[256,128]{1,0:T(8,128)(2,1)S(1)}, bf16[256,128]{1,0:T(8,128)(2,1)S(1)}, u32[]{:S(2)}, u32[]{:S(2)}) collective-permute-start(bf16[256,128]{1,0:T(8,128)(2,1)S(1)} %collective-permute-done.19.refs_1_), channel_id=1, source_target_pairs={{0,4},{1,5},{2,6},{3,7},{4,0},{5,1},{6,2},{7,3},{8,12},{9,13},{10,... | collective-permute-start | bytes 196616 | tf_op jit(solution)/shard_map/ppermute | solution.py:37
  158.8 3.6 %collective-permute-start.13 = (bf16[768,256]{1,0:T(8,128)(2,1)S(1)}, bf16[768,256]{1,0:T(8,128)(2,1)S(1)}, u32[]{:S(2)}, u32[]{:S(2)}) collective-permute-start(bf16[768,256]{1,0:T(8,128)(2,1)S(1)} %pad_maximum_fusion.refs_8_), channel_id=1, source_target_pairs={{0,96},{1,97},{2,98},{3,99},{4,100},{5,101},{6,102},{7,103},{8,104... | collective-permute-start | bytes 1179656 | tf_op jit(solution)/shard_map/ppermute | solution.py:37
  164.9 3.8 %collective-permute-start.23 = (bf16[2,256,256]{2,1,0:T(8,128)(2,1)S(1)}, bf16[2,256,256]{2,1,0:T(8,128)(2,1)S(1)}, u32[]{:S(2)}, u32[]{:S(2)}) collective-permute-start(bf16[2,256,256]{2,1,0:T(8,128)(2,1)S(1)} %shard_map.71.refs_0_), channel_id=1, source_target_pairs={{0,8},{1,9},{2,10},{3,11},{4,12},{5,13},{6,14},{7,15},{8,16},{9,17... | collective-permute-start | bytes 786440 | tf_op jit(solution)/shard_map/ppermute | solution.py:37
  171.3 3.9 %collective-permute-done.23.refs_1_ = bf16[2,256,256]{2,1,0:T(8,128)(2,1)S(1)} collective-permute-done((bf16[2,256,256]{2,1,0:T(8,128)(2,1)S(1)}, bf16[2,256,256]{2,1,0:T(8,128)(2,1)S(1)}, u32[]{:S(2)}, u32[]{:S(2)}) %collective-permute-start.23) | collective-permute-done | bytes 262176 | tf_op jit(solution)/shard_map/ppermute | solution.py:37
  175.2 5.8 %collective-permute-start.26 = (bf16[2,256,256]{2,1,0:T(8,128)(2,1)S(1)}, bf16[2,256,256]{2,1,0:T(8,128)(2,1)S(1)}, u32[]{:S(2)}, u32[]{:S(2)}) collective-permute-start(bf16[2,256,256]{2,1,0:T(8,128)(2,1)S(1)} %shard_map.71.refs_0_), channel_id=1, source_target_pairs={{0,1},{1,0},{2,3},{3,2},{4,5},{5,4},{6,7},{7,6},{8,9},{9,8},{10,11... | collective-permute-start | bytes 786440 | tf_op jit(solution)/shard_map/ppermute | solution.py:37
  185.4 4.4 %collective-permute-start.27 = (bf16[2,256,256]{2,1,0:T(8,128)(2,1)S(1)}, bf16[2,256,256]{2,1,0:T(8,128)(2,1)S(1)}, u32[]{:S(2)}, u32[]{:S(2)}) collective-permute-start(bf16[2,256,256]{2,1,0:T(8,128)(2,1)S(1)} %collective-permute-done.23.refs_1_), channel_id=1, source_target_pairs={{0,1},{1,0},{2,3},{3,2},{4,5},{5,4},{6,7},{7,6},{8,9},{9,8},{10,11... | collective-permute-start | bytes 786440 | tf_op jit(solution)/shard_map/ppermute | solution.py:37
  193.3 7.1 %shard_map.68 = (f32[256,1024]{1,0:T(8,128)}, f32[512,2048]{1,0:T(8,128)}) custom-call(s32[5]{0:T(128)S(1)} %stack.23.refs_0_.where, bf16[2,256,768]{2,1,0:T(8,128)(2,1)S(1)} %shard_map.67.refs_0_, bf16[2,256,768]{2,1,0:T(8,128)(2,1)S(1)} %collective-permute-done.4.refs_1_, bf16[2,256,768]{2,1,0:T(8,128)(2,1)S(1)} %collective-permute-done.5.refs_2_, ...), custom_call_target="tpu_custom_call" | custom-call | flops 3000000000 | bytes 14000000 | tf_op jit(solution)/shard_map/pallas_call | solution.py:214
  200.4 3.1 %shard_map.72 = f32[1024,512]{1,0:T(8,128)} custom-call(s32[5]{0:T(128)S(1)} %stack.23.refs_0_.where, bf16[2,256,256]{2,1,0:T(8,128)(2,1)S(1)} %shard_map.71.refs_0_, bf16[2,256,256]{2,1,0:T(8,128)(2,1)S(1)} %collective-permute-done.23.refs_1_, bf16[2,256,256]{2,1,0:T(8,128)(2,1)S(1)} %collective-permute-done.24.refs_2_, ...), custom_call_target="tpu_custom_call" | custom-call | flops 1000000000 | bytes 5000000 | tf_op jit(solution)/shard_map/pallas_call | solution.py:272
  (85 shorter events, 36.9 us)
Async XLA Ops:
  3.4 20.5 %collective-permute-start.1 = (bf16[128,768]{0,1:T(8,128)(2,1)S(1)}, bf16[128,768]{0,1:T(8,128)(2,1)S(1)}, u32[]{:S(2)}, u32[]{:S(2)}) collective-permute-start(bf16[128,768]{0,1:T(8,128)(2,1)S(1)} %collective-permute-done), channel_id=1, source_target_pairs={{0,2},{1,3},{2,4},{3,5},{4,6},{5,7},{6,0},{7,1},{8,10},{9,11},{10,... | collective-permute-start | bytes 589832 | tf_op jit(solution)/shard_map/ppermute | solution.py:37
  7.3 16.8 %collective-permute-start.2 = (bf16[128,768]{0,1:T(8,128)(2,1)S(1)}, bf16[128,768]{0,1:T(8,128)(2,1)S(1)}, u32[]{:S(2)}, u32[]{:S(2)}) collective-permute-start(bf16[128,768]{0,1:T(8,128)(2,1)S(1)} %collective-permute-done), channel_id=1, source_target_pairs={{0,6},{1,7},{2,0},{3,1},{4,2},{5,3},{6,4},{7,5},{8,14},{9,15},{10,... | collective-permute-start | bytes 589832 | tf_op jit(solution)/shard_map/ppermute | solution.py:37
  20.2 10.5 %collective-permute-start.3 = (bf16[128,768]{0,1:T(8,128)(2,1)S(1)}, bf16[128,768]{0,1:T(8,128)(2,1)S(1)}, u32[]{:S(2)}, u32[]{:S(2)}) collective-permute-start(bf16[128,768]{0,1:T(8,128)(2,1)S(1)} %collective-permute-done), channel_id=1, source_target_pairs={{0,4},{1,5},{2,6},{3,7},{4,0},{5,1},{6,2},{7,3},{8,12},{9,13},{10,... | collective-permute-start | bytes 589832 | tf_op jit(solution)/shard_map/ppermute | solution.py:37
  32.4 32.0 %collective-permute-start.4 = (bf16[2,256,768]{2,1,0:T(8,128)(2,1)S(1)}, bf16[2,256,768]{2,1,0:T(8,128)(2,1)S(1)}, u32[]{:S(2)}, u32[]{:S(2)}) collective-permute-start(bf16[2,256,768]{2,1,0:T(8,128)(2,1)S(1)} %shard_map.67.refs_0_), channel_id=1, source_target_pairs={{0,8},{1,9},{2,10},{3,11},{4,12},{5,13},{6,14},{7,15},{8,16},{9,17... | collective-permute-start | bytes 2359304 | tf_op jit(solution)/shard_map/ppermute | solution.py:37
  40.1 24.3 %collective-permute-start.5 = (bf16[2,256,768]{2,1,0:T(8,128)(2,1)S(1)}, bf16[2,256,768]{2,1,0:T(8,128)(2,1)S(1)}, u32[]{:S(2)}, u32[]{:S(2)}) collective-permute-start(bf16[2,256,768]{2,1,0:T(8,128)(2,1)S(1)} %shard_map.67.refs_0_), channel_id=1, source_target_pairs={{0,24},{1,25},{2,26},{3,27},{4,28},{5,29},{6,30},{7,31},{8,0},{9,1... | collective-permute-start | bytes 2359304 | tf_op jit(solution)/shard_map/ppermute | solution.py:37
  64.5 12.1 %collective-permute-start.6 = (bf16[2,256,768]{2,1,0:T(8,128)(2,1)S(1)}, bf16[2,256,768]{2,1,0:T(8,128)(2,1)S(1)}, u32[]{:S(2)}, u32[]{:S(2)}) collective-permute-start(bf16[2,256,768]{2,1,0:T(8,128)(2,1)S(1)} %broadcast_select_fusion), channel_id=1, source_target_pairs={{0,24},{1,9},{2,26},{3,11},{4,28},{5,13},{6,30},{7,15},{8,0},{9,17... | collective-permute-start | bytes 2359304 | tf_op jit(solution)/shard_map/ppermute | solution.py:44
  65.2 13.6 %collective-permute-start.7 = (bf16[2,256,768]{2,1,0:T(8,128)(2,1)S(1)}, bf16[2,256,768]{2,1,0:T(8,128)(2,1)S(1)}, u32[]{:S(2)}, u32[]{:S(2)}) collective-permute-start(bf16[2,256,768]{2,1,0:T(8,128)(2,1)S(1)} %shard_map.67.refs_0_), channel_id=1, source_target_pairs={{0,1},{1,0},{2,3},{3,2},{4,5},{5,4},{6,7},{7,6},{8,9},{9,8},{10,11... | collective-permute-start | bytes 2359304 | tf_op jit(solution)/shard_map/ppermute | solution.py:37
  92.0 20.7 %collective-permute-start.17 = (f32[2,128,768]{2,1,0:T(8,128)}, f32[2,128,768]{2,1,0:T(8,128)}, u32[]{:S(2)}, u32[]{:S(2)}) collective-permute-start(f32[2,128,768]{2,1,0:T(8,128)} %bitcast.9), channel_id=1, source_target_pairs={{0,64},{1,65},{2,66},{3,67},{4,68},{5,69},{6,70},{7,71},{8,72},{9,... | collective-permute-start | bytes 2359304 | tf_op jit(solution)/shard_map/ppermute | solution.py:37
  92.1 32.8 %collective-permute-start.16 = (f32[2,128,768]{2,1,0:T(8,128)}, f32[2,128,768]{2,1,0:T(8,128)}, u32[]{:S(2)}, u32[]{:S(2)}) collective-permute-start(f32[2,128,768]{2,1,0:T(8,128)} %bitcast.8), channel_id=1, source_target_pairs={{0,96},{1,97},{2,98},{3,99},{4,100},{5,101},{6,102},{7,103},{8,104... | collective-permute-start | bytes 2359304 | tf_op jit(solution)/shard_map/ppermute | solution.py:37
  92.4 37.8 %collective-permute-start.15 = (f32[2,128,768]{2,1,0:T(8,128)}, f32[2,128,768]{2,1,0:T(8,128)}, u32[]{:S(2)}, u32[]{:S(2)}) collective-permute-start(f32[2,128,768]{2,1,0:T(8,128)} %bitcast.7), channel_id=1, source_target_pairs={{0,32},{1,33},{2,34},{3,35},{4,36},{5,37},{6,38},{7,39},{8,40},{9,... | collective-permute-start | bytes 2359304 | tf_op jit(solution)/shard_map/ppermute | solution.py:37
  133.0 11.2 %collective-permute-start.18 = (f32[128,768]{1,0:T(8,128)}, f32[128,768]{1,0:T(8,128)S(1)}, u32[]{:S(2)}, u32[]{:S(2)}) collective-permute-start(f32[128,768]{1,0:T(8,128)} %get-tuple-element.19), channel_id=1, source_target_pairs={{0,128},{1,129},{2,130},{3,131},{4,132},{5,133},{6,134},{7,135},{8... | collective-permute-start | bytes 1179656 | tf_op jit(solution)/shard_map/ppermute | solution.py:37
  134.9 15.2 %collective-permute-start.11 = (bf16[768,128]{1,0:T(8,128)(2,1)S(1)}, bf16[768,128]{1,0:T(8,128)(2,1)S(1)}, u32[]{:S(2)}, u32[]{:S(2)}) collective-permute-start(bf16[768,128]{1,0:T(8,128)(2,1)S(1)} %get-tuple-element.25), channel_id=1, source_target_pairs={{0,128},{1,129},{2,130},{3,131},{4,132},{5,133},{6,134},{7,135},{8... | collective-permute-start | bytes 589832 | tf_op jit(solution)/shard_map/ppermute | solution.py:37
  148.4 20.3 %collective-permute-start.30 = (bf16[128,512]{1,0:T(8,128)(2,1)}, bf16[128,512]{1,0:T(8,128)(2,1)S(1)}, u32[]{:S(2)}, u32[]{:S(2)}) collective-permute-start(bf16[128,512]{1,0:T(8,128)(2,1)} %get-tuple-element.18), channel_id=1, source_target_pairs={{0,128},{1,129},{2,130},{3,131},{4,132},{5,133},{6,134},{7,135},{8... | collective-permute-start | bytes 393224 | tf_op jit(solution)/shard_map/ppermute | solution.py:37
  151.4 11.0 %collective-permute-start.21 = (bf16[256,128]{1,0:T(8,128)(2,1)S(1)}, bf16[256,128]{1,0:T(8,128)(2,1)S(1)}, u32[]{:S(2)}, u32[]{:S(2)}) collective-permute-start(bf16[256,128]{1,0:T(8,128)(2,1)S(1)} %collective-permute-done.19.refs_1_), channel_id=1, source_target_pairs={{0,6},{1,7},{2,0},{3,1},{4,2},{5,3},{6,4},{7,5},{8,14},{9,15},{10,... | collective-permute-start | bytes 196616 | tf_op jit(solution)/shard_map/ppermute | solution.py:37
  158.7 22.5 %collective-permute-start.12 = (bf16[768,256]{1,0:T(8,128)(2,1)S(1)}, bf16[768,256]{1,0:T(8,128)(2,1)S(1)}, u32[]{:S(2)}, u32[]{:S(2)}) collective-permute-start(bf16[768,256]{1,0:T(8,128)(2,1)S(1)} %pad_maximum_fusion.refs_8_), channel_id=1, source_target_pairs={{0,32},{1,33},{2,34},{3,35},{4,36},{5,37},{6,38},{7,39},{8,40},{9,... | collective-permute-start | bytes 1179656 | tf_op jit(solution)/shard_map/ppermute | solution.py:37
  158.8 22.5 %collective-permute-start.13 = (bf16[768,256]{1,0:T(8,128)(2,1)S(1)}, bf16[768,256]{1,0:T(8,128)(2,1)S(1)}, u32[]{:S(2)}, u32[]{:S(2)}) collective-permute-start(bf16[768,256]{1,0:T(8,128)(2,1)S(1)} %pad_maximum_fusion.refs_8_), channel_id=1, source_target_pairs={{0,96},{1,97},{2,98},{3,99},{4,100},{5,101},{6,102},{7,103},{8,104... | collective-permute-start | bytes 1179656 | tf_op jit(solution)/shard_map/ppermute | solution.py:37
  162.4 21.5 %collective-permute-start.14 = (bf16[768,256]{1,0:T(8,128)(2,1)S(1)}, bf16[768,256]{1,0:T(8,128)(2,1)S(1)}, u32[]{:S(2)}, u32[]{:S(2)}) collective-permute-start(bf16[768,256]{1,0:T(8,128)(2,1)S(1)} %pad_maximum_fusion.refs_8_), channel_id=1, source_target_pairs={{0,64},{1,65},{2,66},{3,67},{4,68},{5,69},{6,70},{7,71},{8,72},{9,... | collective-permute-start | bytes 1179656 | tf_op jit(solution)/shard_map/ppermute | solution.py:37
  164.9 10.2 %collective-permute-start.23 = (bf16[2,256,256]{2,1,0:T(8,128)(2,1)S(1)}, bf16[2,256,256]{2,1,0:T(8,128)(2,1)S(1)}, u32[]{:S(2)}, u32[]{:S(2)}) collective-permute-start(bf16[2,256,256]{2,1,0:T(8,128)(2,1)S(1)} %shard_map.71.refs_0_), channel_id=1, source_target_pairs={{0,8},{1,9},{2,10},{3,11},{4,12},{5,13},{6,14},{7,15},{8,16},{9,17... | collective-permute-start | bytes 786440 | tf_op jit(solution)/shard_map/ppermute | solution.py:37
  168.7 12.2 %collective-permute-start.24 = (bf16[2,256,256]{2,1,0:T(8,128)(2,1)S(1)}, bf16[2,256,256]{2,1,0:T(8,128)(2,1)S(1)}, u32[]{:S(2)}, u32[]{:S(2)}) collective-permute-start(bf16[2,256,256]{2,1,0:T(8,128)(2,1)S(1)} %shard_map.71.refs_0_), channel_id=1, source_target_pairs={{0,24},{1,25},{2,26},{3,27},{4,28},{5,29},{6,30},{7,31},{8,0},{9,1... | collective-permute-start | bytes 786440 | tf_op jit(solution)/shard_map/ppermute | solution.py:37
  175.2 10.2 %collective-permute-start.26 = (bf16[2,256,256]{2,1,0:T(8,128)(2,1)S(1)}, bf16[2,256,256]{2,1,0:T(8,128)(2,1)S(1)}, u32[]{:S(2)}, u32[]{:S(2)}) collective-permute-start(bf16[2,256,256]{2,1,0:T(8,128)(2,1)S(1)} %shard_map.71.refs_0_), channel_id=1, source_target_pairs={{0,1},{1,0},{2,3},{3,2},{4,5},{5,4},{6,7},{7,6},{8,9},{9,8},{10,11... | collective-permute-start | bytes 786440 | tf_op jit(solution)/shard_map/ppermute | solution.py:37
  181.3 19.1 %collective-permute-start.32 = (bf16[256,512]{1,0:T(8,128)(2,1)S(1)}, bf16[256,512]{1,0:T(8,128)(2,1)S(1)}, u32[]{:S(2)}, u32[]{:S(2)}) collective-permute-start(bf16[256,512]{1,0:T(8,128)(2,1)S(1)} %pad_maximum_fusion.1.refs_8_), channel_id=1, source_target_pairs={{0,96},{1,97},{2,98},{3,99},{4,100},{5,101},{6,102},{7,103},{8,104... | collective-permute-start | bytes 786440 | tf_op jit(solution)/shard_map/ppermute | solution.py:37
  183.9 16.5 %collective-permute-start.33 = (bf16[256,512]{1,0:T(8,128)(2,1)S(1)}, bf16[256,512]{1,0:T(8,128)(2,1)S(1)}, u32[]{:S(2)}, u32[]{:S(2)}) collective-permute-start(bf16[256,512]{1,0:T(8,128)(2,1)S(1)} %pad_maximum_fusion.1.refs_8_), channel_id=1, source_target_pairs={{0,64},{1,65},{2,66},{3,67},{4,68},{5,69},{6,70},{7,71},{8,72},{9,... | collective-permute-start | bytes 786440 | tf_op jit(solution)/shard_map/ppermute | solution.py:37
  185.4 15.0 %collective-permute-start.27 = (bf16[2,256,256]{2,1,0:T(8,128)(2,1)S(1)}, bf16[2,256,256]{2,1,0:T(8,128)(2,1)S(1)}, u32[]{:S(2)}, u32[]{:S(2)}) collective-permute-start(bf16[2,256,256]{2,1,0:T(8,128)(2,1)S(1)} %collective-permute-done.23.refs_1_), channel_id=1, source_target_pairs={{0,1},{1,0},{2,3},{3,2},{4,5},{5,4},{6,7},{7,6},{8,9},{9,8},{10,11... | collective-permute-start | bytes 786440 | tf_op jit(solution)/shard_map/ppermute | solution.py:37
  190.1 10.3 %collective-permute-start.28 = (bf16[2,256,256]{2,1,0:T(8,128)(2,1)S(1)}, bf16[2,256,256]{2,1,0:T(8,128)(2,1)S(1)}, u32[]{:S(2)}, u32[]{:S(2)}) collective-permute-start(bf16[2,256,256]{2,1,0:T(8,128)(2,1)S(1)} %collective-permute-done.24.refs_2_), channel_id=1, source_target_pairs={{0,1},{1,0},{2,3},{3,2},{4,5},{5,4},{6,7},{7,6},{8,9},{9,8},{10,11... | collective-permute-start | bytes 786440 | tf_op jit(solution)/shard_map/ppermute | solution.py:37
  (20 other events, 203.1 us)
where the time goes:
time: 207 us; the launch traced here: 204 us
  starting transfers between devices  87.8 us (42%)
  waiting for transfers between devices  82.8 us (40%)
  Pallas kernels  23.7 us (11%)
  local copies, waits for them, and re-layouts  5.34 us (3%)
  other arithmetic  3 us (1%)
    ppermute x30, starting transfers between devices, shifted(): return lax.ppermute(value, AXES, permutation(target))  84.8 us
    ppermute x30, waiting for transfers between devices, shifted(): return lax.ppermute(value, AXES, permutation(target))  75.8 us
    pallas_call x1, Pallas kernels, rotate(): pl.pallas_call(rotate_kernel, out_shape=[jax.ShapeDtypeStruct((rows, k),...  9.41 us
    pallas_call x1, Pallas kernels, covariance(): pl.pallas_call(covariance_kernel, out_shape=[jax.ShapeDtypeStruct((n, 4 *...  7.07 us
    ppermute x2, waiting for transfers between devices, folded(): return lax.ppermute(value, AXES, permutation(target))  6.92 us
    unnamed x22, local copies, waits for them, and re-layouts  4.68 us
  transfers between devices with their start and end apart: 34, of which 11 were waited for; matrix products, arithmetic and copies ran while one was open for 0% of the time, Pallas kernels for 5%

commit v1 on v0

--- a/solution.py
+++ b/solution.py
@@ -12,8 +12,11 @@
 ZL, Y, X, ZH, C = range(5)
 STEPS = (0, 1, -1, 2)
 ANY = pl.BlockSpec(memory_space=pl.ANY)
+WHOLE = pl.BlockSpec(memory_space=pltpu.VMEM)
 SCALARS = pl.BlockSpec(memory_space=pltpu.SMEM)
 PARAMS = pltpu.CompilerParams(vmem_limit_bytes=48 * 1024 * 1024)
+
+CHEAP = pl.CostEstimate(flops=1000, bytes_accessed=1000, transcendentals=0)
 
 
 def device_index(q):
@@ -37,11 +40,8 @@
     return lax.ppermute(value, AXES, permutation(target))
 
 
-def folded(value):
-    def target(zl, y, x, zh, c):
-        return zl, y, (x - 1 + 2 * c) % SIZES[X], zh, c
-
-    return lax.ppermute(value, AXES, permutation(target))
+def direct(value, axis):
+    return [value if step == 0 else shifted(value, axis, step) for step in STEPS]
 
 
 def to_group(zl, y, x, zh, c):
@@ -65,7 +65,7 @@
 
 
 def near_kernel(turned, where, *refs):
-    *pieces, near, sems = refs
+    pieces, near, sems = refs[:4], refs[-2], refs[-1]
     copies = []
     for i, (step, piece) in enumerate(zip(STEPS, pieces)):
         zl, h = z_slot(where, step)
@@ -78,23 +78,44 @@
         copy.wait()
 
 
-def gather_group(block, where, turned):
-    block = lax.ppermute(block, AXES, permutation(to_group))
-    pieces = [block if step == 0 else shifted(block, ZH, step) for step in STEPS]
+def gather_near(block, where, turned, after):
     rows, columns = block.shape
     shape = (2, rows, 2 * columns) if turned else (2, 2 * rows, columns)
-    near = pl.pallas_call(
+    return pl.pallas_call(
         lambda *refs: near_kernel(turned, *refs),
         out_shape=jax.ShapeDtypeStruct(shape, block.dtype),
+        in_specs=[SCALARS] + [ANY] * (4 + len(after)),
+        out_specs=ANY,
+        scratch_shapes=[pltpu.SemaphoreType.DMA((4,))],
+        compiler_params=PARAMS,
+        cost_estimate=CHEAP,
+    )(where, *direct(block, ZH), *after)
+
+
+def stack_kernel(where, *refs):
+    *pieces, stack, sems = refs
+    copies = []
+    for i, (step, piece) in enumerate(zip(STEPS, pieces)):
+        copies.append(pltpu.make_async_copy(piece, stack.at[y_slot(where, step)], sems.at[i]))
+        copies[-1].start()
+    for copy in copies:
+        copy.wait()
+
+
+def stack_up(where, pieces):
+    return pl.pallas_call(
+        stack_kernel,
+        out_shape=jax.ShapeDtypeStruct((4,) + pieces[0].shape, pieces[0].dtype),
         in_specs=[SCALARS] + [ANY] * 4,
         out_specs=ANY,
         scratch_shapes=[pltpu.SemaphoreType.DMA((4,))],
         compiler_params=PARAMS,
+        cost_estimate=CHEAP,
     )(where, *pieces)
-    left = shifted(near, X, 1)
-    right = shifted(near, X, -1)
-    far = folded(jnp.where(where[C] == 0, right, left))
-    own = [near, left, right, far]
+
+
+def gather_far(near):
+    own = direct(near, X)
     return own + [shifted(piece, C, 1) for piece in own]
 
 
@@ -117,21 +138,42 @@
     return jnp.dot(a, b, preferred_element_type=jnp.float32)
 
 
+def encode(value, out, low):
+    rows, n = value.shape
+    top = jnp.max(jnp.max(jnp.abs(value), axis=0, keepdims=True), axis=1, keepdims=True)
+    top = jnp.maximum(top, 1e-30).astype(jnp.bfloat16)
+    power = value * (32768.0 / top.astype(jnp.float32))
+    sign = power < 0
+    for _ in range(3):
+        power = power * power
+    out[:rows, low:low + n] = jnp.where(sign, -power, power).astype(jnp.bfloat16)
+    out[rows:, low:low + n] = jnp.broadcast_to(top, (16, n))
+
+
+def decode(coded):
+    rows = coded.shape[0] - 16
+    power = coded[:rows, :].astype(jnp.float32)
+    top = coded[rows:rows + 1, :].astype(jnp.float32) * (1.0 / 32768.0)
+    root = jnp.abs(power)
+    for _ in range(3):
+        root = jnp.sqrt(root)
+    return jnp.where(power < 0, -root, root) * top
+
+
 def rotate_kernel(where, *refs):
-    pieces, (basis_act, basis_grad), outs = refs[:8], refs[8:10], refs[10:14]
-    panel, act, grad, parts, in_sems, basis_sems, out_sems = refs[14:]
+    pieces, (act_ref, grad_ref), outs = refs[:8], refs[8:10], refs[-9:-5]
+    panel, act, grad, in_sems, basis_sems = refs[-5:]
     n = act.shape[1]
-    first = pltpu.make_async_copy(basis_act, act, basis_sems.at[0])
-    second = pltpu.make_async_copy(basis_grad, grad, basis_sems.at[1])
-    first.start()
-    second.start()
-    copies = fetch(where, pieces, panel, in_sems)
-    first.wait()
-    second.wait()
-    for i, step in enumerate(STEPS):
-        copies[2 * i].wait()
-        copies[2 * i + 1].wait()
-        slot = x_slot(where, step)
+    loads = [
+        pltpu.make_async_copy(act_ref, act, basis_sems.at[0]),
+        pltpu.make_async_copy(grad_ref, grad, basis_sems.at[1]),
+    ]
+    for load in loads:
+        load.start()
+    for copy in loads + fetch(where, pieces, panel, in_sems):
+        copy.wait()
+    for out, step in zip(outs, STEPS):
+        slot = (where[Y] + step) & 3
         for basis, low, k in ((act, 0, n), (grad, n, 2 * n)):
             total = None
             for h in range(2):
@@ -139,47 +181,47 @@
                     rows = basis[(2 * h + c) * k:(2 * h + c + 1) * k, :]
                     term = dot(panel[c, slot, h, :, low:low + k], rows)
                     total = term if total is None else total + term
-            parts[i, :, low:low + k] = total
-        for j, y_step in enumerate(STEPS):
-            @pl.when(slot == ((where[Y] + y_step) & 3))
-            def _():
-                pltpu.make_async_copy(parts.at[i], outs[j], out_sems.at[i]).start()
-    for i in range(4):
-        pltpu.make_async_copy(parts.at[i], outs[0], out_sems.at[i]).wait()
-
-
-def rotate(where, pieces, basis_act, basis_grad):
+            if step == 0:
+                out[:, low:low + k] = total
+            else:
+                encode(total, out, low)
+
+
+def rotate(where, pieces, basis_act, basis_grad, after):
     rows, k = pieces[0].shape[1:]
     f32, bf16 = jnp.float32, jnp.bfloat16
     return pl.pallas_call(
         rotate_kernel,
-        out_shape=[jax.ShapeDtypeStruct((rows, k), f32)] * 4,
-        in_specs=[SCALARS] + [ANY] * 10,
-        out_specs=[ANY] * 4,
+        out_shape=[jax.ShapeDtypeStruct((rows, k), f32)]
+        + [jax.ShapeDtypeStruct((rows + 16, k), bf16)] * 3,
+        in_specs=[SCALARS] + [ANY] * (10 + len(after)),
         scratch_shapes=[
             pltpu.VMEM((2, 4, 2, rows, k), bf16),
             pltpu.VMEM(basis_act.shape, bf16),
             pltpu.VMEM(basis_grad.shape, bf16),
-            pltpu.VMEM((4, rows, k), f32),
             pltpu.SemaphoreType.DMA((4, 2)),
             pltpu.SemaphoreType.DMA((2,)),
-            pltpu.SemaphoreType.DMA((4,)),
-        ],
-        compiler_params=PARAMS,
-        cost_estimate=pl.CostEstimate(flops=3 * 10**9, bytes_accessed=12 * 10**6, transcendentals=0),
-    )(where, *pieces, basis_act, basis_grad)
+        ],
+        compiler_params=PARAMS,
+        cost_estimate=CHEAP,
+    )(where, *pieces, basis_act, basis_grad, *after)
 
 
 def covariance_kernel(where, *refs):
-    pieces, mine, outs = refs[:8], refs[8:12], refs[12:14]
-    panel, own, act, grad, in_sems, own_sems, out_sems = refs[14:]
+    pieces, stacks, outs, token = refs[:8], refs[8:10], refs[10:12], refs[12]
+    panel, own, act, grad, in_sems, own_sems, out_sems = refs[13:]
+    token[...] = jnp.zeros_like(token)
     n = act.shape[1]
-    tokens = mine[0].shape[1]
+    rows = stacks[0].shape[2]
+    tokens = 2 * rows
     copies = []
-    for i, step in enumerate(STEPS):
-        span = pl.ds(pl.multiple_of(y_slot(where, step) * tokens, tokens), tokens)
-        copies.append(pltpu.make_async_copy(mine[i], own.at[:, span], own_sems.at[i]))
-        copies[-1].start()
+    for i, stack in enumerate(stacks):
+        for y in range(4):
+            start = pl.multiple_of((2 * y + (where[ZL] ^ i)) * rows, rows)
+            copies.append(
+                pltpu.make_async_copy(stack.at[y], own.at[:, pl.ds(start, rows)], own_sems.at[i, y])
+            )
+            copies[-1].start()
     copies += fetch(where, pieces, panel, in_sems)
     for copy in copies:
         copy.wait()
@@ -216,20 +258,21 @@
         out_shape=[
             jax.ShapeDtypeStruct((n, 4 * n), f32),
             jax.ShapeDtypeStruct((2 * n, 8 * n), f32),
-        ],
-        in_specs=[SCALARS] + [ANY] * 12,
-        out_specs=[ANY] * 2,
+            jax.ShapeDtypeStruct((8, 128), f32),
+        ],
+        in_specs=[SCALARS] + [ANY] * 10,
+        out_specs=[ANY] * 2 + [WHOLE],
         scratch_shapes=[
             pltpu.VMEM((2, 4, 2, rows, k), bf16),
             pltpu.VMEM((k, 4 * rows), bf16),
             pltpu.VMEM((4, n, n), f32),
             pltpu.VMEM((4, 2 * n, 2 * n), f32),
             pltpu.SemaphoreType.DMA((4, 2)),
-            pltpu.SemaphoreType.DMA((4,)),
+            pltpu.SemaphoreType.DMA((2, 4)),
             pltpu.SemaphoreType.DMA((4, 2)),
         ],
         compiler_params=PARAMS,
-        cost_estimate=pl.CostEstimate(flops=3 * 10**9, bytes_accessed=14 * 10**6, transcendentals=0),
+        cost_estimate=CHEAP,
     )(where, *pieces, *mine)
 
 
@@ -283,52 +326,133 @@
             pltpu.SemaphoreType.DMA((4,)),
         ],
         compiler_params=PARAMS,
-        cost_estimate=pl.CostEstimate(flops=10**9, bytes_accessed=5 * 10**6, transcendentals=0),
+        cost_estimate=CHEAP,
     )(where, *pieces, *squares)
 
 
-def square_kernel(part_ref, arrived_ref, act_ref, grad_ref):
-    n = act_ref.shape[0]
-    total = part_ref[...] + arrived_ref[...]
+def half_kernel(where, own, *refs):
+    arrived, kept, sent, total = refs[:3], refs[-3], refs[-2], refs[-1]
+    rows = kept.shape[0]
+    whole = own[...]
+    for coded in arrived:
+        whole = whole + decode(coded)
+    for i in range(2):
+        total[i] = whole[i * rows:(i + 1) * rows]
+    kept[...] = total[where[ZL]]
+    n = kept.shape[1] // 3
+    other = total[1 - where[ZL]]
+    encode(other[:, :n], sent, 0)
+    encode(other[:, n:], sent, n)
+
+
+def sum_over_y(parts, where, after=()):
+    rows, n = parts[0].shape
+    rows = rows // 2
+    parts = [part if step == 0 else shifted(part, Y, step) for step, part in zip(STEPS, parts)]
+    return pl.pallas_call(
+        half_kernel,
+        out_shape=[
+            jax.ShapeDtypeStruct((rows, n), jnp.float32),
+            jax.ShapeDtypeStruct((rows + 16, n), jnp.bfloat16),
+        ],
+        in_specs=[SCALARS] + [WHOLE] * 4 + [ANY] * len(after),
+        scratch_shapes=[pltpu.VMEM((2, rows, n), jnp.float32)],
+        compiler_params=PARAMS,
+        cost_estimate=CHEAP,
+    )(where, *parts, *after)
+
+
+def square_kernel(kept, arrived, act, grad):
+    n = act.shape[0]
+    total = kept[...] + decode(arrived)
     square = total * total
-    act_ref[...] = square[:, :n].T.astype(jnp.bfloat16)
-    grad_ref[...] = square[:, n:].astype(jnp.bfloat16)
+    act[...] = square[:, :n].T.astype(jnp.bfloat16)
+    grad[...] = square[:, n:].astype(jnp.bfloat16)
+
+
+def square_of_sum(kept, sent):
+    rows, n = kept.shape[0], kept.shape[1] // 3
+    return pl.pallas_call(
+        square_kernel,
+        out_shape=[
+            jax.ShapeDtypeStruct((n, rows), jnp.bfloat16),
+            jax.ShapeDtypeStruct((rows, 2 * n), jnp.bfloat16),
+        ],
+        compiler_params=PARAMS,
+        cost_estimate=CHEAP,
+    )(kept, shifted(sent, ZL, 1))
+
+
+def pair_kernel(axis, where, own, other, pair, sems):
+    size = own.shape[axis]
+    copies = []
+    for i, (ref, zl) in enumerate(((own, where[ZL]), (other, 1 - where[ZL]))):
+        span = pl.ds(pl.multiple_of(zl * size, size), size)
+        target = pair.at[:, span] if axis else pair.at[span, :]
+        copies.append(pltpu.make_async_copy(ref, target, sems.at[i]))
+        copies[-1].start()
+    for copy in copies:
+        copy.wait()
 
 
 def pair_up(block, where, axis):
-    other = shifted(block, ZL, 1)
-    low = where[ZL] == 0
-    return jnp.concatenate([jnp.where(low, block, other), jnp.where(low, other, block)], axis=axis)
+    shape = list(block.shape)
+    shape[axis] *= 2
+    return pl.pallas_call(
+        lambda *refs: pair_kernel(axis, *refs),
+        out_shape=jax.ShapeDtypeStruct(shape, block.dtype),
+        in_specs=[SCALARS] + [ANY] * 2,
+        out_specs=ANY,
+        scratch_shapes=[pltpu.SemaphoreType.DMA((2,))],
+        compiler_params=PARAMS,
+        cost_estimate=CHEAP,
+    )(where, block, shifted(block, ZL, 1))
+
+
+def prepare_kernel(tokens, out_grads, joined, turned):
+    n = tokens.shape[1]
+    joined[:, :n] = tokens[...]
+    joined[:, n:] = out_grads[...]
+    turned[:n, :] = tokens[...].T
+    turned[n:, :] = out_grads[...].T
+
+
+def prepare(tokens, out_grads):
+    rows, k = tokens.shape[0], tokens.shape[1] + out_grads.shape[1]
+    return pl.pallas_call(
+        prepare_kernel,
+        out_shape=[
+            jax.ShapeDtypeStruct((rows, k), tokens.dtype),
+            jax.ShapeDtypeStruct((k, rows), tokens.dtype),
+        ],
+        compiler_params=PARAMS,
+        cost_estimate=CHEAP,
+    )(tokens, out_grads)
+
+
+def in_order(first, *later):
+    return lax.optimization_barrier((first, *later))[1:]
 
 
 def body(tokens, out_grads, basis_act, basis_grad):
     where = jnp.stack([lax.axis_index(axis) for axis in AXES]).astype(jnp.int32)
-    n = tokens.shape[1]
-    mine = jnp.concatenate([tokens, out_grads], axis=1)
-    panel = gather_group(mine, where, False)
-    turned = pair_up(mine.T, where, 1)
-    own = [turned if step == 0 else shifted(turned, Y, step) for step in STEPS]
-    parts = rotate(where, panel, basis_act, basis_grad)
-    cov_act, cov_grad = covariance(where, panel, own)
-    parts = [part.reshape(2, -1, 3 * n) for part in parts]
-    parts = [part if step == 0 else shifted(part, Y, step) for step, part in zip(STEPS, parts)]
-
-    def half(which):
-        return sum(lax.dynamic_index_in_dim(part, which, 0, False) for part in parts)
-
-    arrived = shifted(half(1 - where[ZL]), ZL, 1)
-    kept = half(where[ZL])
-    sq_act, sq_grad = pl.pallas_call(
-        square_kernel,
-        out_shape=[
-            jax.ShapeDtypeStruct((n, kept.shape[0]), jnp.bfloat16),
-            jax.ShapeDtypeStruct((kept.shape[0], 2 * n), jnp.bfloat16),
-        ],
-    )(kept, arrived)
-    squares = gather_group(sq_act, where, True)
+    joined, turned = prepare(tokens, out_grads)
+    block = lax.ppermute(joined, AXES, permutation(to_group))
+    (turned,) = in_order(block, turned)
+    own = direct(turned, Y)
+    near = gather_near(block, where, False, own[1:])
+    stack = stack_up(where, own)
+    panel = gather_far(near)
+    stacks = (stack, shifted(stack, ZL, 1))
+    parts = rotate(where, panel, basis_act, basis_grad, stacks)
+    cov_act, cov_grad, done = covariance(where, panel, stacks)
+    sq_act, sq_grad = square_of_sum(*sum_over_y(parts, where, (done,)))
+    block = lax.ppermute(sq_act, AXES, permutation(to_group))
     pair = pair_up(sq_grad, where, 0)
-    square_own = [pair if step == 0 else shifted(pair, Y, step) for step in STEPS]
-    correction = correct(where, squares, square_own)
+    pair, block = lax.optimization_barrier((pair, block))
+    squares_own = direct(pair, Y)
+    squares = gather_far(gather_near(block, where, True, squares_own[1:3]))
+    correction = correct(where, squares, squares_own)
     return (cov_act, cov_grad, correction)
 
 

time: 207 us -> 177 us (0.86); the launches traced: 204 us -> 176 us
  waiting for transfers between devices: 82.8 us -> 44.6 us
  starting transfers between devices: 87.8 us -> 98.7 us
  other arithmetic: 3 us -> 0 us
    ppermute x30 -> x32, waiting for transfers between devices: 75.8 us -> 44.6 us  [shifted(): return lax.ppermute(value, AXES, permutation(target))]
    ppermute x30 -> x32, starting transfers between devices: 84.8 us -> 97.4 us  [shifted(): return lax.ppermute(value, AXES, permutation(target))]
    ppermute x4 -> x2, waiting for transfers between devices: 6.93 us -> 0.01 us  [the longest x1 0.01 us: body(): block = lax.ppermute(joined, AXES, permutation(to_group))]
    pallas_call x3 -> x7, Pallas kernels: 4.13 us -> 8.84 us  [the longest x1 3.5 us: sum_over_y(): pl.pallas_call(half_kernel, out_shape=[jax.ShapeDtypeStruct((rows, n), jn...]
    add x1 -> x0, other arithmetic: 2.7 us -> none  [half(): sum((lax.dynamic_index_in_dim(part, which, 0, False) for part in parts))]
    pallas_call x1, Pallas kernels: 9.41 us -> 6.91 us  [rotate(): pl.pallas_call(rotate_kernel, out_shape=[jax.ShapeDtypeStruct((rows, k),...]
    unnamed x22 -> x24, local copies, waits for them, and re-layouts: 4.68 us -> 6.11 us
where the time goes in v1:
time: 177 us; the launch traced here: 176 us
  starting transfers between devices  98.7 us (56%)
  waiting for transfers between devices  44.6 us (25%)
  Pallas kernels  25.7 us (15%)
  local copies, waits for them, and re-layouts  6.2 us (4%)
    ppermute x32, starting transfers between devices, shifted(): return lax.ppermute(value, AXES, permutation(target))  97.4 us
    ppermute x32, waiting for transfers between devices, shifted(): return lax.ppermute(value, AXES, permutation(target))  44.6 us
    pallas_call x1, Pallas kernels, rotate(): pl.pallas_call(rotate_kernel, out_shape=[jax.ShapeDtypeStruct((rows, k),...  6.91 us
    pallas_call x1, Pallas kernels, covariance(): pl.pallas_call(covariance_kernel, out_shape=[jax.ShapeDtypeStruct((n, 4 *...  6.89 us
    unnamed x24, local copies, waits for them, and re-layouts  6.11 us
  transfers between devices with their start and end apart: 34, of which 11 were waited for; matrix products, arithmetic and copies ran while one was open for 0% of the time, Pallas kernels for 5%

profile of v1, /device:TPU:1, one launch (start us, length us, event | category | flops | bytes accessed | tf_op | source)
XLA Modules:
  0.0 176.2 jit_solution(2403443195283058009)
XLA Ops:
  3.2 13.5 %collective-permute-start.4 = (bf16[768,128]{1,0:T(8,128)(2,1)S(1)}, bf16[768,128]{1,0:T(8,128)(2,1)S(1)}, u32[]{:S(2)}, u32[]{:S(2)}) collective-permute-start(bf16[768,128]{1,0:T(8,128)(2,1)S(1)} %get-tuple-element.21.refs_0_), channel_id=1, source_target_pairs={{0,32},{1,33},{2,34},{3,35},{4,36},{5,37},{6,38},{7,39},{8,40},{9,... | collective-permute-start | bytes 589832 | tf_op jit(solution)/shard_map/ppermute | solution.py:40
  22.8 3.5 %collective-permute-start.2 = (bf16[128,768]{1,0:T(8,128)(2,1)S(1)}, bf16[128,768]{1,0:T(8,128)(2,1)S(1)}, u32[]{:S(2)}, u32[]{:S(2)}) collective-permute-start(bf16[128,768]{1,0:T(8,128)(2,1)S(1)} %collective-permute-done.refs_1_), channel_id=1, source_target_pairs={{0,6},{1,7},{2,0},{3,1},{4,2},{5,3},{6,4},{7,5},{8,14},{9,15},{10,... | collective-permute-start | bytes 589832 | tf_op jit(solution)/shard_map/ppermute | solution.py:40
  30.0 11.3 %collective-permute-done.3.refs_4_ = bf16[128,768]{1,0:T(8,128)(2,1)S(1)} collective-permute-done((bf16[128,768]{1,0:T(8,128)(2,1)S(1)}, bf16[128,768]{1,0:T(8,128)(2,1)S(1)}, u32[]{:S(2)}, u32[]{:S(2)}) %collective-permute-start.3) | collective-permute-done | bytes 196640 | tf_op jit(solution)/shard_map/ppermute | solution.py:40
  43.1 3.2 %collective-permute-start.8 = (bf16[2,256,768]{2,1,0:T(8,128)(2,1)S(1)}, bf16[2,256,768]{2,1,0:T(8,128)(2,1)S(1)}, u32[]{:S(2)}, u32[]{:S(2)}) collective-permute-start(bf16[2,256,768]{2,1,0:T(8,128)(2,1)S(1)} %shard_map.68.refs_0_), channel_id=1, source_target_pairs={{0,24},{1,25},{2,26},{3,27},{4,28},{5,29},{6,30},{7,31},{8,0},{9,1... | collective-permute-start | bytes 2359304 | tf_op jit(solution)/shard_map/ppermute | solution.py:40
  46.3 3.8 %collective-permute-start.9 = (bf16[2,256,768]{2,1,0:T(8,128)(2,1)S(1)}, bf16[2,256,768]{2,1,0:T(8,128)(2,1)S(1)}, u32[]{:S(2)}, u32[]{:S(2)}) collective-permute-start(bf16[2,256,768]{2,1,0:T(8,128)(2,1)S(1)} %shard_map.68.refs_0_), channel_id=1, source_target_pairs={{0,16},{1,17},{2,18},{3,19},{4,20},{5,21},{6,22},{7,23},{8,24},{9,... | collective-permute-start | bytes 2359304 | tf_op jit(solution)/shard_map/ppermute | solution.py:40
  50.1 2.9 %collective-permute-start.10 = (bf16[2,256,768]{2,1,0:T(8,128)(2,1)S(1)}, bf16[2,256,768]{2,1,0:T(8,128)(2,1)S(1)}, u32[]{:S(2)}, u32[]{:S(2)}) collective-permute-start(bf16[2,256,768]{2,1,0:T(8,128)(2,1)S(1)} %shard_map.68.refs_0_), channel_id=1, source_target_pairs={{0,1},{1,0},{2,3},{3,2},{4,5},{5,4},{6,7},{7,6},{8,9},{9,8},{10,11... | collective-permute-start | bytes 2359304 | tf_op jit(solution)/shard_map/ppermute | solution.py:40
  54.6 3.8 %collective-permute-start.14 = (bf16[4,768,128]{2,1,0:T(8,128)(2,1)S(1)}, bf16[4,768,128]{2,1,0:T(8,128)(2,1)S(1)}, u32[]{:S(2)}, u32[]{:S(2)}) collective-permute-start(bf16[4,768,128]{2,1,0:T(8,128)(2,1)S(1)} %shard_map.69.refs_8_.refs_10_), channel_id=1, source_target_pairs={{0,128},{1,129},{2,130},{3,131},{4,132},{5,133},{6,134},{7,135},{8... | collective-permute-start | bytes 2359304 | tf_op jit(solution)/shard_map/ppermute | solution.py:40
  59.1 7.9 %collective-permute-start.11 = (bf16[2,256,768]{2,1,0:T(8,128)(2,1)S(1)}, bf16[2,256,768]{2,1,0:T(8,128)(2,1)S(1)}, u32[]{:S(2)}, u32[]{:S(2)}) collective-permute-start(bf16[2,256,768]{2,1,0:T(8,128)(2,1)S(1)} %collective-permute-done.7.refs_1_), channel_id=1, source_target_pairs={{0,1},{1,0},{2,3},{3,2},{4,5},{5,4},{6,7},{7,6},{8,9},{9,8},{10,11... | collective-permute-start | bytes 2359304 | tf_op jit(solution)/shard_map/ppermute | solution.py:40
  69.5 9.9 %collective-permute-done.9.refs_3_ = bf16[2,256,768]{2,1,0:T(8,128)(2,1)S(1)} collective-permute-done((bf16[2,256,768]{2,1,0:T(8,128)(2,1)S(1)}, bf16[2,256,768]{2,1,0:T(8,128)(2,1)S(1)}, u32[]{:S(2)}, u32[]{:S(2)}) %collective-permute-start.9) | collective-permute-done | bytes 786464 | tf_op jit(solution)/shard_map/ppermute | solution.py:40
  79.4 4.6 %collective-permute-start.13 = (bf16[2,256,768]{2,1,0:T(8,128)(2,1)S(1)}, bf16[2,256,768]{2,1,0:T(8,128)(2,1)S(1)}, u32[]{:S(2)}, u32[]{:S(2)}) collective-permute-start(bf16[2,256,768]{2,1,0:T(8,128)(2,1)S(1)} %collective-permute-done.9.refs_3_), channel_id=1, source_target_pairs={{0,1},{1,0},{2,3},{3,2},{4,5},{5,4},{6,7},{7,6},{8,9},{9,8},{10,11... | collective-permute-start | bytes 2359304 | tf_op jit(solution)/shard_map/ppermute | solution.py:40
  86.8 6.9 %shard_map.71 = (f32[256,768]{1,0:T(8,128)S(1)}, bf16[272,768]{1,0:T(8,128)(2,1)S(1)}, bf16[272,768]{1,0:T(8,128)(2,1)S(1)}, bf16[272,768]{1,0:T(8,128)(2,1)S(1)}) custom-call(s32[5]{0:T(128)S(1)} %stack.23.refs_0_.where, bf16[2,256,768]{2,1,0:T(8,128)(2,1)S(1)} %shard_map.68.refs_0_, bf16[2,256,768]{2,1,0:T(8,128)(2,1)S(1)} %collective-permute-done.7.refs_1_, ...), custom_call_target="tpu_custom_call" | custom-call | flops 1000 | bytes 1000 | tf_op jit(solution)/shard_map/pallas_call | solution.py:193
  101.1 6.9 %shard_map.70 = (f32[256,1024]{1,0:T(8,128)}, f32[512,2048]{1,0:T(8,128)}, f32[8,128]{1,0:T(8,128)S(1)}) custom-call(s32[5]{0:T(128)S(1)} %stack.23.refs_0_.where, bf16[2,256,768]{2,1,0:T(8,128)(2,1)S(1)} %shard_map.68.refs_0_, bf16[2,256,768]{2,1,0:T(8,128)(2,1)S(1)} %collective-permute-done.7.refs_1_, ...), custom_call_target="tpu_custom_call" | custom-call | flops 1000 | bytes 1000 | tf_op jit(solution)/shard_map/pallas_call | solution.py:256
  108.0 6.9 %collective-permute-done.17.refs_2_ = bf16[272,768]{1,0:T(8,128)(2,1)S(1)} collective-permute-done((bf16[272,768]{1,0:T(8,128)(2,1)S(1)}, bf16[272,768]{1,0:T(8,128)(2,1)S(1)}, u32[]{:S(2)}, u32[]{:S(2)}) %collective-permute-start.17) | collective-permute-done | bytes 417824 | tf_op jit(solution)/shard_map/ppermute | solution.py:40
  114.9 3.5 %shard_map.72 = (f32[128,768]{1,0:T(8,128)S(1)}, bf16[144,768]{1,0:T(8,128)(2,1)S(1)}) custom-call(s32[5]{0:T(128)S(1)} %stack.23.refs_0_.where, f32[256,768]{1,0:T(8,128)S(1)} %get-tuple-element.24.own, bf16[272,768]{1,0:T(8,128)(2,1)S(1)} %collective-permute-done.15.refs_0_, bf16[272,768]{1,0:T(8,128)(2,1)S(1)} %collective-permute-done.16.refs_1_, ...), custom_call_target="tpu_custom_call" | custom-call | flops 1000 | bytes 1000 | tf_op jit(solution)/shard_map/pallas_call | solution.py:352
  118.5 4.1 %collective-permute-start.18 = (bf16[144,768]{1,0:T(8,128)(2,1)S(1)}, bf16[144,768]{1,0:T(8,128)(2,1)S(1)}, u32[]{:S(2)}, u32[]{:S(2)}) collective-permute-start(bf16[144,768]{1,0:T(8,128)(2,1)S(1)} %get-tuple-element.30), channel_id=1, source_target_pairs={{0,128},{1,129},{2,130},{3,131},{4,132},{5,133},{6,134},{7,135},{8... | collective-permute-start | bytes 663560 | tf_op jit(solution)/shard_map/ppermute | solution.py:40
  122.5 4.5 %collective-permute-done.18.arrived = bf16[144,768]{1,0:T(8,128)(2,1)S(1)} collective-permute-done((bf16[144,768]{1,0:T(8,128)(2,1)S(1)}, bf16[144,768]{1,0:T(8,128)(2,1)S(1)}, u32[]{:S(2)}, u32[]{:S(2)}) %collective-permute-start.18) | collective-permute-done | bytes 221216 | tf_op jit(solution)/shard_map/ppermute | solution.py:40
  132.6 3.2 %collective-permute-start.24 = (bf16[256,512]{1,0:T(8,128)(2,1)S(1)}, bf16[256,512]{1,0:T(8,128)(2,1)S(1)}, u32[]{:S(2)}, u32[]{:S(2)}) collective-permute-start(bf16[256,512]{1,0:T(8,128)(2,1)S(1)} %shard_map.74.refs_8_), channel_id=1, source_target_pairs={{0,32},{1,33},{2,34},{3,35},{4,36},{5,37},{6,38},{7,39},{8,40},{9,... | collective-permute-start | bytes 786440 | tf_op jit(solution)/shard_map/ppermute | solution.py:40
  135.8 3.3 %collective-permute-start.25 = (bf16[256,512]{1,0:T(8,128)(2,1)S(1)}, bf16[256,512]{1,0:T(8,128)(2,1)S(1)}, u32[]{:S(2)}, u32[]{:S(2)}) collective-permute-start(bf16[256,512]{1,0:T(8,128)(2,1)S(1)} %shard_map.74.refs_8_), channel_id=1, source_target_pairs={{0,96},{1,97},{2,98},{3,99},{4,100},{5,101},{6,102},{7,103},{8,104... | collective-permute-start | bytes 786440 | tf_op jit(solution)/shard_map/ppermute | solution.py:40
  139.0 3.8 %collective-permute-start.21 = (bf16[256,128]{1,0:T(8,128)(2,1)S(1)}, bf16[256,128]{1,0:T(8,128)(2,1)S(1)}, u32[]{:S(2)}, u32[]{:S(2)}) collective-permute-start(bf16[256,128]{1,0:T(8,128)(2,1)S(1)} %collective-permute-done.20.refs_1_), channel_id=1, source_target_pairs={{0,2},{1,3},{2,4},{3,5},{4,6},{5,7},{6,0},{7,1},{8,10},{9,11},{10,... | collective-permute-start | bytes 196616 | tf_op jit(solution)/shard_map/ppermute | solution.py:40
  142.8 3.3 %collective-permute-start.23 = (bf16[256,128]{1,0:T(8,128)(2,1)S(1)}, bf16[256,128]{1,0:T(8,128)(2,1)S(1)}, u32[]{:S(2)}, u32[]{:S(2)}) collective-permute-start(bf16[256,128]{1,0:T(8,128)(2,1)S(1)} %collective-permute-done.20.refs_1_), channel_id=1, source_target_pairs={{0,4},{1,5},{2,6},{3,7},{4,0},{5,1},{6,2},{7,3},{8,12},{9,13},{10,... | collective-permute-start | bytes 196616 | tf_op jit(solution)/shard_map/ppermute | solution.py:40
  147.1 4.1 %collective-permute-done.23.refs_4_ = bf16[256,128]{1,0:T(8,128)(2,1)S(1)} collective-permute-done((bf16[256,128]{1,0:T(8,128)(2,1)S(1)}, bf16[256,128]{1,0:T(8,128)(2,1)S(1)}, u32[]{:S(2)}, u32[]{:S(2)}) %collective-permute-start.23) | collective-permute-done | bytes 65568 | tf_op jit(solution)/shard_map/ppermute | solution.py:40
  152.0 5.3 %collective-permute-start.27 = (bf16[2,256,256]{2,1,0:T(8,128)(2,1)S(1)}, bf16[2,256,256]{2,1,0:T(8,128)(2,1)S(1)}, u32[]{:S(2)}, u32[]{:S(2)}) collective-permute-start(bf16[2,256,256]{2,1,0:T(8,128)(2,1)S(1)} %shard_map.75.refs_0_), channel_id=1, source_target_pairs={{0,24},{1,25},{2,26},{3,27},{4,28},{5,29},{6,30},{7,31},{8,0},{9,1... | collective-permute-start | bytes 786440 | tf_op jit(solution)/shard_map/ppermute | solution.py:40
  159.6 6.5 %collective-permute-start.29 = (bf16[2,256,256]{2,1,0:T(8,128)(2,1)S(1)}, bf16[2,256,256]{2,1,0:T(8,128)(2,1)S(1)}, u32[]{:S(2)}, u32[]{:S(2)}) collective-permute-start(bf16[2,256,256]{2,1,0:T(8,128)(2,1)S(1)} %shard_map.75.refs_0_), channel_id=1, source_target_pairs={{0,1},{1,0},{2,3},{3,2},{4,5},{5,4},{6,7},{7,6},{8,9},{9,8},{10,11... | collective-permute-start | bytes 786440 | tf_op jit(solution)/shard_map/ppermute | solution.py:40
  173.0 3.0 %shard_map.76 = f32[1024,512]{1,0:T(8,128)} custom-call(s32[5]{0:T(128)S(1)} %stack.23.refs_0_.where, bf16[2,256,256]{2,1,0:T(8,128)(2,1)S(1)} %shard_map.75.refs_0_, bf16[2,256,256]{2,1,0:T(8,128)(2,1)S(1)} %collective-permute-done.26.refs_1_, bf16[2,256,256]{2,1,0:T(8,128)(2,1)S(1)} %collective-permute-done.27.refs_2_, ...), custom_call_target="tpu_custom_call" | custom-call | flops 1000 | bytes 1000 | tf_op jit(solution)/shard_map/pallas_call | solution.py:315
  (79 shorter events, 45.3 us)
Async XLA Ops:
  3.2 23.0 %collective-permute-start.4 = (bf16[768,128]{1,0:T(8,128)(2,1)S(1)}, bf16[768,128]{1,0:T(8,128)(2,1)S(1)}, u32[]{:S(2)}, u32[]{:S(2)}) collective-permute-start(bf16[768,128]{1,0:T(8,128)(2,1)S(1)} %get-tuple-element.21.refs_0_), channel_id=1, source_target_pairs={{0,32},{1,33},{2,34},{3,35},{4,36},{5,37},{6,38},{7,39},{8,40},{9,... | collective-permute-start | bytes 589832 | tf_op jit(solution)/shard_map/ppermute | solution.py:40
  16.8 12.2 %collective-permute-start.5 = (bf16[768,128]{1,0:T(8,128)(2,1)S(1)}, bf16[768,128]{1,0:T(8,128)(2,1)S(1)}, u32[]{:S(2)}, u32[]{:S(2)}) collective-permute-start(bf16[768,128]{1,0:T(8,128)(2,1)S(1)} %get-tuple-element.21.refs_0_), channel_id=1, source_target_pairs={{0,96},{1,97},{2,98},{3,99},{4,100},{5,101},{6,102},{7,103},{8,104... | collective-permute-start | bytes 589832 | tf_op jit(solution)/shard_map/ppermute | solution.py:40
  19.3 9.7 %collective-permute-start.6 = (bf16[768,128]{1,0:T(8,128)(2,1)S(1)}, bf16[768,128]{1,0:T(8,128)(2,1)S(1)}, u32[]{:S(2)}, u32[]{:S(2)}) collective-permute-start(bf16[768,128]{1,0:T(8,128)(2,1)S(1)} %get-tuple-element.21.refs_0_), channel_id=1, source_target_pairs={{0,64},{1,65},{2,66},{3,67},{4,68},{5,69},{6,70},{7,71},{8,72},{9,... | collective-permute-start | bytes 589832 | tf_op jit(solution)/shard_map/ppermute | solution.py:40
  20.5 9.5 %collective-permute-start.1 = (bf16[128,768]{1,0:T(8,128)(2,1)S(1)}, bf16[128,768]{1,0:T(8,128)(2,1)S(1)}, u32[]{:S(2)}, u32[]{:S(2)}) collective-permute-start(bf16[128,768]{1,0:T(8,128)(2,1)S(1)} %collective-permute-done.refs_1_), channel_id=1, source_target_pairs={{0,2},{1,3},{2,4},{3,5},{4,6},{5,7},{6,0},{7,1},{8,10},{9,11},{10,... | collective-permute-start | bytes 589832 | tf_op jit(solution)/shard_map/ppermute | solution.py:40
  26.3 15.1 %collective-permute-start.3 = (bf16[128,768]{1,0:T(8,128)(2,1)S(1)}, bf16[128,768]{1,0:T(8,128)(2,1)S(1)}, u32[]{:S(2)}, u32[]{:S(2)}) collective-permute-start(bf16[128,768]{1,0:T(8,128)(2,1)S(1)} %collective-permute-done.refs_1_), channel_id=1, source_target_pairs={{0,4},{1,5},{2,6},{3,7},{4,0},{5,1},{6,2},{7,3},{8,12},{9,13},{10,... | collective-permute-start | bytes 589832 | tf_op jit(solution)/shard_map/ppermute | solution.py:40
  43.0 16.2 %collective-permute-start.7 = (bf16[2,256,768]{2,1,0:T(8,128)(2,1)S(1)}, bf16[2,256,768]{2,1,0:T(8,128)(2,1)S(1)}, u32[]{:S(2)}, u32[]{:S(2)}) collective-permute-start(bf16[2,256,768]{2,1,0:T(8,128)(2,1)S(1)} %shard_map.68.refs_0_), channel_id=1, source_target_pairs={{0,8},{1,9},{2,10},{3,11},{4,12},{5,13},{6,14},{7,15},{8,16},{9,17... | collective-permute-start | bytes 2359304 | tf_op jit(solution)/shard_map/ppermute | solution.py:40
  43.1 24.0 %collective-permute-start.8 = (bf16[2,256,768]{2,1,0:T(8,128)(2,1)S(1)}, bf16[2,256,768]{2,1,0:T(8,128)(2,1)S(1)}, u32[]{:S(2)}, u32[]{:S(2)}) collective-permute-start(bf16[2,256,768]{2,1,0:T(8,128)(2,1)S(1)} %shard_map.68.refs_0_), channel_id=1, source_target_pairs={{0,24},{1,25},{2,26},{3,27},{4,28},{5,29},{6,30},{7,31},{8,0},{9,1... | collective-permute-start | bytes 2359304 | tf_op jit(solution)/shard_map/ppermute | solution.py:40
  46.3 33.1 %collective-permute-start.9 = (bf16[2,256,768]{2,1,0:T(8,128)(2,1)S(1)}, bf16[2,256,768]{2,1,0:T(8,128)(2,1)S(1)}, u32[]{:S(2)}, u32[]{:S(2)}) collective-permute-start(bf16[2,256,768]{2,1,0:T(8,128)(2,1)S(1)} %shard_map.68.refs_0_), channel_id=1, source_target_pairs={{0,16},{1,17},{2,18},{3,19},{4,20},{5,21},{6,22},{7,23},{8,24},{9,... | collective-permute-start | bytes 2359304 | tf_op jit(solution)/shard_map/ppermute | solution.py:40
  50.1 33.9 %collective-permute-start.10 = (bf16[2,256,768]{2,1,0:T(8,128)(2,1)S(1)}, bf16[2,256,768]{2,1,0:T(8,128)(2,1)S(1)}, u32[]{:S(2)}, u32[]{:S(2)}) collective-permute-start(bf16[2,256,768]{2,1,0:T(8,128)(2,1)S(1)} %shard_map.68.refs_0_), channel_id=1, source_target_pairs={{0,1},{1,0},{2,3},{3,2},{4,5},{5,4},{6,7},{7,6},{8,9},{9,8},{10,11... | collective-permute-start | bytes 2359304 | tf_op jit(solution)/shard_map/ppermute | solution.py:40
  54.6 29.4 %collective-permute-start.14 = (bf16[4,768,128]{2,1,0:T(8,128)(2,1)S(1)}, bf16[4,768,128]{2,1,0:T(8,128)(2,1)S(1)}, u32[]{:S(2)}, u32[]{:S(2)}) collective-permute-start(bf16[4,768,128]{2,1,0:T(8,128)(2,1)S(1)} %shard_map.69.refs_8_.refs_10_), channel_id=1, source_target_pairs={{0,128},{1,129},{2,130},{3,131},{4,132},{5,133},{6,134},{7,135},{8... | collective-permute-start | bytes 2359304 | tf_op jit(solution)/shard_map/ppermute | solution.py:40
  59.1 24.9 %collective-permute-start.11 = (bf16[2,256,768]{2,1,0:T(8,128)(2,1)S(1)}, bf16[2,256,768]{2,1,0:T(8,128)(2,1)S(1)}, u32[]{:S(2)}, u32[]{:S(2)}) collective-permute-start(bf16[2,256,768]{2,1,0:T(8,128)(2,1)S(1)} %collective-permute-done.7.refs_1_), channel_id=1, source_target_pairs={{0,1},{1,0},{2,3},{3,2},{4,5},{5,4},{6,7},{7,6},{8,9},{9,8},{10,11... | collective-permute-start | bytes 2359304 | tf_op jit(solution)/shard_map/ppermute | solution.py:40
  67.0 17.0 %collective-permute-start.12 = (bf16[2,256,768]{2,1,0:T(8,128)(2,1)S(1)}, bf16[2,256,768]{2,1,0:T(8,128)(2,1)S(1)}, u32[]{:S(2)}, u32[]{:S(2)}) collective-permute-start(bf16[2,256,768]{2,1,0:T(8,128)(2,1)S(1)} %collective-permute-done.8.refs_2_), channel_id=1, source_target_pairs={{0,1},{1,0},{2,3},{3,2},{4,5},{5,4},{6,7},{7,6},{8,9},{9,8},{10,11... | collective-permute-start | bytes 2359304 | tf_op jit(solution)/shard_map/ppermute | solution.py:40
  93.8 14.2 %collective-permute-start.15 = (bf16[272,768]{1,0:T(8,128)(2,1)S(1)}, bf16[272,768]{1,0:T(8,128)(2,1)S(1)}, u32[]{:S(2)}, u32[]{:S(2)}) collective-permute-start(bf16[272,768]{1,0:T(8,128)(2,1)S(1)} %get-tuple-element.25), channel_id=1, source_target_pairs={{0,32},{1,33},{2,34},{3,35},{4,36},{5,37},{6,38},{7,39},{8,40},{9,... | collective-permute-start | bytes 1253384 | tf_op jit(solution)/shard_map/ppermute | solution.py:40
  95.2 12.8 %collective-permute-start.16 = (bf16[272,768]{1,0:T(8,128)(2,1)S(1)}, bf16[272,768]{1,0:T(8,128)(2,1)S(1)}, u32[]{:S(2)}, u32[]{:S(2)}) collective-permute-start(bf16[272,768]{1,0:T(8,128)(2,1)S(1)} %get-tuple-element.26), channel_id=1, source_target_pairs={{0,96},{1,97},{2,98},{3,99},{4,100},{5,101},{6,102},{7,103},{8,104... | collective-permute-start | bytes 1253384 | tf_op jit(solution)/shard_map/ppermute | solution.py:40
  96.5 18.4 %collective-permute-start.17 = (bf16[272,768]{1,0:T(8,128)(2,1)S(1)}, bf16[272,768]{1,0:T(8,128)(2,1)S(1)}, u32[]{:S(2)}, u32[]{:S(2)}) collective-permute-start(bf16[272,768]{1,0:T(8,128)(2,1)S(1)} %get-tuple-element.27), channel_id=1, source_target_pairs={{0,64},{1,65},{2,66},{3,67},{4,68},{5,69},{6,70},{7,71},{8,72},{9,... | collective-permute-start | bytes 1253384 | tf_op jit(solution)/shard_map/ppermute | solution.py:40
  118.5 8.6 %collective-permute-start.18 = (bf16[144,768]{1,0:T(8,128)(2,1)S(1)}, bf16[144,768]{1,0:T(8,128)(2,1)S(1)}, u32[]{:S(2)}, u32[]{:S(2)}) collective-permute-start(bf16[144,768]{1,0:T(8,128)(2,1)S(1)} %get-tuple-element.30), channel_id=1, source_target_pairs={{0,128},{1,129},{2,130},{3,131},{4,132},{5,133},{6,134},{7,135},{8... | collective-permute-start | bytes 663560 | tf_op jit(solution)/shard_map/ppermute | solution.py:40
  132.6 18.7 %collective-permute-start.24 = (bf16[256,512]{1,0:T(8,128)(2,1)S(1)}, bf16[256,512]{1,0:T(8,128)(2,1)S(1)}, u32[]{:S(2)}, u32[]{:S(2)}) collective-permute-start(bf16[256,512]{1,0:T(8,128)(2,1)S(1)} %shard_map.74.refs_8_), channel_id=1, source_target_pairs={{0,32},{1,33},{2,34},{3,35},{4,36},{5,37},{6,38},{7,39},{8,40},{9,... | collective-permute-start | bytes 786440 | tf_op jit(solution)/shard_map/ppermute | solution.py:40
  135.8 15.5 %collective-permute-start.25 = (bf16[256,512]{1,0:T(8,128)(2,1)S(1)}, bf16[256,512]{1,0:T(8,128)(2,1)S(1)}, u32[]{:S(2)}, u32[]{:S(2)}) collective-permute-start(bf16[256,512]{1,0:T(8,128)(2,1)S(1)} %shard_map.74.refs_8_), channel_id=1, source_target_pairs={{0,96},{1,97},{2,98},{3,99},{4,100},{5,101},{6,102},{7,103},{8,104... | collective-permute-start | bytes 786440 | tf_op jit(solution)/shard_map/ppermute | solution.py:40
  142.8 8.4 %collective-permute-start.23 = (bf16[256,128]{1,0:T(8,128)(2,1)S(1)}, bf16[256,128]{1,0:T(8,128)(2,1)S(1)}, u32[]{:S(2)}, u32[]{:S(2)}) collective-permute-start(bf16[256,128]{1,0:T(8,128)(2,1)S(1)} %collective-permute-done.20.refs_1_), channel_id=1, source_target_pairs={{0,4},{1,5},{2,6},{3,7},{4,0},{5,1},{6,2},{7,3},{8,12},{9,13},{10,... | collective-permute-start | bytes 196616 | tf_op jit(solution)/shard_map/ppermute | solution.py:40
  151.9 14.2 %collective-permute-start.26 = (bf16[2,256,256]{2,1,0:T(8,128)(2,1)S(1)}, bf16[2,256,256]{2,1,0:T(8,128)(2,1)S(1)}, u32[]{:S(2)}, u32[]{:S(2)}) collective-permute-start(bf16[2,256,256]{2,1,0:T(8,128)(2,1)S(1)} %shard_map.75.refs_0_), channel_id=1, source_target_pairs={{0,8},{1,9},{2,10},{3,11},{4,12},{5,13},{6,14},{7,15},{8,16},{9,17... | collective-permute-start | bytes 786440 | tf_op jit(solution)/shard_map/ppermute | solution.py:40
  152.0 16.4 %collective-permute-start.27 = (bf16[2,256,256]{2,1,0:T(8,128)(2,1)S(1)}, bf16[2,256,256]{2,1,0:T(8,128)(2,1)S(1)}, u32[]{:S(2)}, u32[]{:S(2)}) collective-permute-start(bf16[2,256,256]{2,1,0:T(8,128)(2,1)S(1)} %shard_map.75.refs_0_), channel_id=1, source_target_pairs={{0,24},{1,25},{2,26},{3,27},{4,28},{5,29},{6,30},{7,31},{8,0},{9,1... | collective-permute-start | bytes 786440 | tf_op jit(solution)/shard_map/ppermute | solution.py:40
  157.3 12.7 %collective-permute-start.28 = (bf16[2,256,256]{2,1,0:T(8,128)(2,1)S(1)}, bf16[2,256,256]{2,1,0:T(8,128)(2,1)S(1)}, u32[]{:S(2)}, u32[]{:S(2)}) collective-permute-start(bf16[2,256,256]{2,1,0:T(8,128)(2,1)S(1)} %shard_map.75.refs_0_), channel_id=1, source_target_pairs={{0,16},{1,17},{2,18},{3,19},{4,20},{5,21},{6,22},{7,23},{8,24},{9,... | collective-permute-start | bytes 786440 | tf_op jit(solution)/shard_map/ppermute | solution.py:40
  158.4 13.4 %collective-permute-start.33 = (bf16[256,512]{1,0:T(8,128)(2,1)S(1)}, bf16[256,512]{1,0:T(8,128)(2,1)S(1)}, u32[]{:S(2)}, u32[]{:S(2)}) collective-permute-start(bf16[256,512]{1,0:T(8,128)(2,1)S(1)} %shard_map.74.refs_8_), channel_id=1, source_target_pairs={{0,64},{1,65},{2,66},{3,67},{4,68},{5,69},{6,70},{7,71},{8,72},{9,... | collective-permute-start | bytes 786440 | tf_op jit(solution)/shard_map/ppermute | solution.py:40
  159.6 12.2 %collective-permute-start.29 = (bf16[2,256,256]{2,1,0:T(8,128)(2,1)S(1)}, bf16[2,256,256]{2,1,0:T(8,128)(2,1)S(1)}, u32[]{:S(2)}, u32[]{:S(2)}) collective-permute-start(bf16[2,256,256]{2,1,0:T(8,128)(2,1)S(1)} %shard_map.75.refs_0_), channel_id=1, source_target_pairs={{0,1},{1,0},{2,3},{3,2},{4,5},{5,4},{6,7},{7,6},{8,9},{9,8},{10,11... | collective-permute-start | bytes 786440 | tf_op jit(solution)/shard_map/ppermute | solution.py:40
  (22 other events, 176.8 us)

commit v2 on v1

--- a/solution.py
+++ b/solution.py
@@ -42,6 +42,13 @@
 
 def direct(value, axis):
     return [value if step == 0 else shifted(value, axis, step) for step in STEPS]
+
+
+def folded(value):
+    def target(zl, y, x, zh, c):
+        return zl, y, (x - 1 + 2 * c) % SIZES[X], zh, c
+
+    return lax.ppermute(value, AXES, permutation(target))
 
 
 def to_group(zl, y, x, zh, c):
@@ -114,8 +121,13 @@
     )(where, *pieces)
 
 
-def gather_far(near):
-    own = direct(near, X)
+def gather_far(near, where=None, after=None):
+    if where is None:
+        own = direct(near, X)
+    else:
+        left, right = shifted(near, X, 1), shifted(near, X, -1)
+        _, passed = lax.optimization_barrier((after, jnp.where(where[C] == 0, right, left)))
+        own = [near, left, right, folded(passed)]
     return own + [shifted(piece, C, 1) for piece in own]
 
 
@@ -138,7 +150,7 @@
     return jnp.dot(a, b, preferred_element_type=jnp.float32)
 
 
-def encode(value, out, low):
+def encode(value, out):
     rows, n = value.shape
     top = jnp.max(jnp.max(jnp.abs(value), axis=0, keepdims=True), axis=1, keepdims=True)
     top = jnp.maximum(top, 1e-30).astype(jnp.bfloat16)
@@ -146,8 +158,8 @@
     sign = power < 0
     for _ in range(3):
         power = power * power
-    out[:rows, low:low + n] = jnp.where(sign, -power, power).astype(jnp.bfloat16)
-    out[rows:, low:low + n] = jnp.broadcast_to(top, (16, n))
+    out[:rows, :] = jnp.where(sign, -power, power).astype(jnp.bfloat16)
+    out[rows:, :] = jnp.broadcast_to(top, (16, n))
 
 
 def decode(coded):
@@ -161,8 +173,9 @@
 
 
 def rotate_kernel(where, *refs):
-    pieces, (act_ref, grad_ref), outs = refs[:8], refs[8:10], refs[-9:-5]
-    panel, act, grad, in_sems, basis_sems = refs[-5:]
+    pieces, (act_ref, grad_ref) = refs[:8], refs[8:10]
+    outs, act_kept, act_sent = refs[-12:-8], refs[-8], refs[-7]
+    panel, act, grad, held, in_sems, basis_sems = refs[-6:]
     n = act.shape[1]
     loads = [
         pltpu.make_async_copy(act_ref, act, basis_sems.at[0]),
@@ -172,33 +185,49 @@
         load.start()
     for copy in loads + fetch(where, pieces, panel, in_sems):
         copy.wait()
-    for out, step in zip(outs, STEPS):
+
+    def product(basis, low, k, slot):
+        total = None
+        for h in range(2):
+            for c in range(2):
+                rows = basis[(2 * h + c) * k:(2 * h + c + 1) * k, :]
+                term = dot(panel[c, slot, h, :, low:low + k], rows)
+                total = term if total is None else total + term
+        return total
+
+    rows = act_kept.shape[1]
+    for i, (out, step) in enumerate(zip(outs, STEPS)):
         slot = (where[Y] + step) & 3
-        for basis, low, k in ((act, 0, n), (grad, n, 2 * n)):
-            total = None
-            for h in range(2):
-                for c in range(2):
-                    rows = basis[(2 * h + c) * k:(2 * h + c + 1) * k, :]
-                    term = dot(panel[c, slot, h, :, low:low + k], rows)
-                    total = term if total is None else total + term
-            if step == 0:
-                out[:, low:low + k] = total
-            else:
-                encode(total, out, low)
+        total = product(grad, n, 2 * n, slot)
+        if step == 0:
+            out[...] = total
+        else:
+            encode(total, out)
+        total = product(act, 0, n, slot)
+        held[0, i] = total[:rows]
+        held[1, i] = total[rows:]
+    act_kept[...] = held[where[ZL]]
+    encode(held[1 - where[ZL]].reshape(4 * rows, n), act_sent)
 
 
 def rotate(where, pieces, basis_act, basis_grad, after):
     rows, k = pieces[0].shape[1:]
+    n = k // 3
     f32, bf16 = jnp.float32, jnp.bfloat16
     return pl.pallas_call(
         rotate_kernel,
-        out_shape=[jax.ShapeDtypeStruct((rows, k), f32)]
-        + [jax.ShapeDtypeStruct((rows + 16, k), bf16)] * 3,
+        out_shape=[jax.ShapeDtypeStruct((rows, 2 * n), f32)]
+        + [jax.ShapeDtypeStruct((rows + 16, 2 * n), bf16)] * 3
+        + [
+            jax.ShapeDtypeStruct((4, rows // 2, n), f32),
+            jax.ShapeDtypeStruct((2 * rows + 16, n), bf16),
+        ],
         in_specs=[SCALARS] + [ANY] * (10 + len(after)),
         scratch_shapes=[
             pltpu.VMEM((2, 4, 2, rows, k), bf16),
             pltpu.VMEM(basis_act.shape, bf16),
             pltpu.VMEM(basis_grad.shape, bf16),
+            pltpu.VMEM((2, 4, rows // 2, n), f32),
             pltpu.SemaphoreType.DMA((4, 2)),
             pltpu.SemaphoreType.DMA((2,)),
         ],
@@ -339,10 +368,7 @@
     for i in range(2):
         total[i] = whole[i * rows:(i + 1) * rows]
     kept[...] = total[where[ZL]]
-    n = kept.shape[1] // 3
-    other = total[1 - where[ZL]]
-    encode(other[:, :n], sent, 0)
-    encode(other[:, n:], sent, n)
+    encode(total[1 - where[ZL]], sent)
 
 
 def sum_over_y(parts, where, after=()):
@@ -362,25 +388,50 @@
     )(where, *parts, *after)
 
 
-def square_kernel(kept, arrived, act, grad):
-    n = act.shape[0]
+def grad_square_kernel(kept, arrived, out):
     total = kept[...] + decode(arrived)
-    square = total * total
-    act[...] = square[:, :n].T.astype(jnp.bfloat16)
-    grad[...] = square[:, n:].astype(jnp.bfloat16)
-
-
-def square_of_sum(kept, sent):
-    rows, n = kept.shape[0], kept.shape[1] // 3
-    return pl.pallas_call(
-        square_kernel,
-        out_shape=[
-            jax.ShapeDtypeStruct((n, rows), jnp.bfloat16),
-            jax.ShapeDtypeStruct((rows, 2 * n), jnp.bfloat16),
-        ],
+    out[...] = (total * total).astype(jnp.bfloat16)
+
+
+def grad_squares(kept, sent):
+    return pl.pallas_call(
+        grad_square_kernel,
+        out_shape=jax.ShapeDtypeStruct(kept.shape, jnp.bfloat16),
         compiler_params=PARAMS,
         cost_estimate=CHEAP,
     )(kept, shifted(sent, ZL, 1))
+
+
+def split_kernel(kept, arrived, *outs):
+    rows, n = kept.shape[1:]
+    total = kept[...] + decode(arrived).reshape(4, rows, n)
+    outs[0][...] = total[0]
+    for i in range(1, 4):
+        encode(total[i], outs[i])
+
+
+def act_square_kernel(own, *refs):
+    total = own[...]
+    for coded in refs[:3]:
+        total = total + decode(coded)
+    refs[3][...] = (total * total).T.astype(jnp.bfloat16)
+
+
+def act_squares(kept, sent):
+    rows, n = kept.shape[1:]
+    parts = pl.pallas_call(
+        split_kernel,
+        out_shape=[jax.ShapeDtypeStruct((rows, n), jnp.float32)]
+        + [jax.ShapeDtypeStruct((rows + 16, n), jnp.bfloat16)] * 3,
+        compiler_params=PARAMS,
+        cost_estimate=CHEAP,
+    )(kept, shifted(sent, ZL, 1))
+    return parts[0], pl.pallas_call(
+        act_square_kernel,
+        out_shape=jax.ShapeDtypeStruct((n, rows), jnp.bfloat16),
+        compiler_params=PARAMS,
+        cost_estimate=CHEAP,
+    )(*[part if step == 0 else shifted(part, Y, step) for step, part in zip(STEPS, parts)])
 
 
 def pair_kernel(axis, where, own, other, pair, sems):
@@ -442,11 +493,13 @@
     own = direct(turned, Y)
     near = gather_near(block, where, False, own[1:])
     stack = stack_up(where, own)
-    panel = gather_far(near)
+    stack, near = lax.optimization_barrier((stack, near))
     stacks = (stack, shifted(stack, ZL, 1))
-    parts = rotate(where, panel, basis_act, basis_grad, stacks)
+    panel = gather_far(near, where, stacks[1])
+    *parts, act_kept, act_sent = rotate(where, panel, basis_act, basis_grad, stacks)
     cov_act, cov_grad, done = covariance(where, panel, stacks)
-    sq_act, sq_grad = square_of_sum(*sum_over_y(parts, where, (done,)))
+    split, sq_act = act_squares(act_kept, act_sent)
+    sq_grad = grad_squares(*sum_over_y(parts, where, (done, split)))
     block = lax.ppermute(sq_act, AXES, permutation(to_group))
     pair = pair_up(sq_grad, where, 0)
     pair, block = lax.optimization_barrier((pair, block))

time: 177 us -> 167 us (0.944)
  starting transfers between devices: 98.7 us -> 86.9 us
  waiting for transfers between devices: 44.6 us -> 46.8 us
    ppermute x32 -> x35, starting transfers between devices: 97.4 us -> 85.6 us  [shifted(): return lax.ppermute(value, AXES, permutation(target))]
    ppermute x0 -> x1, waiting for transfers between devices: none -> 7.83 us  [folded(): return lax.ppermute(value, AXES, permutation(target))]
    ppermute x32 -> x35, waiting for transfers between devices: 44.6 us -> 38.9 us  [shifted(): return lax.ppermute(value, AXES, permutation(target))]
    pallas_call x2 -> x4, Pallas kernels: 7.35 us -> 8.42 us  [the longest x1 6.91 us: rotate(): pl.pallas_call(rotate_kernel, out_shape=[jax.ShapeDtypeStruct((rows, 2 *...]
    unnamed x24 -> x22, local copies, waits for them, and re-layouts: 6.11 us -> 6.04 us
  transfers between devices with their start and end apart: 34 -> 38, of which waited for: 11 -> 10; matrix products, arithmetic and copies ran while one was open for 0% -> 0% of each run, Pallas kernels for 5% -> 7%
where the time goes in v2:
time: 167 us
  starting transfers between devices  86.9 us (52%)
  waiting for transfers between devices  46.8 us (28%)
  Pallas kernels  25.8 us (15%)
  local copies, waits for them, and re-layouts  6.12 us (4%)
    ppermute x35, starting transfers between devices, shifted(): return lax.ppermute(value, AXES, permutation(target))  85.6 us
    ppermute x35, waiting for transfers between devices, shifted(): return lax.ppermute(value, AXES, permutation(target))  38.9 us
    ppermute x1, waiting for transfers between devices, folded(): return lax.ppermute(value, AXES, permutation(target))  7.83 us
    pallas_call x1, Pallas kernels, rotate(): pl.pallas_call(rotate_kernel, out_shape=[jax.ShapeDtypeStruct((rows, 2 *...  6.91 us
    pallas_call x1, Pallas kernels, covariance(): pl.pallas_call(covariance_kernel, out_shape=[jax.ShapeDtypeStruct((n, 4 *...  6.89 us
    unnamed x22, local copies, waits for them, and re-layouts  6.04 us
  transfers between devices with their start and end apart: 38, of which 10 were waited for; matrix products, arithmetic and copies ran while one was open for 0% of the time, Pallas kernels for 7%

profile of v2, /device:TPU:1, one launch (start us, length us, event | category | flops | bytes accessed | tf_op | source)
XLA Modules:
  0.0 166.8 jit_solution(14480110138094190332)
XLA Ops:
  3.2 13.5 %collective-permute-start.1 = (bf16[768,128]{1,0:T(8,128)(2,1)S(1)}, bf16[768,128]{1,0:T(8,128)(2,1)S(1)}, u32[]{:S(2)}, u32[]{:S(2)}) collective-permute-start(bf16[768,128]{1,0:T(8,128)(2,1)S(1)} %get-tuple-element.28.refs_0_), channel_id=1, source_target_pairs={{0,32},{1,33},{2,34},{3,35},{4,36},{5,37},{6,38},{7,39},{8,40},{9,... | collective-permute-start | bytes 589832 | tf_op jit(solution)/shard_map/ppermute | solution.py:40
  22.7 3.5 %collective-permute-start.5 = (bf16[128,768]{1,0:T(8,128)(2,1)S(1)}, bf16[128,768]{1,0:T(8,128)(2,1)S(1)}, u32[]{:S(2)}, u32[]{:S(2)}) collective-permute-start(bf16[128,768]{1,0:T(8,128)(2,1)S(1)} %collective-permute-done.refs_1_), channel_id=1, source_target_pairs={{0,6},{1,7},{2,0},{3,1},{4,2},{5,3},{6,4},{7,5},{8,14},{9,15},{10,... | collective-permute-start | bytes 589832 | tf_op jit(solution)/shard_map/ppermute | solution.py:40
  26.2 2.7 %collective-permute-start.6 = (bf16[128,768]{1,0:T(8,128)(2,1)S(1)}, bf16[128,768]{1,0:T(8,128)(2,1)S(1)}, u32[]{:S(2)}, u32[]{:S(2)}) collective-permute-start(bf16[128,768]{1,0:T(8,128)(2,1)S(1)} %collective-permute-done.refs_1_), channel_id=1, source_target_pairs={{0,4},{1,5},{2,6},{3,7},{4,0},{5,1},{6,2},{7,3},{8,12},{9,13},{10,... | collective-permute-start | bytes 589832 | tf_op jit(solution)/shard_map/ppermute | solution.py:40
  30.6 10.7 %collective-permute-done.6.refs_4_ = bf16[128,768]{1,0:T(8,128)(2,1)S(1)} collective-permute-done((bf16[128,768]{1,0:T(8,128)(2,1)S(1)}, bf16[128,768]{1,0:T(8,128)(2,1)S(1)}, u32[]{:S(2)}, u32[]{:S(2)}) %collective-permute-start.6) | collective-permute-done | bytes 196640 | tf_op jit(solution)/shard_map/ppermute | solution.py:40
  43.0 3.2 %collective-permute-start.8 = (bf16[2,256,768]{2,1,0:T(8,128)(2,1)S(1)}, bf16[2,256,768]{2,1,0:T(8,128)(2,1)S(1)}, u32[]{:S(2)}, u32[]{:S(2)}) collective-permute-start(bf16[2,256,768]{2,1,0:T(8,128)(2,1)S(1)} %shard_map.69.refs_0_), channel_id=1, source_target_pairs={{0,24},{1,25},{2,26},{3,27},{4,28},{5,29},{6,30},{7,31},{8,0},{9,1... | collective-permute-start | bytes 2359304 | tf_op jit(solution)/shard_map/ppermute | solution.py:40
  46.2 6.0 %collective-permute-start.9 = (bf16[4,768,128]{2,1,0:T(8,128)(2,1)S(1)}, bf16[4,768,128]{2,1,0:T(8,128)(2,1)}, u32[]{:S(2)}, u32[]{:S(2)}) collective-permute-start(bf16[4,768,128]{2,1,0:T(8,128)(2,1)S(1)} %shard_map.68.refs_8_.refs_10_), channel_id=1, source_target_pairs={{0,128},{1,129},{2,130},{3,131},{4,132},{5,133},{6,134},{7,135},{8... | collective-permute-start | bytes 2359304 | tf_op jit(solution)/shard_map/ppermute | solution.py:40
  52.3 6.8 %collective-permute-done.7.refs_1_ = bf16[2,256,768]{2,1,0:T(8,128)(2,1)S(1)} collective-permute-done((bf16[2,256,768]{2,1,0:T(8,128)(2,1)S(1)}, bf16[2,256,768]{2,1,0:T(8,128)(2,1)S(1)}, u32[]{:S(2)}, u32[]{:S(2)}) %collective-permute-start.7) | collective-permute-done | bytes 786464 | tf_op jit(solution)/shard_map/ppermute | solution.py:40
  59.1 4.7 %collective-permute-done.8.refs_2_ = bf16[2,256,768]{2,1,0:T(8,128)(2,1)S(1)} collective-permute-done((bf16[2,256,768]{2,1,0:T(8,128)(2,1)S(1)}, bf16[2,256,768]{2,1,0:T(8,128)(2,1)S(1)}, u32[]{:S(2)}, u32[]{:S(2)}) %collective-permute-start.8) | collective-permute-done | bytes 786464 | tf_op jit(solution)/shard_map/ppermute | solution.py:40
  63.9 4.1 %collective-permute-done.9.refs_9_.refs_11_ = bf16[4,768,128]{2,1,0:T(8,128)(2,1)} collective-permute-done((bf16[4,768,128]{2,1,0:T(8,128)(2,1)S(1)}, bf16[4,768,128]{2,1,0:T(8,128)(2,1)}, u32[]{:S(2)}, u32[]{:S(2)}) %collective-permute-start.9) | collective-permute-done | bytes 786464 | tf_op jit(solution)/shard_map/ppermute | solution.py:40
  68.0 3.7 %collective-permute-start.11 = (bf16[2,256,768]{2,1,0:T(8,128)(2,1)S(1)}, bf16[2,256,768]{2,1,0:T(8,128)(2,1)S(1)}, u32[]{:S(2)}, u32[]{:S(2)}) collective-permute-start(bf16[2,256,768]{2,1,0:T(8,128)(2,1)S(1)} %shard_map.69.refs_0_), channel_id=1, source_target_pairs={{0,1},{1,0},{2,3},{3,2},{4,5},{5,4},{6,7},{7,6},{8,9},{9,8},{10,11... | collective-permute-start | bytes 2359304 | tf_op jit(solution)/shard_map/ppermute | solution.py:40
  72.2 7.8 %collective-permute-done.10.refs_3_ = bf16[2,256,768]{2,1,0:T(8,128)(2,1)S(1)} collective-permute-done((bf16[2,256,768]{2,1,0:T(8,128)(2,1)S(1)}, bf16[2,256,768]{2,1,0:T(8,128)(2,1)S(1)}, u32[]{:S(2)}, u32[]{:S(2)}) %collective-permute-start.10) | collective-permute-done | bytes 786464 | tf_op jit(solution)/shard_map/ppermute | solution.py:51
  80.0 2.9 %collective-permute-start.14 = (bf16[2,256,768]{2,1,0:T(8,128)(2,1)S(1)}, bf16[2,256,768]{2,1,0:T(8,128)(2,1)S(1)}, u32[]{:S(2)}, u32[]{:S(2)}) collective-permute-start(bf16[2,256,768]{2,1,0:T(8,128)(2,1)S(1)} %collective-permute-done.10.refs_3_), channel_id=1, source_target_pairs={{0,1},{1,0},{2,3},{3,2},{4,5},{5,4},{6,7},{7,6},{8,9},{9,8},{10,11... | collective-permute-start | bytes 2359304 | tf_op jit(solution)/shard_map/ppermute | solution.py:40
  85.7 6.9 %shard_map.71 = (f32[256,512]{1,0:T(8,128)S(1)}, bf16[272,512]{1,0:T(8,128)(2,1)S(1)}, bf16[272,512]{1,0:T(8,128)(2,1)S(1)}, bf16[272,512]{1,0:T(8,128)(2,1)S(1)...) custom-call(s32[5]{0:T(128)S(1)} %stack.23.where.refs_0_, bf16[2,256,768]{2,1,0:T(8,128)(2,1)S(1)} %shard_map.69.refs_0_, ...), custom_call_target="tpu_custom_call" | custom-call | flops 1000 | bytes 1000 | tf_op jit(solution)/shard_map/pallas_call | solution.py:217
  92.7 2.7 %collective-permute-start.16 = (bf16[272,512]{1,0:T(8,128)(2,1)S(1)}, bf16[272,512]{1,0:T(8,128)(2,1)S(1)}, u32[]{:S(2)}, u32[]{:S(2)}) collective-permute-start(bf16[272,512]{1,0:T(8,128)(2,1)S(1)} %get-tuple-element.36), channel_id=1, source_target_pairs={{0,96},{1,97},{2,98},{3,99},{4,100},{5,101},{6,102},{7,103},{8,104... | collective-permute-start | bytes 835592 | tf_op jit(solution)/shard_map/ppermute | solution.py:40
  100.2 6.9 %shard_map.70 = (f32[256,1024]{1,0:T(8,128)}, f32[512,2048]{1,0:T(8,128)}, f32[8,128]{1,0:T(8,128)S(1)}) custom-call(s32[5]{0:T(128)S(1)} %stack.23.where.refs_0_, bf16[2,256,768]{2,1,0:T(8,128)(2,1)S(1)} %shard_map.69.refs_0_, bf16[2,256,768]{2,1,0:T(8,128)(2,1)S(1)} %collective-permute-done.7.refs_1_, ...), custom_call_target="tpu_custom_call" | custom-call | flops 1000 | bytes 1000 | tf_op jit(solution)/shard_map/pallas_call | solution.py:285
  116.8 3.0 %collective-permute-done.23.refs_2_ = bf16[144,256]{1,0:T(8,128)(2,1)S(1)} collective-permute-done((bf16[144,256]{1,0:T(8,128)(2,1)S(1)}, bf16[144,256]{1,0:T(8,128)(2,1)S(1)}, u32[]{:S(2)}, u32[]{:S(2)}) %collective-permute-start.23) | collective-permute-done | bytes 73760 | tf_op jit(solution)/shard_map/ppermute | solution.py:40
  121.9 3.6 %collective-permute-start.28 = (bf16[256,512]{1,0:T(8,128)(2,1)S(1)}, bf16[256,512]{1,0:T(8,128)(2,1)S(1)}, u32[]{:S(2)}, u32[]{:S(2)}) collective-permute-start(bf16[256,512]{1,0:T(8,128)(2,1)S(1)} %shard_map.75.refs_8_), channel_id=1, source_target_pairs={{0,32},{1,33},{2,34},{3,35},{4,36},{5,37},{6,38},{7,39},{8,40},{9,... | collective-permute-start | bytes 786440 | tf_op jit(solution)/shard_map/ppermute | solution.py:40
  125.4 4.1 %collective-permute-start.29 = (bf16[256,512]{1,0:T(8,128)(2,1)S(1)}, bf16[256,512]{1,0:T(8,128)(2,1)S(1)}, u32[]{:S(2)}, u32[]{:S(2)}) collective-permute-start(bf16[256,512]{1,0:T(8,128)(2,1)S(1)} %shard_map.75.refs_8_), channel_id=1, source_target_pairs={{0,96},{1,97},{2,98},{3,99},{4,100},{5,101},{6,102},{7,103},{8,104... | collective-permute-start | bytes 786440 | tf_op jit(solution)/shard_map/ppermute | solution.py:40
  130.5 2.6 %collective-permute-start.26 = (bf16[256,128]{1,0:T(8,128)(2,1)S(1)}, bf16[256,128]{1,0:T(8,128)(2,1)S(1)}, u32[]{:S(2)}, u32[]{:S(2)}) collective-permute-start(bf16[256,128]{1,0:T(8,128)(2,1)S(1)} %collective-permute-done.24.refs_1_), channel_id=1, source_target_pairs={{0,6},{1,7},{2,0},{3,1},{4,2},{5,3},{6,4},{7,5},{8,14},{9,15},{10,... | collective-permute-start | bytes 196616 | tf_op jit(solution)/shard_map/ppermute | solution.py:40
  134.8 5.7 %collective-permute-done.27.refs_4_ = bf16[256,128]{1,0:T(8,128)(2,1)S(1)} collective-permute-done((bf16[256,128]{1,0:T(8,128)(2,1)S(1)}, bf16[256,128]{1,0:T(8,128)(2,1)S(1)}, u32[]{:S(2)}, u32[]{:S(2)}) %collective-permute-start.27) | collective-permute-done | bytes 65568 | tf_op jit(solution)/shard_map/ppermute | solution.py:40
  141.2 6.5 %collective-permute-start.31 = (bf16[2,256,256]{2,1,0:T(8,128)(2,1)S(1)}, bf16[2,256,256]{2,1,0:T(8,128)(2,1)S(1)}, u32[]{:S(2)}, u32[]{:S(2)}) collective-permute-start(bf16[2,256,256]{2,1,0:T(8,128)(2,1)S(1)} %shard_map.77.refs_0_), channel_id=1, source_target_pairs={{0,24},{1,25},{2,26},{3,27},{4,28},{5,29},{6,30},{7,31},{8,0},{9,1... | collective-permute-start | bytes 786440 | tf_op jit(solution)/shard_map/ppermute | solution.py:40
  149.3 7.0 %collective-permute-start.33 = (bf16[2,256,256]{2,1,0:T(8,128)(2,1)S(1)}, bf16[2,256,256]{2,1,0:T(8,128)(2,1)S(1)}, u32[]{:S(2)}, u32[]{:S(2)}) collective-permute-start(bf16[2,256,256]{2,1,0:T(8,128)(2,1)S(1)} %shard_map.77.refs_0_), channel_id=1, source_target_pairs={{0,1},{1,0},{2,3},{3,2},{4,5},{5,4},{6,7},{7,6},{8,9},{9,8},{10,11... | collective-permute-start | bytes 786440 | tf_op jit(solution)/shard_map/ppermute | solution.py:40
  156.3 2.6 %collective-permute-start.34 = (bf16[2,256,256]{2,1,0:T(8,128)(2,1)S(1)}, bf16[2,256,256]{2,1,0:T(8,128)(2,1)S(1)}, u32[]{:S(2)}, u32[]{:S(2)}) collective-permute-start(bf16[2,256,256]{2,1,0:T(8,128)(2,1)S(1)} %collective-permute-done.30.refs_1_), channel_id=1, source_target_pairs={{0,1},{1,0},{2,3},{3,2},{4,5},{5,4},{6,7},{7,6},{8,9},{9,8},{10,11... | collective-permute-start | bytes 786440 | tf_op jit(solution)/shard_map/ppermute | solution.py:40
  163.6 3.0 %shard_map.78 = f32[1024,512]{1,0:T(8,128)} custom-call(s32[5]{0:T(128)S(1)} %stack.23.where.refs_0_, bf16[2,256,256]{2,1,0:T(8,128)(2,1)S(1)} %shard_map.77.refs_0_, bf16[2,256,256]{2,1,0:T(8,128)(2,1)S(1)} %collective-permute-done.30.refs_1_, bf16[2,256,256]{2,1,0:T(8,128)(2,1)S(1)} %collective-permute-done.31.refs_2_, ...), custom_call_target="tpu_custom_call" | custom-call | flops 1000 | bytes 1000 | tf_op jit(solution)/shard_map/pallas_call | solution.py:344
  (88 shorter events, 41.6 us)
Async XLA Ops:
  3.2 23.0 %collective-permute-start.1 = (bf16[768,128]{1,0:T(8,128)(2,1)S(1)}, bf16[768,128]{1,0:T(8,128)(2,1)S(1)}, u32[]{:S(2)}, u32[]{:S(2)}) collective-permute-start(bf16[768,128]{1,0:T(8,128)(2,1)S(1)} %get-tuple-element.28.refs_0_), channel_id=1, source_target_pairs={{0,32},{1,33},{2,34},{3,35},{4,36},{5,37},{6,38},{7,39},{8,40},{9,... | collective-permute-start | bytes 589832 | tf_op jit(solution)/shard_map/ppermute | solution.py:40
  16.7 12.2 %collective-permute-start.2 = (bf16[768,128]{1,0:T(8,128)(2,1)S(1)}, bf16[768,128]{1,0:T(8,128)(2,1)S(1)}, u32[]{:S(2)}, u32[]{:S(2)}) collective-permute-start(bf16[768,128]{1,0:T(8,128)(2,1)S(1)} %get-tuple-element.28.refs_0_), channel_id=1, source_target_pairs={{0,96},{1,97},{2,98},{3,99},{4,100},{5,101},{6,102},{7,103},{8,104... | collective-permute-start | bytes 589832 | tf_op jit(solution)/shard_map/ppermute | solution.py:40
  19.3 9.7 %collective-permute-start.3 = (bf16[768,128]{1,0:T(8,128)(2,1)S(1)}, bf16[768,128]{1,0:T(8,128)(2,1)S(1)}, u32[]{:S(2)}, u32[]{:S(2)}) collective-permute-start(bf16[768,128]{1,0:T(8,128)(2,1)S(1)} %get-tuple-element.28.refs_0_), channel_id=1, source_target_pairs={{0,64},{1,65},{2,66},{3,67},{4,68},{5,69},{6,70},{7,71},{8,72},{9,... | collective-permute-start | bytes 589832 | tf_op jit(solution)/shard_map/ppermute | solution.py:40
  20.5 10.1 %collective-permute-start.4 = (bf16[128,768]{1,0:T(8,128)(2,1)S(1)}, bf16[128,768]{1,0:T(8,128)(2,1)S(1)}, u32[]{:S(2)}, u32[]{:S(2)}) collective-permute-start(bf16[128,768]{1,0:T(8,128)(2,1)S(1)} %collective-permute-done.refs_1_), channel_id=1, source_target_pairs={{0,2},{1,3},{2,4},{3,5},{4,6},{5,7},{6,0},{7,1},{8,10},{9,11},{10,... | collective-permute-start | bytes 589832 | tf_op jit(solution)/shard_map/ppermute | solution.py:40
  22.7 7.9 %collective-permute-start.5 = (bf16[128,768]{1,0:T(8,128)(2,1)S(1)}, bf16[128,768]{1,0:T(8,128)(2,1)S(1)}, u32[]{:S(2)}, u32[]{:S(2)}) collective-permute-start(bf16[128,768]{1,0:T(8,128)(2,1)S(1)} %collective-permute-done.refs_1_), channel_id=1, source_target_pairs={{0,6},{1,7},{2,0},{3,1},{4,2},{5,3},{6,4},{7,5},{8,14},{9,15},{10,... | collective-permute-start | bytes 589832 | tf_op jit(solution)/shard_map/ppermute | solution.py:40
  26.2 15.1 %collective-permute-start.6 = (bf16[128,768]{1,0:T(8,128)(2,1)S(1)}, bf16[128,768]{1,0:T(8,128)(2,1)S(1)}, u32[]{:S(2)}, u32[]{:S(2)}) collective-permute-start(bf16[128,768]{1,0:T(8,128)(2,1)S(1)} %collective-permute-done.refs_1_), channel_id=1, source_target_pairs={{0,4},{1,5},{2,6},{3,7},{4,0},{5,1},{6,2},{7,3},{8,12},{9,13},{10,... | collective-permute-start | bytes 589832 | tf_op jit(solution)/shard_map/ppermute | solution.py:40
  42.9 16.2 %collective-permute-start.7 = (bf16[2,256,768]{2,1,0:T(8,128)(2,1)S(1)}, bf16[2,256,768]{2,1,0:T(8,128)(2,1)S(1)}, u32[]{:S(2)}, u32[]{:S(2)}) collective-permute-start(bf16[2,256,768]{2,1,0:T(8,128)(2,1)S(1)} %shard_map.69.refs_0_), channel_id=1, source_target_pairs={{0,8},{1,9},{2,10},{3,11},{4,12},{5,13},{6,14},{7,15},{8,16},{9,17... | collective-permute-start | bytes 2359304 | tf_op jit(solution)/shard_map/ppermute | solution.py:40
  43.0 20.8 %collective-permute-start.8 = (bf16[2,256,768]{2,1,0:T(8,128)(2,1)S(1)}, bf16[2,256,768]{2,1,0:T(8,128)(2,1)S(1)}, u32[]{:S(2)}, u32[]{:S(2)}) collective-permute-start(bf16[2,256,768]{2,1,0:T(8,128)(2,1)S(1)} %shard_map.69.refs_0_), channel_id=1, source_target_pairs={{0,24},{1,25},{2,26},{3,27},{4,28},{5,29},{6,30},{7,31},{8,0},{9,1... | collective-permute-start | bytes 2359304 | tf_op jit(solution)/shard_map/ppermute | solution.py:40
  46.2 21.7 %collective-permute-start.9 = (bf16[4,768,128]{2,1,0:T(8,128)(2,1)S(1)}, bf16[4,768,128]{2,1,0:T(8,128)(2,1)}, u32[]{:S(2)}, u32[]{:S(2)}) collective-permute-start(bf16[4,768,128]{2,1,0:T(8,128)(2,1)S(1)} %shard_map.68.refs_8_.refs_10_), channel_id=1, source_target_pairs={{0,128},{1,129},{2,130},{3,131},{4,132},{5,133},{6,134},{7,135},{8... | collective-permute-start | bytes 2359304 | tf_op jit(solution)/shard_map/ppermute | solution.py:40
  68.0 12.1 %collective-permute-start.10 = (bf16[2,256,768]{2,1,0:T(8,128)(2,1)S(1)}, bf16[2,256,768]{2,1,0:T(8,128)(2,1)S(1)}, u32[]{:S(2)}, u32[]{:S(2)}) collective-permute-start(bf16[2,256,768]{2,1,0:T(8,128)(2,1)S(1)} %broadcast_select_fusion), channel_id=1, source_target_pairs={{0,24},{1,9},{2,26},{3,11},{4,28},{5,13},{6,30},{7,15},{8,0},{9,17... | collective-permute-start | bytes 2359304 | tf_op jit(solution)/shard_map/ppermute | solution.py:51
  68.0 14.9 %collective-permute-start.11 = (bf16[2,256,768]{2,1,0:T(8,128)(2,1)S(1)}, bf16[2,256,768]{2,1,0:T(8,128)(2,1)S(1)}, u32[]{:S(2)}, u32[]{:S(2)}) collective-permute-start(bf16[2,256,768]{2,1,0:T(8,128)(2,1)S(1)} %shard_map.69.refs_0_), channel_id=1, source_target_pairs={{0,1},{1,0},{2,3},{3,2},{4,5},{5,4},{6,7},{7,6},{8,9},{9,8},{10,11... | collective-permute-start | bytes 2359304 | tf_op jit(solution)/shard_map/ppermute | solution.py:40
  71.7 11.2 %collective-permute-start.12 = (bf16[2,256,768]{2,1,0:T(8,128)(2,1)S(1)}, bf16[2,256,768]{2,1,0:T(8,128)(2,1)S(1)}, u32[]{:S(2)}, u32[]{:S(2)}) collective-permute-start(bf16[2,256,768]{2,1,0:T(8,128)(2,1)S(1)} %collective-permute-done.7.refs_1_), channel_id=1, source_target_pairs={{0,1},{1,0},{2,3},{3,2},{4,5},{5,4},{6,7},{7,6},{8,9},{9,8},{10,11... | collective-permute-start | bytes 2359304 | tf_op jit(solution)/shard_map/ppermute | solution.py:40
  71.7 11.2 %collective-permute-start.13 = (bf16[2,256,768]{2,1,0:T(8,128)(2,1)S(1)}, bf16[2,256,768]{2,1,0:T(8,128)(2,1)S(1)}, u32[]{:S(2)}, u32[]{:S(2)}) collective-permute-start(bf16[2,256,768]{2,1,0:T(8,128)(2,1)S(1)} %collective-permute-done.8.refs_2_), channel_id=1, source_target_pairs={{0,1},{1,0},{2,3},{3,2},{4,5},{5,4},{6,7},{7,6},{8,9},{9,8},{10,11... | collective-permute-start | bytes 2359304 | tf_op jit(solution)/shard_map/ppermute | solution.py:40
  92.6 15.3 %collective-permute-start.15 = (bf16[272,512]{1,0:T(8,128)(2,1)S(1)}, bf16[272,512]{1,0:T(8,128)(2,1)S(1)}, u32[]{:S(2)}, u32[]{:S(2)}) collective-permute-start(bf16[272,512]{1,0:T(8,128)(2,1)S(1)} %get-tuple-element.35), channel_id=1, source_target_pairs={{0,32},{1,33},{2,34},{3,35},{4,36},{5,37},{6,38},{7,39},{8,40},{9,... | collective-permute-start | bytes 835592 | tf_op jit(solution)/shard_map/ppermute | solution.py:40
  92.7 15.3 %collective-permute-start.16 = (bf16[272,512]{1,0:T(8,128)(2,1)S(1)}, bf16[272,512]{1,0:T(8,128)(2,1)S(1)}, u32[]{:S(2)}, u32[]{:S(2)}) collective-permute-start(bf16[272,512]{1,0:T(8,128)(2,1)S(1)} %get-tuple-element.36), channel_id=1, source_target_pairs={{0,96},{1,97},{2,98},{3,99},{4,100},{5,101},{6,102},{7,103},{8,104... | collective-permute-start | bytes 835592 | tf_op jit(solution)/shard_map/ppermute | solution.py:40
  95.3 12.6 %collective-permute-start.17 = (bf16[272,512]{1,0:T(8,128)(2,1)S(1)}, bf16[272,512]{1,0:T(8,128)(2,1)S(1)}, u32[]{:S(2)}, u32[]{:S(2)}) collective-permute-start(bf16[272,512]{1,0:T(8,128)(2,1)S(1)} %get-tuple-element.37), channel_id=1, source_target_pairs={{0,64},{1,65},{2,66},{3,67},{4,68},{5,69},{6,70},{7,71},{8,72},{9,... | collective-permute-start | bytes 835592 | tf_op jit(solution)/shard_map/ppermute | solution.py:40
  95.3 11.8 %collective-permute-start.18 = (bf16[528,256]{1,0:T(8,128)(2,1)S(1)}, bf16[528,256]{1,0:T(8,128)(2,1)S(1)}, u32[]{:S(2)}, u32[]{:S(2)}) collective-permute-start(bf16[528,256]{1,0:T(8,128)(2,1)S(1)} %get-tuple-element.40), channel_id=1, source_target_pairs={{0,128},{1,129},{2,130},{3,131},{4,132},{5,133},{6,134},{7,135},{8... | collective-permute-start | bytes 811016 | tf_op jit(solution)/shard_map/ppermute | solution.py:40
  121.9 18.6 %collective-permute-start.28 = (bf16[256,512]{1,0:T(8,128)(2,1)S(1)}, bf16[256,512]{1,0:T(8,128)(2,1)S(1)}, u32[]{:S(2)}, u32[]{:S(2)}) collective-permute-start(bf16[256,512]{1,0:T(8,128)(2,1)S(1)} %shard_map.75.refs_8_), channel_id=1, source_target_pairs={{0,32},{1,33},{2,34},{3,35},{4,36},{5,37},{6,38},{7,39},{8,40},{9,... | collective-permute-start | bytes 786440 | tf_op jit(solution)/shard_map/ppermute | solution.py:40
  125.4 15.0 %collective-permute-start.29 = (bf16[256,512]{1,0:T(8,128)(2,1)S(1)}, bf16[256,512]{1,0:T(8,128)(2,1)S(1)}, u32[]{:S(2)}, u32[]{:S(2)}) collective-permute-start(bf16[256,512]{1,0:T(8,128)(2,1)S(1)} %shard_map.75.refs_8_), channel_id=1, source_target_pairs={{0,96},{1,97},{2,98},{3,99},{4,100},{5,101},{6,102},{7,103},{8,104... | collective-permute-start | bytes 786440 | tf_op jit(solution)/shard_map/ppermute | solution.py:40
  141.1 15.2 %collective-permute-start.30 = (bf16[2,256,256]{2,1,0:T(8,128)(2,1)S(1)}, bf16[2,256,256]{2,1,0:T(8,128)(2,1)S(1)}, u32[]{:S(2)}, u32[]{:S(2)}) collective-permute-start(bf16[2,256,256]{2,1,0:T(8,128)(2,1)S(1)} %shard_map.77.refs_0_), channel_id=1, source_target_pairs={{0,8},{1,9},{2,10},{3,11},{4,12},{5,13},{6,14},{7,15},{8,16},{9,17... | collective-permute-start | bytes 786440 | tf_op jit(solution)/shard_map/ppermute | solution.py:40
  141.2 17.7 %collective-permute-start.31 = (bf16[2,256,256]{2,1,0:T(8,128)(2,1)S(1)}, bf16[2,256,256]{2,1,0:T(8,128)(2,1)S(1)}, u32[]{:S(2)}, u32[]{:S(2)}) collective-permute-start(bf16[2,256,256]{2,1,0:T(8,128)(2,1)S(1)} %shard_map.77.refs_0_), channel_id=1, source_target_pairs={{0,24},{1,25},{2,26},{3,27},{4,28},{5,29},{6,30},{7,31},{8,0},{9,1... | collective-permute-start | bytes 786440 | tf_op jit(solution)/shard_map/ppermute | solution.py:40
  147.7 12.9 %collective-permute-start.32 = (bf16[2,256,256]{2,1,0:T(8,128)(2,1)S(1)}, bf16[2,256,256]{2,1,0:T(8,128)(2,1)S(1)}, u32[]{:S(2)}, u32[]{:S(2)}) collective-permute-start(bf16[2,256,256]{2,1,0:T(8,128)(2,1)S(1)} %shard_map.77.refs_0_), channel_id=1, source_target_pairs={{0,16},{1,17},{2,18},{3,19},{4,20},{5,21},{6,22},{7,23},{8,24},{9,... | collective-permute-start | bytes 786440 | tf_op jit(solution)/shard_map/ppermute | solution.py:40
  148.8 13.6 %collective-permute-start.37 = (bf16[256,512]{1,0:T(8,128)(2,1)S(1)}, bf16[256,512]{1,0:T(8,128)(2,1)S(1)}, u32[]{:S(2)}, u32[]{:S(2)}) collective-permute-start(bf16[256,512]{1,0:T(8,128)(2,1)S(1)} %shard_map.75.refs_8_), channel_id=1, source_target_pairs={{0,64},{1,65},{2,66},{3,67},{4,68},{5,69},{6,70},{7,71},{8,72},{9,... | collective-permute-start | bytes 786440 | tf_op jit(solution)/shard_map/ppermute | solution.py:40
  149.3 13.1 %collective-permute-start.33 = (bf16[2,256,256]{2,1,0:T(8,128)(2,1)S(1)}, bf16[2,256,256]{2,1,0:T(8,128)(2,1)S(1)}, u32[]{:S(2)}, u32[]{:S(2)}) collective-permute-start(bf16[2,256,256]{2,1,0:T(8,128)(2,1)S(1)} %shard_map.77.refs_0_), channel_id=1, source_target_pairs={{0,1},{1,0},{2,3},{3,2},{4,5},{5,4},{6,7},{7,6},{8,9},{9,8},{10,11... | collective-permute-start | bytes 786440 | tf_op jit(solution)/shard_map/ppermute | solution.py:40
  (25 other events, 139.9 us)

commit v3 on v2

--- a/solution.py
+++ b/solution.py
@@ -17,6 +17,7 @@
 PARAMS = pltpu.CompilerParams(vmem_limit_bytes=48 * 1024 * 1024)
 
 CHEAP = pl.CostEstimate(flops=1000, bytes_accessed=1000, transcendentals=0)
+LONG = pl.CostEstimate(flops=5 * 10**9, bytes_accessed=20 * 10**6, transcendentals=0)
 
 
 def device_index(q):
@@ -121,14 +122,13 @@
     )(where, *pieces)
 
 
-def gather_far(near, where=None, after=None):
-    if where is None:
-        own = direct(near, X)
-    else:
-        left, right = shifted(near, X, 1), shifted(near, X, -1)
-        _, passed = lax.optimization_barrier((after, jnp.where(where[C] == 0, right, left)))
-        own = [near, left, right, folded(passed)]
+def gather_far(near):
+    own = direct(near, X)
     return own + [shifted(piece, C, 1) for piece in own]
+
+
+def relay(where, left, right):
+    return folded(jnp.where(where[C] == 0, right, left))
 
 
 def fetch(where, pieces, panel, sems):
@@ -172,68 +172,154 @@
     return jnp.where(power < 0, -root, root) * top
 
 
-def rotate_kernel(where, *refs):
-    pieces, (act_ref, grad_ref) = refs[:8], refs[8:10]
-    outs, act_kept, act_sent = refs[-12:-8], refs[-8], refs[-7]
+def product(panel, basis, low, k):
+    total = None
+    for h in range(2):
+        for c in range(2):
+            rows = basis[(2 * h + c) * k:(2 * h + c + 1) * k, :]
+            term = dot(panel(h, c)[:, low:low + k], rows)
+            total = term if total is None else total + term
+    return total
+
+
+def rotate_some_kernel(where, *refs):
+    pieces, (act_ref, grad_ref) = refs[:6], refs[6:8]
+    grad_full, grad_coded, act_kept, act_sent, token = refs[-11:-6]
     panel, act, grad, held, in_sems, basis_sems = refs[-6:]
+    token[...] = jnp.zeros_like(token)
     n = act.shape[1]
-    loads = [
+    copies = [
         pltpu.make_async_copy(act_ref, act, basis_sems.at[0]),
         pltpu.make_async_copy(grad_ref, grad, basis_sems.at[1]),
     ]
-    for load in loads:
-        load.start()
-    for copy in loads + fetch(where, pieces, panel, in_sems):
-        copy.wait()
-
-    def product(basis, low, k, slot):
-        total = None
-        for h in range(2):
-            for c in range(2):
-                rows = basis[(2 * h + c) * k:(2 * h + c + 1) * k, :]
-                term = dot(panel[c, slot, h, :, low:low + k], rows)
-                total = term if total is None else total + term
-        return total
-
+    for i in range(3):
+        for j in range(2):
+            copies.append(
+                pltpu.make_async_copy(
+                    pieces[i + 3 * j], panel.at[where[C] ^ j, i], in_sems.at[i, j]
+                )
+            )
+    for copy in copies:
+        copy.start()
+    for copy in copies:
+        copy.wait()
     rows = act_kept.shape[1]
-    for i, (out, step) in enumerate(zip(outs, STEPS)):
-        slot = (where[Y] + step) & 3
-        total = product(grad, n, 2 * n, slot)
-        if step == 0:
-            out[...] = total
-        else:
-            encode(total, out)
-        total = product(act, 0, n, slot)
-        held[0, i] = total[:rows]
-        held[1, i] = total[rows:]
-    act_kept[...] = held[where[ZL]]
-    encode(held[1 - where[ZL]].reshape(4 * rows, n), act_sent)
-
-
-def rotate(where, pieces, basis_act, basis_grad, after):
+    for i in range(3):
+        total = product(lambda h, c: panel[c, i, h], grad, n, 2 * n)
+        grad_full[i] = total
+        encode(total, grad_coded.at[i])
+        total = product(lambda h, c: panel[c, i, h], act, 0, n)
+        held[0] = total[:rows]
+        held[1] = total[rows:]
+        act_kept[i] = held[where[ZL]]
+        encode(held[1 - where[ZL]], act_sent.at[i])
+
+
+def rotate_some(where, pieces, basis_act, basis_grad):
     rows, k = pieces[0].shape[1:]
     n = k // 3
     f32, bf16 = jnp.float32, jnp.bfloat16
     return pl.pallas_call(
-        rotate_kernel,
+        rotate_some_kernel,
+        out_shape=[
+            jax.ShapeDtypeStruct((3, rows, 2 * n), f32),
+            jax.ShapeDtypeStruct((3, rows + 16, 2 * n), bf16),
+            jax.ShapeDtypeStruct((3, rows // 2, n), f32),
+            jax.ShapeDtypeStruct((3, rows // 2 + 16, n), bf16),
+            jax.ShapeDtypeStruct((8, 128), f32),
+        ],
+        in_specs=[SCALARS] + [ANY] * 8,
+        scratch_shapes=[
+            pltpu.VMEM((2, 3, 2, rows, k), bf16),
+            pltpu.VMEM(basis_act.shape, bf16),
+            pltpu.VMEM(basis_grad.shape, bf16),
+            pltpu.VMEM((2, rows // 2, n), f32),
+            pltpu.SemaphoreType.DMA((3, 2)),
+            pltpu.SemaphoreType.DMA((2,)),
+        ],
+        compiler_params=PARAMS,
+        cost_estimate=LONG,
+    )(where, *pieces, basis_act, basis_grad)
+
+
+def rotate_last_kernel(where, *refs):
+    pieces, (act_ref, grad_ref), done = refs[:2], refs[2:4], refs[4:8]
+    outs, act_kept, act_sent = refs[8:12], refs[12], refs[13]
+    panel, act, grad, held, grad_full, grad_coded, kept, sent, in_sems, out_sems = refs[14:]
+    n = act.shape[1]
+    copies = [
+        pltpu.make_async_copy(act_ref, act, in_sems.at[0]),
+        pltpu.make_async_copy(grad_ref, grad, in_sems.at[1]),
+    ]
+    for j in range(2):
+        copies.append(
+            pltpu.make_async_copy(pieces[j], panel.at[where[C] ^ j], in_sems.at[2 + j])
+        )
+    for copy in copies:
+        copy.start()
+
+    def route(i, step, sources, act_on):
+        due = (x_slot(where, step) - where[Y]) & 3
+        for j, y_step in enumerate(STEPS):
+            @pl.when(due == (y_step & 3))
+            def _():
+                source = sources[0] if j == 0 else sources[1]
+                for copy in (
+                    pltpu.make_async_copy(source, outs[j], out_sems.at[i, 0]),
+                    pltpu.make_async_copy(sources[2], act_kept.at[j], out_sems.at[i, 1]),
+                    pltpu.make_async_copy(sources[3], act_sent.at[j], out_sems.at[i, 2]),
+                ):
+                    act_on(copy)
+
+    parts = [(i, STEPS[i], [ref.at[i] for ref in done]) for i in range(3)]
+    for part in parts:
+        route(*part, lambda copy: copy.start())
+    for copy in copies:
+        copy.wait()
+    rows = kept.shape[0]
+    total = product(lambda h, c: panel[c, h], grad, n, 2 * n)
+    grad_full[...] = total
+    encode(total, grad_coded)
+    total = product(lambda h, c: panel[c, h], act, 0, n)
+    held[0] = total[:rows]
+    held[1] = total[rows:]
+    kept[...] = held[where[ZL]]
+    encode(held[1 - where[ZL]], sent)
+    parts.append((3, STEPS[3], [grad_full, grad_coded, kept, sent]))
+    route(*parts[3], lambda copy: copy.start())
+    for part in parts:
+        route(*part, lambda copy: copy.wait())
+
+
+def rotate_last(where, pieces, basis_act, basis_grad, done):
+    rows, k = pieces[0].shape[1:]
+    n = k // 3
+    f32, bf16 = jnp.float32, jnp.bfloat16
+    return pl.pallas_call(
+        rotate_last_kernel,
         out_shape=[jax.ShapeDtypeStruct((rows, 2 * n), f32)]
         + [jax.ShapeDtypeStruct((rows + 16, 2 * n), bf16)] * 3
         + [
             jax.ShapeDtypeStruct((4, rows // 2, n), f32),
-            jax.ShapeDtypeStruct((2 * rows + 16, n), bf16),
-        ],
-        in_specs=[SCALARS] + [ANY] * (10 + len(after)),
+            jax.ShapeDtypeStruct((4, rows // 2 + 16, n), bf16),
+        ],
+        in_specs=[SCALARS] + [ANY] * 8,
+        out_specs=[ANY] * 6,
         scratch_shapes=[
-            pltpu.VMEM((2, 4, 2, rows, k), bf16),
+            pltpu.VMEM((2, 2, rows, k), bf16),
             pltpu.VMEM(basis_act.shape, bf16),
             pltpu.VMEM(basis_grad.shape, bf16),
-            pltpu.VMEM((2, 4, rows // 2, n), f32),
-            pltpu.SemaphoreType.DMA((4, 2)),
-            pltpu.SemaphoreType.DMA((2,)),
-        ],
-        compiler_params=PARAMS,
-        cost_estimate=CHEAP,
-    )(where, *pieces, basis_act, basis_grad, *after)
+            pltpu.VMEM((2, rows // 2, n), f32),
+            pltpu.VMEM((rows, 2 * n), f32),
+            pltpu.VMEM((rows + 16, 2 * n), bf16),
+            pltpu.VMEM((rows // 2, n), f32),
+            pltpu.VMEM((rows // 2 + 16, n), bf16),
+            pltpu.SemaphoreType.DMA((4,)),
+            pltpu.SemaphoreType.DMA((4, 3)),
+        ],
+        compiler_params=PARAMS,
+        cost_estimate=CHEAP,
+    )(where, *pieces, basis_act, basis_grad, *done)
 
 
 def covariance_kernel(where, *refs):
@@ -301,7 +387,7 @@
             pltpu.SemaphoreType.DMA((4, 2)),
         ],
         compiler_params=PARAMS,
-        cost_estimate=CHEAP,
+        cost_estimate=LONG,
     )(where, *pieces, *mine)
 
 
@@ -404,10 +490,9 @@
 
 def split_kernel(kept, arrived, *outs):
     rows, n = kept.shape[1:]
-    total = kept[...] + decode(arrived).reshape(4, rows, n)
-    outs[0][...] = total[0]
+    outs[0][...] = kept[0] + decode(arrived.at[0])
     for i in range(1, 4):
-        encode(total[i], outs[i])
+        encode(kept[i] + decode(arrived.at[i]), outs[i])
 
 
 def act_square_kernel(own, *refs):
@@ -483,6 +568,24 @@
 
 def in_order(first, *later):
     return lax.optimization_barrier((first, *later))[1:]
+
+
+def pass_kernel(value, after, out, sem):
+    copy = pltpu.make_async_copy(value, out, sem)
+    copy.start()
+    copy.wait()
+
+
+def pass_on(value, after):
+    return pl.pallas_call(
+        pass_kernel,
+        out_shape=jax.ShapeDtypeStruct(value.shape, value.dtype),
+        in_specs=[ANY] * 2,
+        out_specs=ANY,
+        scratch_shapes=[pltpu.SemaphoreType.DMA],
+        compiler_params=PARAMS,
+        cost_estimate=CHEAP,
+    )(value, after)
 
 
 def body(tokens, out_grads, basis_act, basis_grad):
@@ -495,16 +598,23 @@
     stack = stack_up(where, own)
     stack, near = lax.optimization_barrier((stack, near))
     stacks = (stack, shifted(stack, ZL, 1))
-    panel = gather_far(near, where, stacks[1])
-    *parts, act_kept, act_sent = rotate(where, panel, basis_act, basis_grad, stacks)
+    left, right = shifted(near, X, 1), shifted(near, X, -1)
+    own = [near, left, right]
+    _, left, right = lax.optimization_barrier((stacks[1], left, right))
+    far = relay(where, left, right)
+    other = [shifted(piece, C, 1) for piece in own]
+    *some, token = rotate_some(where, own + other, basis_act, basis_grad)
+    last = [far, shifted(pass_on(far, token), C, 1)]
+    panel = own + last[:1] + other + last[1:]
+    *parts, act_kept, act_sent = rotate_last(where, last, basis_act, basis_grad, some)
     cov_act, cov_grad, done = covariance(where, panel, stacks)
     split, sq_act = act_squares(act_kept, act_sent)
-    sq_grad = grad_squares(*sum_over_y(parts, where, (done, split)))
+    sq_grad = grad_squares(*sum_over_y(parts, where, (split,)))
     block = lax.ppermute(sq_act, AXES, permutation(to_group))
     pair = pair_up(sq_grad, where, 0)
     pair, block = lax.optimization_barrier((pair, block))
     squares_own = direct(pair, Y)
-    squares = gather_far(gather_near(block, where, True, squares_own[1:3]))
+    squares = gather_far(gather_near(block, where, True, squares_own[1:3] + [done]))
     correction = correct(where, squares, squares_own)
     return (cov_act, cov_grad, correction)
 

time: 167 us -> 165 us (0.988)
  waiting for transfers between devices: 46.8 us -> 39.9 us
  Pallas kernels: 25.8 us -> 30.5 us
  local copies, waits for them, and re-layouts: 6.12 us -> 1.84 us
  starting transfers between devices: 86.9 us -> 89.8 us
    unnamed x22 -> x12, local copies, waits for them, and re-layouts: 6.04 us -> 1.75 us
    pallas_call x1 -> x3, Pallas kernels: 6.91 us -> 11.1 us  [the longest x1 7.11 us: rotate_some(): pl.pallas_call(rotate_some_kernel, out_shape=[jax.ShapeDtypeStruct((3, ro...]
    ppermute x1, waiting for transfers between devices: 7.83 us -> 4.24 us  [folded(): return lax.ppermute(value, AXES, permutation(target))]
    ppermute x35, waiting for transfers between devices: 38.9 us -> 35.6 us  [shifted(): return lax.ppermute(value, AXES, permutation(target))]
    ppermute x35, starting transfers between devices: 85.6 us -> 88.1 us  [shifted(): return lax.ppermute(value, AXES, permutation(target))]
  transfers between devices with their start and end apart: 38 -> 38, of which waited for: 10 -> 12; matrix products, arithmetic and copies ran while one was open for 0% -> 0% of each run, Pallas kernels for 7% -> 11%
where the time goes in v3:
time: 165 us; the launch traced here: 163 us
  starting transfers between devices  89.8 us (54%)
  waiting for transfers between devices  39.9 us (24%)
  Pallas kernels  30.5 us (18%)
  local copies, waits for them, and re-layouts  1.84 us (1%)
    ppermute x35, starting transfers between devices, shifted(): return lax.ppermute(value, AXES, permutation(target))  88.1 us
    ppermute x35, waiting for transfers between devices, shifted(): return lax.ppermute(value, AXES, permutation(target))  35.6 us
    pallas_call x1, Pallas kernels, covariance(): pl.pallas_call(covariance_kernel, out_shape=[jax.ShapeDtypeStruct((n, 4 *...  7.56 us
    pallas_call x1, Pallas kernels, rotate_some(): pl.pallas_call(rotate_some_kernel, out_shape=[jax.ShapeDtypeStruct((3, ro...  7.11 us
    ppermute x1, waiting for transfers between devices, folded(): return lax.ppermute(value, AXES, permutation(target))  4.24 us
    pallas_call x1, Pallas kernels, rotate_last(): pl.pallas_call(rotate_last_kernel, out_shape=[jax.ShapeDtypeStruct((rows,...  3.88 us
  transfers between devices with their start and end apart: 38, of which 12 were waited for; matrix products, arithmetic and copies ran while one was open for 0% of the time, Pallas kernels for 11%

profile of v3, /device:TPU:1, one launch (start us, length us, event | category | flops | bytes accessed | tf_op | source)
XLA Modules:
  0.0 163.1 jit_solution(12748891908572431156)
XLA Ops:
  3.2 13.5 %collective-permute-start.1 = (bf16[768,128]{1,0:T(8,128)(2,1)S(1)}, bf16[768,128]{1,0:T(8,128)(2,1)S(1)}, u32[]{:S(2)}, u32[]{:S(2)}) collective-permute-start(bf16[768,128]{1,0:T(8,128)(2,1)S(1)} %get-tuple-element.34.refs_0_), channel_id=1, source_target_pairs={{0,32},{1,33},{2,34},{3,35},{4,36},{5,37},{6,38},{7,39},{8,40},{9,... | collective-permute-start | bytes 589832 | tf_op jit(solution)/shard_map/ppermute | solution.py:41
  22.7 3.5 %collective-permute-start.5 = (bf16[128,768]{1,0:T(8,128)(2,1)S(1)}, bf16[128,768]{1,0:T(8,128)(2,1)S(1)}, u32[]{:S(2)}, u32[]{:S(2)}) collective-permute-start(bf16[128,768]{1,0:T(8,128)(2,1)S(1)} %collective-permute-done.refs_1_), channel_id=1, source_target_pairs={{0,6},{1,7},{2,0},{3,1},{4,2},{5,3},{6,4},{7,5},{8,14},{9,15},{10,... | collective-permute-start | bytes 589832 | tf_op jit(solution)/shard_map/ppermute | solution.py:41
  26.2 2.7 %collective-permute-start.6 = (bf16[128,768]{1,0:T(8,128)(2,1)S(1)}, bf16[128,768]{1,0:T(8,128)(2,1)S(1)}, u32[]{:S(2)}, u32[]{:S(2)}) collective-permute-start(bf16[128,768]{1,0:T(8,128)(2,1)S(1)} %collective-permute-done.refs_1_), channel_id=1, source_target_pairs={{0,4},{1,5},{2,6},{3,7},{4,0},{5,1},{6,2},{7,3},{8,12},{9,13},{10,... | collective-permute-start | bytes 589832 | tf_op jit(solution)/shard_map/ppermute | solution.py:41
  30.6 10.7 %collective-permute-done.6.refs_4_ = bf16[128,768]{1,0:T(8,128)(2,1)S(1)} collective-permute-done((bf16[128,768]{1,0:T(8,128)(2,1)S(1)}, bf16[128,768]{1,0:T(8,128)(2,1)S(1)}, u32[]{:S(2)}, u32[]{:S(2)}) %collective-permute-start.6) | collective-permute-done | bytes 196640 | tf_op jit(solution)/shard_map/ppermute | solution.py:41
  43.0 3.2 %collective-permute-start.8 = (bf16[2,256,768]{2,1,0:T(8,128)(2,1)S(1)}, bf16[2,256,768]{2,1,0:T(8,128)(2,1)S(1)}, u32[]{:S(2)}, u32[]{:S(2)}) collective-permute-start(bf16[2,256,768]{2,1,0:T(8,128)(2,1)S(1)} %shard_map.69.refs_0_), channel_id=1, source_target_pairs={{0,24},{1,25},{2,26},{3,27},{4,28},{5,29},{6,30},{7,31},{8,0},{9,1... | collective-permute-start | bytes 2359304 | tf_op jit(solution)/shard_map/ppermute | solution.py:41
  46.2 6.0 %collective-permute-start.9 = (bf16[4,768,128]{2,1,0:T(8,128)(2,1)S(1)}, bf16[4,768,128]{2,1,0:T(8,128)(2,1)}, u32[]{:S(2)}, u32[]{:S(2)}) collective-permute-start(bf16[4,768,128]{2,1,0:T(8,128)(2,1)S(1)} %shard_map.68.refs_8_), channel_id=1, source_target_pairs={{0,128},{1,129},{2,130},{3,131},{4,132},{5,133},{6,134},{7,135},{8... | collective-permute-start | bytes 2359304 | tf_op jit(solution)/shard_map/ppermute | solution.py:41
  52.3 2.6 %collective-permute-start.11 = (bf16[2,256,768]{2,1,0:T(8,128)(2,1)S(1)}, bf16[2,256,768]{2,1,0:T(8,128)(2,1)}, u32[]{:S(2)}, u32[]{:S(2)}) collective-permute-start(bf16[2,256,768]{2,1,0:T(8,128)(2,1)S(1)} %shard_map.69.refs_0_), channel_id=1, source_target_pairs={{0,1},{1,0},{2,3},{3,2},{4,5},{5,4},{6,7},{7,6},{8,9},{9,8},{10,11... | collective-permute-start | bytes 2359304 | tf_op jit(solution)/shard_map/ppermute | solution.py:41
  54.8 4.3 %collective-permute-done.7.refs_1_ = bf16[2,256,768]{2,1,0:T(8,128)(2,1)S(1)} collective-permute-done((bf16[2,256,768]{2,1,0:T(8,128)(2,1)S(1)}, bf16[2,256,768]{2,1,0:T(8,128)(2,1)S(1)}, u32[]{:S(2)}, u32[]{:S(2)}) %collective-permute-start.7) | collective-permute-done | bytes 786464 | tf_op jit(solution)/shard_map/ppermute | solution.py:41
  59.1 5.6 %collective-permute-start.12 = (bf16[2,256,768]{2,1,0:T(8,128)(2,1)S(1)}, bf16[2,256,768]{2,1,0:T(8,128)(2,1)}, u32[]{:S(2)}, u32[]{:S(2)}) collective-permute-start(bf16[2,256,768]{2,1,0:T(8,128)(2,1)S(1)} %collective-permute-done.7.refs_1_), channel_id=1, source_target_pairs={{0,1},{1,0},{2,3},{3,2},{4,5},{5,4},{6,7},{7,6},{8,9},{9,8},{10,11... | collective-permute-start | bytes 2359304 | tf_op jit(solution)/shard_map/ppermute | solution.py:41
  68.8 7.1 %shard_map.70 = (f32[3,256,512]{2,1,0:T(8,128)}, bf16[3,272,512]{2,1,0:T(8,128)(2,1)}, f32[3,128,256]{2,1,0:T(8,128)S(1)}, bf16[3,144,256]{2,1,0:T(8,128)(2,1)S(1)}, f32[8,128]{1,0:T(8,128)S(1)}) custom-call(s32[5]{0:T(128)S(1)} %stack.23.where.refs_0_, bf16[2,256,768]{2,1,0:T(8,128)(2,1)S(1)} %shard_map.69.refs_0_, ...), custom_call_target="tpu_custom_call" | custom-call | flops 5000000000 | bytes 20000000 | tf_op jit(solution)/shard_map/pallas_call | solution.py:222
  75.9 4.2 %collective-permute-done.10.value.refs_3_.refs_0_ = bf16[2,256,768]{2,1,0:T(8,128)(2,1)S(1)} collective-permute-done((bf16[2,256,768]{2,1,0:T(8,128)(2,1)S(1)}, bf16[2,256,768]{2,1,0:T(8,128)(2,1)S(1)}, u32[]{:S(2)}, u32[]{:S(2)}) %collective-permute-start.10) | collective-permute-done | bytes 786464 | tf_op jit(solution)/shard_map/ppermute | solution.py:52
  80.3 3.1 %collective-permute-start.14 = (bf16[2,256,768]{2,1,0:T(8,128)(2,1)S(1)}, bf16[2,256,768]{2,1,0:T(8,128)(2,1)S(1)}, u32[]{:S(2)}, u32[]{:S(2)}) collective-permute-start(bf16[2,256,768]{2,1,0:T(8,128)(2,1)S(1)} %shard_map.71), channel_id=1, source_target_pairs={{0,1},{1,0},{2,3},{3,2},{4,5},{5,4},{6,7},{7,6},{8,9},{9,8},{10,11... | collective-permute-start | bytes 2359304 | tf_op jit(solution)/shard_map/ppermute | solution.py:41
  85.3 3.9 %shard_map.73 = (f32[256,512]{1,0:T(8,128)S(1)}, bf16[272,512]{1,0:T(8,128)(2,1)S(1)}, bf16[272,512]{1,0:T(8,128)(2,1)S(1)}, bf16[272,512]{1,0:T(8,128)(2,1)S(1)...) custom-call(s32[5]{0:T(128)S(1)} %stack.23.where.refs_0_, ...), custom_call_target="tpu_custom_call" | custom-call | flops 1000 | bytes 1000 | tf_op jit(solution)/shard_map/pallas_call | solution.py:298
  90.7 2.7 %collective-permute-start.16 = (bf16[272,512]{1,0:T(8,128)(2,1)S(1)}, bf16[272,512]{1,0:T(8,128)(2,1)S(1)}, u32[]{:S(2)}, u32[]{:S(2)}) collective-permute-start(bf16[272,512]{1,0:T(8,128)(2,1)S(1)} %get-tuple-element.48), channel_id=1, source_target_pairs={{0,96},{1,97},{2,98},{3,99},{4,100},{5,101},{6,102},{7,103},{8,104... | collective-permute-start | bytes 835592 | tf_op jit(solution)/shard_map/ppermute | solution.py:41
  93.4 4.1 %collective-permute-done.18.arrived = bf16[4,144,256]{2,1,0:T(8,128)(2,1)S(1)} collective-permute-done((bf16[4,144,256]{2,1,0:T(8,128)(2,1)S(1)}, bf16[4,144,256]{2,1,0:T(8,128)(2,1)S(1)}, u32[]{:S(2)}, u32[]{:S(2)}) %collective-permute-start.18) | collective-permute-done | bytes 294944 | tf_op jit(solution)/shard_map/ppermute | solution.py:41
  98.2 7.3 %collective-permute-done.15.refs_0_ = bf16[272,512]{1,0:T(8,128)(2,1)S(1)} collective-permute-done((bf16[272,512]{1,0:T(8,128)(2,1)S(1)}, bf16[272,512]{1,0:T(8,128)(2,1)S(1)}, u32[]{:S(2)}, u32[]{:S(2)}) %collective-permute-start.15) | collective-permute-done | bytes 278560 | tf_op jit(solution)/shard_map/ppermute | solution.py:41
  112.7 3.5 %collective-permute-done.23.refs_2_ = bf16[144,256]{1,0:T(8,128)(2,1)S(1)} collective-permute-done((bf16[144,256]{1,0:T(8,128)(2,1)S(1)}, bf16[144,256]{1,0:T(8,128)(2,1)S(1)}, u32[]{:S(2)}, u32[]{:S(2)}) %collective-permute-start.23) | collective-permute-done | bytes 73760 | tf_op jit(solution)/shard_map/ppermute | solution.py:41
  118.2 3.5 %collective-permute-start.28 = (bf16[256,512]{1,0:T(8,128)(2,1)S(1)}, bf16[256,512]{1,0:T(8,128)(2,1)S(1)}, u32[]{:S(2)}, u32[]{:S(2)}) collective-permute-start(bf16[256,512]{1,0:T(8,128)(2,1)S(1)} %shard_map.77.refs_8_), channel_id=1, source_target_pairs={{0,32},{1,33},{2,34},{3,35},{4,36},{5,37},{6,38},{7,39},{8,40},{9,... | collective-permute-start | bytes 786440 | tf_op jit(solution)/shard_map/ppermute | solution.py:41
  121.7 3.2 %collective-permute-start.29 = (bf16[256,512]{1,0:T(8,128)(2,1)S(1)}, bf16[256,512]{1,0:T(8,128)(2,1)S(1)}, u32[]{:S(2)}, u32[]{:S(2)}) collective-permute-start(bf16[256,512]{1,0:T(8,128)(2,1)S(1)} %shard_map.77.refs_8_), channel_id=1, source_target_pairs={{0,96},{1,97},{2,98},{3,99},{4,100},{5,101},{6,102},{7,103},{8,104... | collective-permute-start | bytes 786440 | tf_op jit(solution)/shard_map/ppermute | solution.py:41
  130.3 7.6 %shard_map.72 = (f32[256,1024]{1,0:T(8,128)}, f32[512,2048]{1,0:T(8,128)}, f32[8,128]{1,0:T(8,128)S(1)}) custom-call(s32[5]{0:T(128)S(1)} %stack.23.where.refs_0_, bf16[2,256,768]{2,1,0:T(8,128)(2,1)S(1)} %shard_map.69.refs_0_, bf16[2,256,768]{2,1,0:T(8,128)(2,1)S(1)} %collective-permute-done.7.refs_1_, ...), custom_call_target="tpu_custom_call" | custom-call | flops 5000000000 | bytes 20000000 | tf_op jit(solution)/shard_map/pallas_call | solution.py:371
  139.6 5.0 %collective-permute-start.31 = (bf16[2,256,256]{2,1,0:T(8,128)(2,1)S(1)}, bf16[2,256,256]{2,1,0:T(8,128)(2,1)S(1)}, u32[]{:S(2)}, u32[]{:S(2)}) collective-permute-start(bf16[2,256,256]{2,1,0:T(8,128)(2,1)S(1)} %shard_map.79.refs_0_), channel_id=1, source_target_pairs={{0,24},{1,25},{2,26},{3,27},{4,28},{5,29},{6,30},{7,31},{8,0},{9,1... | collective-permute-start | bytes 786440 | tf_op jit(solution)/shard_map/ppermute | solution.py:41
  146.6 6.5 %collective-permute-start.33 = (bf16[2,256,256]{2,1,0:T(8,128)(2,1)S(1)}, bf16[2,256,256]{2,1,0:T(8,128)(2,1)S(1)}, u32[]{:S(2)}, u32[]{:S(2)}) collective-permute-start(bf16[2,256,256]{2,1,0:T(8,128)(2,1)S(1)} %shard_map.79.refs_0_), channel_id=1, source_target_pairs={{0,1},{1,0},{2,3},{3,2},{4,5},{5,4},{6,7},{7,6},{8,9},{9,8},{10,11... | collective-permute-start | bytes 786440 | tf_op jit(solution)/shard_map/ppermute | solution.py:41
  153.0 2.7 %collective-permute-start.34 = (bf16[2,256,256]{2,1,0:T(8,128)(2,1)S(1)}, bf16[2,256,256]{2,1,0:T(8,128)(2,1)S(1)}, u32[]{:S(2)}, u32[]{:S(2)}) collective-permute-start(bf16[2,256,256]{2,1,0:T(8,128)(2,1)S(1)} %collective-permute-done.30.refs_1_), channel_id=1, source_target_pairs={{0,1},{1,0},{2,3},{3,2},{4,5},{5,4},{6,7},{7,6},{8,9},{9,8},{10,11... | collective-permute-start | bytes 786440 | tf_op jit(solution)/shard_map/ppermute | solution.py:41
  159.9 3.0 %shard_map.80 = f32[1024,512]{1,0:T(8,128)} custom-call(s32[5]{0:T(128)S(1)} %stack.23.where.refs_0_, bf16[2,256,256]{2,1,0:T(8,128)(2,1)S(1)} %shard_map.79.refs_0_, bf16[2,256,256]{2,1,0:T(8,128)(2,1)S(1)} %collective-permute-done.30.refs_1_, bf16[2,256,256]{2,1,0:T(8,128)(2,1)S(1)} %collective-permute-done.31.refs_2_, ...), custom_call_target="tpu_custom_call" | custom-call | flops 1000 | bytes 1000 | tf_op jit(solution)/shard_map/pallas_call | solution.py:430
  (80 shorter events, 42.8 us)
Async XLA Ops:
  3.2 23.0 %collective-permute-start.1 = (bf16[768,128]{1,0:T(8,128)(2,1)S(1)}, bf16[768,128]{1,0:T(8,128)(2,1)S(1)}, u32[]{:S(2)}, u32[]{:S(2)}) collective-permute-start(bf16[768,128]{1,0:T(8,128)(2,1)S(1)} %get-tuple-element.34.refs_0_), channel_id=1, source_target_pairs={{0,32},{1,33},{2,34},{3,35},{4,36},{5,37},{6,38},{7,39},{8,40},{9,... | collective-permute-start | bytes 589832 | tf_op jit(solution)/shard_map/ppermute | solution.py:41
  16.7 12.2 %collective-permute-start.2 = (bf16[768,128]{1,0:T(8,128)(2,1)S(1)}, bf16[768,128]{1,0:T(8,128)(2,1)S(1)}, u32[]{:S(2)}, u32[]{:S(2)}) collective-permute-start(bf16[768,128]{1,0:T(8,128)(2,1)S(1)} %get-tuple-element.34.refs_0_), channel_id=1, source_target_pairs={{0,96},{1,97},{2,98},{3,99},{4,100},{5,101},{6,102},{7,103},{8,104... | collective-permute-start | bytes 589832 | tf_op jit(solution)/shard_map/ppermute | solution.py:41
  19.3 9.7 %collective-permute-start.3 = (bf16[768,128]{1,0:T(8,128)(2,1)S(1)}, bf16[768,128]{1,0:T(8,128)(2,1)S(1)}, u32[]{:S(2)}, u32[]{:S(2)}) collective-permute-start(bf16[768,128]{1,0:T(8,128)(2,1)S(1)} %get-tuple-element.34.refs_0_), channel_id=1, source_target_pairs={{0,64},{1,65},{2,66},{3,67},{4,68},{5,69},{6,70},{7,71},{8,72},{9,... | collective-permute-start | bytes 589832 | tf_op jit(solution)/shard_map/ppermute | solution.py:41
  20.5 10.1 %collective-permute-start.4 = (bf16[128,768]{1,0:T(8,128)(2,1)S(1)}, bf16[128,768]{1,0:T(8,128)(2,1)S(1)}, u32[]{:S(2)}, u32[]{:S(2)}) collective-permute-start(bf16[128,768]{1,0:T(8,128)(2,1)S(1)} %collective-permute-done.refs_1_), channel_id=1, source_target_pairs={{0,2},{1,3},{2,4},{3,5},{4,6},{5,7},{6,0},{7,1},{8,10},{9,11},{10,... | collective-permute-start | bytes 589832 | tf_op jit(solution)/shard_map/ppermute | solution.py:41
  26.2 15.1 %collective-permute-start.6 = (bf16[128,768]{1,0:T(8,128)(2,1)S(1)}, bf16[128,768]{1,0:T(8,128)(2,1)S(1)}, u32[]{:S(2)}, u32[]{:S(2)}) collective-permute-start(bf16[128,768]{1,0:T(8,128)(2,1)S(1)} %collective-permute-done.refs_1_), channel_id=1, source_target_pairs={{0,4},{1,5},{2,6},{3,7},{4,0},{5,1},{6,2},{7,3},{8,12},{9,13},{10,... | collective-permute-start | bytes 589832 | tf_op jit(solution)/shard_map/ppermute | solution.py:41
  42.9 16.2 %collective-permute-start.7 = (bf16[2,256,768]{2,1,0:T(8,128)(2,1)S(1)}, bf16[2,256,768]{2,1,0:T(8,128)(2,1)S(1)}, u32[]{:S(2)}, u32[]{:S(2)}) collective-permute-start(bf16[2,256,768]{2,1,0:T(8,128)(2,1)S(1)} %shard_map.69.refs_0_), channel_id=1, source_target_pairs={{0,8},{1,9},{2,10},{3,11},{4,12},{5,13},{6,14},{7,15},{8,16},{9,17... | collective-permute-start | bytes 2359304 | tf_op jit(solution)/shard_map/ppermute | solution.py:41
  43.0 21.6 %collective-permute-start.8 = (bf16[2,256,768]{2,1,0:T(8,128)(2,1)S(1)}, bf16[2,256,768]{2,1,0:T(8,128)(2,1)S(1)}, u32[]{:S(2)}, u32[]{:S(2)}) collective-permute-start(bf16[2,256,768]{2,1,0:T(8,128)(2,1)S(1)} %shard_map.69.refs_0_), channel_id=1, source_target_pairs={{0,24},{1,25},{2,26},{3,27},{4,28},{5,29},{6,30},{7,31},{8,0},{9,1... | collective-permute-start | bytes 2359304 | tf_op jit(solution)/shard_map/ppermute | solution.py:41
  46.2 21.7 %collective-permute-start.9 = (bf16[4,768,128]{2,1,0:T(8,128)(2,1)S(1)}, bf16[4,768,128]{2,1,0:T(8,128)(2,1)}, u32[]{:S(2)}, u32[]{:S(2)}) collective-permute-start(bf16[4,768,128]{2,1,0:T(8,128)(2,1)S(1)} %shard_map.68.refs_8_), channel_id=1, source_target_pairs={{0,128},{1,129},{2,130},{3,131},{4,132},{5,133},{6,134},{7,135},{8... | collective-permute-start | bytes 2359304 | tf_op jit(solution)/shard_map/ppermute | solution.py:41
  52.3 16.1 %collective-permute-start.11 = (bf16[2,256,768]{2,1,0:T(8,128)(2,1)S(1)}, bf16[2,256,768]{2,1,0:T(8,128)(2,1)}, u32[]{:S(2)}, u32[]{:S(2)}) collective-permute-start(bf16[2,256,768]{2,1,0:T(8,128)(2,1)S(1)} %shard_map.69.refs_0_), channel_id=1, source_target_pairs={{0,1},{1,0},{2,3},{3,2},{4,5},{5,4},{6,7},{7,6},{8,9},{9,8},{10,11... | collective-permute-start | bytes 2359304 | tf_op jit(solution)/shard_map/ppermute | solution.py:41
  59.1 9.3 %collective-permute-start.12 = (bf16[2,256,768]{2,1,0:T(8,128)(2,1)S(1)}, bf16[2,256,768]{2,1,0:T(8,128)(2,1)}, u32[]{:S(2)}, u32[]{:S(2)}) collective-permute-start(bf16[2,256,768]{2,1,0:T(8,128)(2,1)S(1)} %collective-permute-done.7.refs_1_), channel_id=1, source_target_pairs={{0,1},{1,0},{2,3},{3,2},{4,5},{5,4},{6,7},{7,6},{8,9},{9,8},{10,11... | collective-permute-start | bytes 2359304 | tf_op jit(solution)/shard_map/ppermute | solution.py:41
  68.1 12.1 %collective-permute-start.10 = (bf16[2,256,768]{2,1,0:T(8,128)(2,1)S(1)}, bf16[2,256,768]{2,1,0:T(8,128)(2,1)S(1)}, u32[]{:S(2)}, u32[]{:S(2)}) collective-permute-start(bf16[2,256,768]{2,1,0:T(8,128)(2,1)S(1)} %broadcast_select_fusion), channel_id=1, source_target_pairs={{0,24},{1,9},{2,26},{3,11},{4,28},{5,13},{6,30},{7,15},{8,0},{9,17... | collective-permute-start | bytes 2359304 | tf_op jit(solution)/shard_map/ppermute | solution.py:52
  90.7 14.7 %collective-permute-start.15 = (bf16[272,512]{1,0:T(8,128)(2,1)S(1)}, bf16[272,512]{1,0:T(8,128)(2,1)S(1)}, u32[]{:S(2)}, u32[]{:S(2)}) collective-permute-start(bf16[272,512]{1,0:T(8,128)(2,1)S(1)} %get-tuple-element.47), channel_id=1, source_target_pairs={{0,32},{1,33},{2,34},{3,35},{4,36},{5,37},{6,38},{7,39},{8,40},{9,... | collective-permute-start | bytes 835592 | tf_op jit(solution)/shard_map/ppermute | solution.py:41
  90.7 14.7 %collective-permute-start.16 = (bf16[272,512]{1,0:T(8,128)(2,1)S(1)}, bf16[272,512]{1,0:T(8,128)(2,1)S(1)}, u32[]{:S(2)}, u32[]{:S(2)}) collective-permute-start(bf16[272,512]{1,0:T(8,128)(2,1)S(1)} %get-tuple-element.48), channel_id=1, source_target_pairs={{0,96},{1,97},{2,98},{3,99},{4,100},{5,101},{6,102},{7,103},{8,104... | collective-permute-start | bytes 835592 | tf_op jit(solution)/shard_map/ppermute | solution.py:41
  93.4 12.1 %collective-permute-start.17 = (bf16[272,512]{1,0:T(8,128)(2,1)S(1)}, bf16[272,512]{1,0:T(8,128)(2,1)S(1)}, u32[]{:S(2)}, u32[]{:S(2)}) collective-permute-start(bf16[272,512]{1,0:T(8,128)(2,1)S(1)} %get-tuple-element.49), channel_id=1, source_target_pairs={{0,64},{1,65},{2,66},{3,67},{4,68},{5,69},{6,70},{7,71},{8,72},{9,... | collective-permute-start | bytes 835592 | tf_op jit(solution)/shard_map/ppermute | solution.py:41
  118.2 19.7 %collective-permute-start.28 = (bf16[256,512]{1,0:T(8,128)(2,1)S(1)}, bf16[256,512]{1,0:T(8,128)(2,1)S(1)}, u32[]{:S(2)}, u32[]{:S(2)}) collective-permute-start(bf16[256,512]{1,0:T(8,128)(2,1)S(1)} %shard_map.77.refs_8_), channel_id=1, source_target_pairs={{0,32},{1,33},{2,34},{3,35},{4,36},{5,37},{6,38},{7,39},{8,40},{9,... | collective-permute-start | bytes 786440 | tf_op jit(solution)/shard_map/ppermute | solution.py:41
  121.7 16.2 %collective-permute-start.29 = (bf16[256,512]{1,0:T(8,128)(2,1)S(1)}, bf16[256,512]{1,0:T(8,128)(2,1)S(1)}, u32[]{:S(2)}, u32[]{:S(2)}) collective-permute-start(bf16[256,512]{1,0:T(8,128)(2,1)S(1)} %shard_map.77.refs_8_), channel_id=1, source_target_pairs={{0,96},{1,97},{2,98},{3,99},{4,100},{5,101},{6,102},{7,103},{8,104... | collective-permute-start | bytes 786440 | tf_op jit(solution)/shard_map/ppermute | solution.py:41
  124.9 12.9 %collective-permute-start.25 = (bf16[256,128]{1,0:T(8,128)(2,1)S(1)}, bf16[256,128]{1,0:T(8,128)(2,1)S(1)}, u32[]{:S(2)}, u32[]{:S(2)}) collective-permute-start(bf16[256,128]{1,0:T(8,128)(2,1)S(1)} %collective-permute-done.24.refs_1_), channel_id=1, source_target_pairs={{0,2},{1,3},{2,4},{3,5},{4,6},{5,7},{6,0},{7,1},{8,10},{9,11},{10,... | collective-permute-start | bytes 196616 | tf_op jit(solution)/shard_map/ppermute | solution.py:41
  127.0 10.9 %collective-permute-start.26 = (bf16[256,128]{1,0:T(8,128)(2,1)S(1)}, bf16[256,128]{1,0:T(8,128)(2,1)S(1)}, u32[]{:S(2)}, u32[]{:S(2)}) collective-permute-start(bf16[256,128]{1,0:T(8,128)(2,1)S(1)} %collective-permute-done.24.refs_1_), channel_id=1, source_target_pairs={{0,6},{1,7},{2,0},{3,1},{4,2},{5,3},{6,4},{7,5},{8,14},{9,15},{10,... | collective-permute-start | bytes 196616 | tf_op jit(solution)/shard_map/ppermute | solution.py:41
  128.5 9.4 %collective-permute-start.27 = (bf16[256,128]{1,0:T(8,128)(2,1)S(1)}, bf16[256,128]{1,0:T(8,128)(2,1)S(1)}, u32[]{:S(2)}, u32[]{:S(2)}) collective-permute-start(bf16[256,128]{1,0:T(8,128)(2,1)S(1)} %collective-permute-done.24.refs_1_), channel_id=1, source_target_pairs={{0,4},{1,5},{2,6},{3,7},{4,0},{5,1},{6,2},{7,3},{8,12},{9,13},{10,... | collective-permute-start | bytes 196616 | tf_op jit(solution)/shard_map/ppermute | solution.py:41
  138.6 14.5 %collective-permute-start.30 = (bf16[2,256,256]{2,1,0:T(8,128)(2,1)S(1)}, bf16[2,256,256]{2,1,0:T(8,128)(2,1)S(1)}, u32[]{:S(2)}, u32[]{:S(2)}) collective-permute-start(bf16[2,256,256]{2,1,0:T(8,128)(2,1)S(1)} %shard_map.79.refs_0_), channel_id=1, source_target_pairs={{0,8},{1,9},{2,10},{3,11},{4,12},{5,13},{6,14},{7,15},{8,16},{9,17... | collective-permute-start | bytes 786440 | tf_op jit(solution)/shard_map/ppermute | solution.py:41
  139.6 16.1 %collective-permute-start.31 = (bf16[2,256,256]{2,1,0:T(8,128)(2,1)S(1)}, bf16[2,256,256]{2,1,0:T(8,128)(2,1)S(1)}, u32[]{:S(2)}, u32[]{:S(2)}) collective-permute-start(bf16[2,256,256]{2,1,0:T(8,128)(2,1)S(1)} %shard_map.79.refs_0_), channel_id=1, source_target_pairs={{0,24},{1,25},{2,26},{3,27},{4,28},{5,29},{6,30},{7,31},{8,0},{9,1... | collective-permute-start | bytes 786440 | tf_op jit(solution)/shard_map/ppermute | solution.py:41
  144.6 12.4 %collective-permute-start.32 = (bf16[2,256,256]{2,1,0:T(8,128)(2,1)S(1)}, bf16[2,256,256]{2,1,0:T(8,128)(2,1)S(1)}, u32[]{:S(2)}, u32[]{:S(2)}) collective-permute-start(bf16[2,256,256]{2,1,0:T(8,128)(2,1)S(1)} %shard_map.79.refs_0_), channel_id=1, source_target_pairs={{0,16},{1,17},{2,18},{3,19},{4,20},{5,21},{6,22},{7,23},{8,24},{9,... | collective-permute-start | bytes 786440 | tf_op jit(solution)/shard_map/ppermute | solution.py:41
  145.9 12.8 %collective-permute-start.37 = (bf16[256,512]{1,0:T(8,128)(2,1)S(1)}, bf16[256,512]{1,0:T(8,128)(2,1)S(1)}, u32[]{:S(2)}, u32[]{:S(2)}) collective-permute-start(bf16[256,512]{1,0:T(8,128)(2,1)S(1)} %shard_map.77.refs_8_), channel_id=1, source_target_pairs={{0,64},{1,65},{2,66},{3,67},{4,68},{5,69},{6,70},{7,71},{8,72},{9,... | collective-permute-start | bytes 786440 | tf_op jit(solution)/shard_map/ppermute | solution.py:41
  146.6 12.2 %collective-permute-start.33 = (bf16[2,256,256]{2,1,0:T(8,128)(2,1)S(1)}, bf16[2,256,256]{2,1,0:T(8,128)(2,1)S(1)}, u32[]{:S(2)}, u32[]{:S(2)}) collective-permute-start(bf16[2,256,256]{2,1,0:T(8,128)(2,1)S(1)} %shard_map.79.refs_0_), channel_id=1, source_target_pairs={{0,1},{1,0},{2,3},{3,2},{4,5},{5,4},{6,7},{7,6},{8,9},{9,8},{10,11... | collective-permute-start | bytes 786440 | tf_op jit(solution)/shard_map/ppermute | solution.py:41
  (20 other events, 116.4 us)

commit v4 on v3

--- a/solution.py
+++ b/solution.py
@@ -215,7 +215,7 @@
         encode(held[1 - where[ZL]], act_sent.at[i])
 
 
-def rotate_some(where, pieces, basis_act, basis_grad):
+def rotate_some(where, pieces, basis_act, basis_grad, after):
     rows, k = pieces[0].shape[1:]
     n = k // 3
     f32, bf16 = jnp.float32, jnp.bfloat16
@@ -228,7 +228,7 @@
             jax.ShapeDtypeStruct((3, rows // 2 + 16, n), bf16),
             jax.ShapeDtypeStruct((8, 128), f32),
         ],
-        in_specs=[SCALARS] + [ANY] * 8,
+        in_specs=[SCALARS] + [ANY] * 9,
         scratch_shapes=[
             pltpu.VMEM((2, 3, 2, rows, k), bf16),
             pltpu.VMEM(basis_act.shape, bf16),
@@ -239,7 +239,7 @@
         ],
         compiler_params=PARAMS,
         cost_estimate=LONG,
-    )(where, *pieces, basis_act, basis_grad)
+    )(where, *pieces, basis_act, basis_grad, after)
 
 
 def rotate_last_kernel(where, *refs):
@@ -600,10 +600,9 @@
     stacks = (stack, shifted(stack, ZL, 1))
     left, right = shifted(near, X, 1), shifted(near, X, -1)
     own = [near, left, right]
-    _, left, right = lax.optimization_barrier((stacks[1], left, right))
     far = relay(where, left, right)
     other = [shifted(piece, C, 1) for piece in own]
-    *some, token = rotate_some(where, own + other, basis_act, basis_grad)
+    *some, token = rotate_some(where, own + other, basis_act, basis_grad, stacks[1])
     last = [far, shifted(pass_on(far, token), C, 1)]
     panel = own + last[:1] + other + last[1:]
     *parts, act_kept, act_sent = rotate_last(where, last, basis_act, basis_grad, some)

time: 165 us -> 163 us (0.988); the launches traced: 163 us -> 163 us
  waiting for transfers between devices: 39.9 us -> 37.5 us
  starting transfers between devices: 89.8 us -> 91.9 us
    ppermute x1, waiting for transfers between devices: 4.24 us -> 0.01 us  [folded(): return lax.ppermute(value, AXES, permutation(target))]
    ppermute x35, waiting for transfers between devices: 35.6 us -> 37.5 us  [shifted(): return lax.ppermute(value, AXES, permutation(target))]
  transfers between devices with their start and end apart: 38 -> 38, of which waited for: 12 -> 9; matrix products, arithmetic and copies ran while one was open for 0% -> 0% of each run, Pallas kernels for 11% -> 11%
where the time goes in v4:
time: 163 us
  starting transfers between devices  91.9 us (56%)
  waiting for transfers between devices  37.5 us (23%)
  Pallas kernels  30.5 us (19%)
  local copies, waits for them, and re-layouts  1.84 us (1%)
    ppermute x35, starting transfers between devices, shifted(): return lax.ppermute(value, AXES, permutation(target))  89 us
    ppermute x35, waiting for transfers between devices, shifted(): return lax.ppermute(value, AXES, permutation(target))  37.5 us
    pallas_call x1, Pallas kernels, covariance(): pl.pallas_call(covariance_kernel, out_shape=[jax.ShapeDtypeStruct((n, 4 *...  7.56 us
    pallas_call x1, Pallas kernels, rotate_some(): pl.pallas_call(rotate_some_kernel, out_shape=[jax.ShapeDtypeStruct((3, ro...  7.11 us
    pallas_call x1, Pallas kernels, rotate_last(): pl.pallas_call(rotate_last_kernel, out_shape=[jax.ShapeDtypeStruct((rows,...  3.88 us
  transfers between devices with their start and end apart: 38, of which 9 were waited for; matrix products, arithmetic and copies ran while one was open for 0% of the time, Pallas kernels for 11%

profile of v4, /device:TPU:1, one launch (start us, length us, event | category | flops | bytes accessed | tf_op | source)
XLA Modules:
  0.0 162.9 jit_solution(14858854152253468310)
XLA Ops:
  3.2 13.5 %collective-permute-start.1 = (bf16[768,128]{1,0:T(8,128)(2,1)S(1)}, bf16[768,128]{1,0:T(8,128)(2,1)S(1)}, u32[]{:S(2)}, u32[]{:S(2)}) collective-permute-start(bf16[768,128]{1,0:T(8,128)(2,1)S(1)} %get-tuple-element.32.refs_0_), channel_id=1, source_target_pairs={{0,32},{1,33},{2,34},{3,35},{4,36},{5,37},{6,38},{7,39},{8,40},{9,... | collective-permute-start | bytes 589832 | tf_op jit(solution)/shard_map/ppermute | solution.py:41
  22.7 3.5 %collective-permute-start.5 = (bf16[128,768]{1,0:T(8,128)(2,1)S(1)}, bf16[128,768]{1,0:T(8,128)(2,1)S(1)}, u32[]{:S(2)}, u32[]{:S(2)}) collective-permute-start(bf16[128,768]{1,0:T(8,128)(2,1)S(1)} %collective-permute-done.refs_1_), channel_id=1, source_target_pairs={{0,6},{1,7},{2,0},{3,1},{4,2},{5,3},{6,4},{7,5},{8,14},{9,15},{10,... | collective-permute-start | bytes 589832 | tf_op jit(solution)/shard_map/ppermute | solution.py:41
  26.2 2.7 %collective-permute-start.6 = (bf16[128,768]{1,0:T(8,128)(2,1)S(1)}, bf16[128,768]{1,0:T(8,128)(2,1)S(1)}, u32[]{:S(2)}, u32[]{:S(2)}) collective-permute-start(bf16[128,768]{1,0:T(8,128)(2,1)S(1)} %collective-permute-done.refs_1_), channel_id=1, source_target_pairs={{0,4},{1,5},{2,6},{3,7},{4,0},{5,1},{6,2},{7,3},{8,12},{9,13},{10,... | collective-permute-start | bytes 589832 | tf_op jit(solution)/shard_map/ppermute | solution.py:41
  30.6 10.7 %collective-permute-done.6.refs_4_ = bf16[128,768]{1,0:T(8,128)(2,1)S(1)} collective-permute-done((bf16[128,768]{1,0:T(8,128)(2,1)S(1)}, bf16[128,768]{1,0:T(8,128)(2,1)S(1)}, u32[]{:S(2)}, u32[]{:S(2)}) %collective-permute-start.6) | collective-permute-done | bytes 196640 | tf_op jit(solution)/shard_map/ppermute | solution.py:41
  43.0 3.2 %collective-permute-start.8 = (bf16[2,256,768]{2,1,0:T(8,128)(2,1)S(1)}, bf16[2,256,768]{2,1,0:T(8,128)(2,1)S(1)}, u32[]{:S(2)}, u32[]{:S(2)}) collective-permute-start(bf16[2,256,768]{2,1,0:T(8,128)(2,1)S(1)} %shard_map.69.refs_0_), channel_id=1, source_target_pairs={{0,24},{1,25},{2,26},{3,27},{4,28},{5,29},{6,30},{7,31},{8,0},{9,1... | collective-permute-start | bytes 2359304 | tf_op jit(solution)/shard_map/ppermute | solution.py:41
  46.2 5.2 %collective-permute-start.10 = (bf16[2,256,768]{2,1,0:T(8,128)(2,1)S(1)}, bf16[2,256,768]{2,1,0:T(8,128)(2,1)}, u32[]{:S(2)}, u32[]{:S(2)}) collective-permute-start(bf16[2,256,768]{2,1,0:T(8,128)(2,1)S(1)} %shard_map.69.refs_0_), channel_id=1, source_target_pairs={{0,1},{1,0},{2,3},{3,2},{4,5},{5,4},{6,7},{7,6},{8,9},{9,8},{10,11... | collective-permute-start | bytes 2359304 | tf_op jit(solution)/shard_map/ppermute | solution.py:41
  51.5 3.1 %collective-permute-start.13 = (bf16[4,768,128]{2,1,0:T(8,128)(2,1)S(1)}, bf16[4,768,128]{2,1,0:T(8,128)(2,1)}, u32[]{:S(2)}, u32[]{:S(2)}) collective-permute-start(bf16[4,768,128]{2,1,0:T(8,128)(2,1)S(1)} %shard_map.68.refs_8_), channel_id=1, source_target_pairs={{0,128},{1,129},{2,130},{3,131},{4,132},{5,133},{6,134},{7,135},{8... | collective-permute-start | bytes 2359304 | tf_op jit(solution)/shard_map/ppermute | solution.py:41
  54.5 4.5 %collective-permute-done.7.refs_1_ = bf16[2,256,768]{2,1,0:T(8,128)(2,1)S(1)} collective-permute-done((bf16[2,256,768]{2,1,0:T(8,128)(2,1)S(1)}, bf16[2,256,768]{2,1,0:T(8,128)(2,1)S(1)}, u32[]{:S(2)}, u32[]{:S(2)}) %collective-permute-start.7) | collective-permute-done | bytes 786464 | tf_op jit(solution)/shard_map/ppermute | solution.py:41
  59.1 5.6 %collective-permute-start.11 = (bf16[2,256,768]{2,1,0:T(8,128)(2,1)S(1)}, bf16[2,256,768]{2,1,0:T(8,128)(2,1)}, u32[]{:S(2)}, u32[]{:S(2)}) collective-permute-start(bf16[2,256,768]{2,1,0:T(8,128)(2,1)S(1)} %collective-permute-done.7.refs_1_), channel_id=1, source_target_pairs={{0,1},{1,0},{2,3},{3,2},{4,5},{5,4},{6,7},{7,6},{8,9},{9,8},{10,11... | collective-permute-start | bytes 2359304 | tf_op jit(solution)/shard_map/ppermute | solution.py:41
  68.4 4.2 %collective-permute-done.13.refs_8_.refs_9_ = bf16[4,768,128]{2,1,0:T(8,128)(2,1)} collective-permute-done((bf16[4,768,128]{2,1,0:T(8,128)(2,1)S(1)}, bf16[4,768,128]{2,1,0:T(8,128)(2,1)}, u32[]{:S(2)}, u32[]{:S(2)}) %collective-permute-start.13) | collective-permute-done | bytes 786464 | tf_op jit(solution)/shard_map/ppermute | solution.py:41
  72.6 7.1 %shard_map.70 = (f32[3,256,512]{2,1,0:T(8,128)}, bf16[3,272,512]{2,1,0:T(8,128)(2,1)}, f32[3,128,256]{2,1,0:T(8,128)S(1)}, bf16[3,144,256]{2,1,0:T(8,128)(2,1)S(1)}, f32[8,128]{1,0:T(8,128)S(1)}) custom-call(s32[5]{0:T(128)S(1)} %stack.23.where.refs_0_, bf16[2,256,768]{2,1,0:T(8,128)(2,1)S(1)} %shard_map.69.refs_0_, ...), custom_call_target="tpu_custom_call" | custom-call | flops 5000000000 | bytes 20000000 | tf_op jit(solution)/shard_map/pallas_call | solution.py:222
  82.6 3.9 %shard_map.73 = (f32[256,512]{1,0:T(8,128)S(1)}, bf16[272,512]{1,0:T(8,128)(2,1)S(1)}, bf16[272,512]{1,0:T(8,128)(2,1)S(1)}, bf16[272,512]{1,0:T(8,128)(2,1)S(1)...) custom-call(s32[5]{0:T(128)S(1)} %stack.23.where.refs_0_, ...), custom_call_target="tpu_custom_call" | custom-call | flops 1000 | bytes 1000 | tf_op jit(solution)/shard_map/pallas_call | solution.py:298
  86.5 3.2 %collective-permute-start.18 = (bf16[4,144,256]{2,1,0:T(8,128)(2,1)S(1)}, bf16[4,144,256]{2,1,0:T(8,128)(2,1)S(1)}, u32[]{:S(2)}, u32[]{:S(2)}) collective-permute-start(bf16[4,144,256]{2,1,0:T(8,128)(2,1)S(1)} %get-tuple-element.47), channel_id=1, source_target_pairs={{0,128},{1,129},{2,130},{3,131},{4,132},{5,133},{6,134},{7,135},{8... | collective-permute-start | bytes 884744 | tf_op jit(solution)/shard_map/ppermute | solution.py:41
  89.7 2.7 %collective-permute-start.16 = (bf16[272,512]{1,0:T(8,128)(2,1)S(1)}, bf16[272,512]{1,0:T(8,128)(2,1)S(1)}, u32[]{:S(2)}, u32[]{:S(2)}) collective-permute-start(bf16[272,512]{1,0:T(8,128)(2,1)S(1)} %get-tuple-element.44), channel_id=1, source_target_pairs={{0,96},{1,97},{2,98},{3,99},{4,100},{5,101},{6,102},{7,103},{8,104... | collective-permute-start | bytes 835592 | tf_op jit(solution)/shard_map/ppermute | solution.py:41
  92.4 4.4 %collective-permute-done.18.arrived = bf16[4,144,256]{2,1,0:T(8,128)(2,1)S(1)} collective-permute-done((bf16[4,144,256]{2,1,0:T(8,128)(2,1)S(1)}, bf16[4,144,256]{2,1,0:T(8,128)(2,1)S(1)}, u32[]{:S(2)}, u32[]{:S(2)}) %collective-permute-start.18) | collective-permute-done | bytes 294944 | tf_op jit(solution)/shard_map/ppermute | solution.py:41
  97.5 6.9 %collective-permute-done.15.refs_0_ = bf16[272,512]{1,0:T(8,128)(2,1)S(1)} collective-permute-done((bf16[272,512]{1,0:T(8,128)(2,1)S(1)}, bf16[272,512]{1,0:T(8,128)(2,1)S(1)}, u32[]{:S(2)}, u32[]{:S(2)}) %collective-permute-start.15) | collective-permute-done | bytes 278560 | tf_op jit(solution)/shard_map/ppermute | solution.py:41
  111.8 3.6 %collective-permute-done.23.refs_2_ = bf16[144,256]{1,0:T(8,128)(2,1)S(1)} collective-permute-done((bf16[144,256]{1,0:T(8,128)(2,1)S(1)}, bf16[144,256]{1,0:T(8,128)(2,1)S(1)}, u32[]{:S(2)}, u32[]{:S(2)}) %collective-permute-start.23) | collective-permute-done | bytes 73760 | tf_op jit(solution)/shard_map/ppermute | solution.py:41
  117.5 3.6 %collective-permute-start.28 = (bf16[256,512]{1,0:T(8,128)(2,1)S(1)}, bf16[256,512]{1,0:T(8,128)(2,1)S(1)}, u32[]{:S(2)}, u32[]{:S(2)}) collective-permute-start(bf16[256,512]{1,0:T(8,128)(2,1)S(1)} %shard_map.77.refs_8_), channel_id=1, source_target_pairs={{0,32},{1,33},{2,34},{3,35},{4,36},{5,37},{6,38},{7,39},{8,40},{9,... | collective-permute-start | bytes 786440 | tf_op jit(solution)/shard_map/ppermute | solution.py:41
  121.1 4.1 %collective-permute-start.29 = (bf16[256,512]{1,0:T(8,128)(2,1)S(1)}, bf16[256,512]{1,0:T(8,128)(2,1)S(1)}, u32[]{:S(2)}, u32[]{:S(2)}) collective-permute-start(bf16[256,512]{1,0:T(8,128)(2,1)S(1)} %shard_map.77.refs_8_), channel_id=1, source_target_pairs={{0,96},{1,97},{2,98},{3,99},{4,100},{5,101},{6,102},{7,103},{8,104... | collective-permute-start | bytes 786440 | tf_op jit(solution)/shard_map/ppermute | solution.py:41
  129.5 7.6 %shard_map.72 = (f32[256,1024]{1,0:T(8,128)}, f32[512,2048]{1,0:T(8,128)}, f32[8,128]{1,0:T(8,128)S(1)}) custom-call(s32[5]{0:T(128)S(1)} %stack.23.where.refs_0_, bf16[2,256,768]{2,1,0:T(8,128)(2,1)S(1)} %shard_map.69.refs_0_, bf16[2,256,768]{2,1,0:T(8,128)(2,1)S(1)} %collective-permute-done.7.refs_1_, ...), custom_call_target="tpu_custom_call" | custom-call | flops 5000000000 | bytes 20000000 | tf_op jit(solution)/shard_map/pallas_call | solution.py:371
  139.5 4.8 %collective-permute-start.31 = (bf16[2,256,256]{2,1,0:T(8,128)(2,1)S(1)}, bf16[2,256,256]{2,1,0:T(8,128)(2,1)S(1)}, u32[]{:S(2)}, u32[]{:S(2)}) collective-permute-start(bf16[2,256,256]{2,1,0:T(8,128)(2,1)S(1)} %shard_map.79.refs_0_), channel_id=1, source_target_pairs={{0,24},{1,25},{2,26},{3,27},{4,28},{5,29},{6,30},{7,31},{8,0},{9,1... | collective-permute-start | bytes 786440 | tf_op jit(solution)/shard_map/ppermute | solution.py:41
  146.6 6.2 %collective-permute-start.33 = (bf16[2,256,256]{2,1,0:T(8,128)(2,1)S(1)}, bf16[2,256,256]{2,1,0:T(8,128)(2,1)S(1)}, u32[]{:S(2)}, u32[]{:S(2)}) collective-permute-start(bf16[2,256,256]{2,1,0:T(8,128)(2,1)S(1)} %shard_map.79.refs_0_), channel_id=1, source_target_pairs={{0,1},{1,0},{2,3},{3,2},{4,5},{5,4},{6,7},{7,6},{8,9},{9,8},{10,11... | collective-permute-start | bytes 786440 | tf_op jit(solution)/shard_map/ppermute | solution.py:41
  152.8 2.7 %collective-permute-start.34 = (bf16[2,256,256]{2,1,0:T(8,128)(2,1)S(1)}, bf16[2,256,256]{2,1,0:T(8,128)(2,1)S(1)}, u32[]{:S(2)}, u32[]{:S(2)}) collective-permute-start(bf16[2,256,256]{2,1,0:T(8,128)(2,1)S(1)} %collective-permute-done.30.refs_1_), channel_id=1, source_target_pairs={{0,1},{1,0},{2,3},{3,2},{4,5},{5,4},{6,7},{7,6},{8,9},{9,8},{10,11... | collective-permute-start | bytes 786440 | tf_op jit(solution)/shard_map/ppermute | solution.py:41
  159.7 3.0 %shard_map.80 = f32[1024,512]{1,0:T(8,128)} custom-call(s32[5]{0:T(128)S(1)} %stack.23.where.refs_0_, bf16[2,256,256]{2,1,0:T(8,128)(2,1)S(1)} %shard_map.79.refs_0_, bf16[2,256,256]{2,1,0:T(8,128)(2,1)S(1)} %collective-permute-done.30.refs_1_, bf16[2,256,256]{2,1,0:T(8,128)(2,1)S(1)} %collective-permute-done.31.refs_2_, ...), custom_call_target="tpu_custom_call" | custom-call | flops 1000 | bytes 1000 | tf_op jit(solution)/shard_map/pallas_call | solution.py:430
  (80 shorter events, 41.9 us)
Async XLA Ops:
  3.2 23.0 %collective-permute-start.1 = (bf16[768,128]{1,0:T(8,128)(2,1)S(1)}, bf16[768,128]{1,0:T(8,128)(2,1)S(1)}, u32[]{:S(2)}, u32[]{:S(2)}) collective-permute-start(bf16[768,128]{1,0:T(8,128)(2,1)S(1)} %get-tuple-element.32.refs_0_), channel_id=1, source_target_pairs={{0,32},{1,33},{2,34},{3,35},{4,36},{5,37},{6,38},{7,39},{8,40},{9,... | collective-permute-start | bytes 589832 | tf_op jit(solution)/shard_map/ppermute | solution.py:41
  16.7 12.2 %collective-permute-start.2 = (bf16[768,128]{1,0:T(8,128)(2,1)S(1)}, bf16[768,128]{1,0:T(8,128)(2,1)S(1)}, u32[]{:S(2)}, u32[]{:S(2)}) collective-permute-start(bf16[768,128]{1,0:T(8,128)(2,1)S(1)} %get-tuple-element.32.refs_0_), channel_id=1, source_target_pairs={{0,96},{1,97},{2,98},{3,99},{4,100},{5,101},{6,102},{7,103},{8,104... | collective-permute-start | bytes 589832 | tf_op jit(solution)/shard_map/ppermute | solution.py:41
  19.3 9.7 %collective-permute-start.3 = (bf16[768,128]{1,0:T(8,128)(2,1)S(1)}, bf16[768,128]{1,0:T(8,128)(2,1)S(1)}, u32[]{:S(2)}, u32[]{:S(2)}) collective-permute-start(bf16[768,128]{1,0:T(8,128)(2,1)S(1)} %get-tuple-element.32.refs_0_), channel_id=1, source_target_pairs={{0,64},{1,65},{2,66},{3,67},{4,68},{5,69},{6,70},{7,71},{8,72},{9,... | collective-permute-start | bytes 589832 | tf_op jit(solution)/shard_map/ppermute | solution.py:41
  20.5 10.1 %collective-permute-start.4 = (bf16[128,768]{1,0:T(8,128)(2,1)S(1)}, bf16[128,768]{1,0:T(8,128)(2,1)S(1)}, u32[]{:S(2)}, u32[]{:S(2)}) collective-permute-start(bf16[128,768]{1,0:T(8,128)(2,1)S(1)} %collective-permute-done.refs_1_), channel_id=1, source_target_pairs={{0,2},{1,3},{2,4},{3,5},{4,6},{5,7},{6,0},{7,1},{8,10},{9,11},{10,... | collective-permute-start | bytes 589832 | tf_op jit(solution)/shard_map/ppermute | solution.py:41
  26.2 15.1 %collective-permute-start.6 = (bf16[128,768]{1,0:T(8,128)(2,1)S(1)}, bf16[128,768]{1,0:T(8,128)(2,1)S(1)}, u32[]{:S(2)}, u32[]{:S(2)}) collective-permute-start(bf16[128,768]{1,0:T(8,128)(2,1)S(1)} %collective-permute-done.refs_1_), channel_id=1, source_target_pairs={{0,4},{1,5},{2,6},{3,7},{4,0},{5,1},{6,2},{7,3},{8,12},{9,13},{10,... | collective-permute-start | bytes 589832 | tf_op jit(solution)/shard_map/ppermute | solution.py:41
  42.9 16.2 %collective-permute-start.7 = (bf16[2,256,768]{2,1,0:T(8,128)(2,1)S(1)}, bf16[2,256,768]{2,1,0:T(8,128)(2,1)S(1)}, u32[]{:S(2)}, u32[]{:S(2)}) collective-permute-start(bf16[2,256,768]{2,1,0:T(8,128)(2,1)S(1)} %shard_map.69.refs_0_), channel_id=1, source_target_pairs={{0,8},{1,9},{2,10},{3,11},{4,12},{5,13},{6,14},{7,15},{8,16},{9,17... | collective-permute-start | bytes 2359304 | tf_op jit(solution)/shard_map/ppermute | solution.py:41
  43.0 21.6 %collective-permute-start.8 = (bf16[2,256,768]{2,1,0:T(8,128)(2,1)S(1)}, bf16[2,256,768]{2,1,0:T(8,128)(2,1)S(1)}, u32[]{:S(2)}, u32[]{:S(2)}) collective-permute-start(bf16[2,256,768]{2,1,0:T(8,128)(2,1)S(1)} %shard_map.69.refs_0_), channel_id=1, source_target_pairs={{0,24},{1,25},{2,26},{3,27},{4,28},{5,29},{6,30},{7,31},{8,0},{9,1... | collective-permute-start | bytes 2359304 | tf_op jit(solution)/shard_map/ppermute | solution.py:41
  46.2 22.2 %collective-permute-start.10 = (bf16[2,256,768]{2,1,0:T(8,128)(2,1)S(1)}, bf16[2,256,768]{2,1,0:T(8,128)(2,1)}, u32[]{:S(2)}, u32[]{:S(2)}) collective-permute-start(bf16[2,256,768]{2,1,0:T(8,128)(2,1)S(1)} %shard_map.69.refs_0_), channel_id=1, source_target_pairs={{0,1},{1,0},{2,3},{3,2},{4,5},{5,4},{6,7},{7,6},{8,9},{9,8},{10,11... | collective-permute-start | bytes 2359304 | tf_op jit(solution)/shard_map/ppermute | solution.py:41
  51.5 21.1 %collective-permute-start.13 = (bf16[4,768,128]{2,1,0:T(8,128)(2,1)S(1)}, bf16[4,768,128]{2,1,0:T(8,128)(2,1)}, u32[]{:S(2)}, u32[]{:S(2)}) collective-permute-start(bf16[4,768,128]{2,1,0:T(8,128)(2,1)S(1)} %shard_map.68.refs_8_), channel_id=1, source_target_pairs={{0,128},{1,129},{2,130},{3,131},{4,132},{5,133},{6,134},{7,135},{8... | collective-permute-start | bytes 2359304 | tf_op jit(solution)/shard_map/ppermute | solution.py:41
  59.1 13.5 %collective-permute-start.11 = (bf16[2,256,768]{2,1,0:T(8,128)(2,1)S(1)}, bf16[2,256,768]{2,1,0:T(8,128)(2,1)}, u32[]{:S(2)}, u32[]{:S(2)}) collective-permute-start(bf16[2,256,768]{2,1,0:T(8,128)(2,1)S(1)} %collective-permute-done.7.refs_1_), channel_id=1, source_target_pairs={{0,1},{1,0},{2,3},{3,2},{4,5},{5,4},{6,7},{7,6},{8,9},{9,8},{10,11... | collective-permute-start | bytes 2359304 | tf_op jit(solution)/shard_map/ppermute | solution.py:41
  66.9 12.8 %collective-permute-start.9 = (bf16[2,256,768]{2,1,0:T(8,128)(2,1)S(1)}, bf16[2,256,768]{2,1,0:T(8,128)(2,1)S(1)}, u32[]{:S(2)}, u32[]{:S(2)}) collective-permute-start(bf16[2,256,768]{2,1,0:T(8,128)(2,1)S(1)} %broadcast_select_fusion), channel_id=1, source_target_pairs={{0,24},{1,9},{2,26},{3,11},{4,28},{5,13},{6,30},{7,15},{8,0},{9,17... | collective-permute-start | bytes 2359304 | tf_op jit(solution)/shard_map/ppermute | solution.py:52
  86.5 10.3 %collective-permute-start.18 = (bf16[4,144,256]{2,1,0:T(8,128)(2,1)S(1)}, bf16[4,144,256]{2,1,0:T(8,128)(2,1)S(1)}, u32[]{:S(2)}, u32[]{:S(2)}) collective-permute-start(bf16[4,144,256]{2,1,0:T(8,128)(2,1)S(1)} %get-tuple-element.47), channel_id=1, source_target_pairs={{0,128},{1,129},{2,130},{3,131},{4,132},{5,133},{6,134},{7,135},{8... | collective-permute-start | bytes 884744 | tf_op jit(solution)/shard_map/ppermute | solution.py:41
  89.7 14.7 %collective-permute-start.15 = (bf16[272,512]{1,0:T(8,128)(2,1)S(1)}, bf16[272,512]{1,0:T(8,128)(2,1)S(1)}, u32[]{:S(2)}, u32[]{:S(2)}) collective-permute-start(bf16[272,512]{1,0:T(8,128)(2,1)S(1)} %get-tuple-element.43), channel_id=1, source_target_pairs={{0,32},{1,33},{2,34},{3,35},{4,36},{5,37},{6,38},{7,39},{8,40},{9,... | collective-permute-start | bytes 835592 | tf_op jit(solution)/shard_map/ppermute | solution.py:41
  89.7 14.7 %collective-permute-start.16 = (bf16[272,512]{1,0:T(8,128)(2,1)S(1)}, bf16[272,512]{1,0:T(8,128)(2,1)S(1)}, u32[]{:S(2)}, u32[]{:S(2)}) collective-permute-start(bf16[272,512]{1,0:T(8,128)(2,1)S(1)} %get-tuple-element.44), channel_id=1, source_target_pairs={{0,96},{1,97},{2,98},{3,99},{4,100},{5,101},{6,102},{7,103},{8,104... | collective-permute-start | bytes 835592 | tf_op jit(solution)/shard_map/ppermute | solution.py:41
  92.4 12.1 %collective-permute-start.17 = (bf16[272,512]{1,0:T(8,128)(2,1)S(1)}, bf16[272,512]{1,0:T(8,128)(2,1)S(1)}, u32[]{:S(2)}, u32[]{:S(2)}) collective-permute-start(bf16[272,512]{1,0:T(8,128)(2,1)S(1)} %get-tuple-element.45), channel_id=1, source_target_pairs={{0,64},{1,65},{2,66},{3,67},{4,68},{5,69},{6,70},{7,71},{8,72},{9,... | collective-permute-start | bytes 835592 | tf_op jit(solution)/shard_map/ppermute | solution.py:41
  117.5 19.6 %collective-permute-start.28 = (bf16[256,512]{1,0:T(8,128)(2,1)S(1)}, bf16[256,512]{1,0:T(8,128)(2,1)S(1)}, u32[]{:S(2)}, u32[]{:S(2)}) collective-permute-start(bf16[256,512]{1,0:T(8,128)(2,1)S(1)} %shard_map.77.refs_8_), channel_id=1, source_target_pairs={{0,32},{1,33},{2,34},{3,35},{4,36},{5,37},{6,38},{7,39},{8,40},{9,... | collective-permute-start | bytes 786440 | tf_op jit(solution)/shard_map/ppermute | solution.py:41
  121.1 16.0 %collective-permute-start.29 = (bf16[256,512]{1,0:T(8,128)(2,1)S(1)}, bf16[256,512]{1,0:T(8,128)(2,1)S(1)}, u32[]{:S(2)}, u32[]{:S(2)}) collective-permute-start(bf16[256,512]{1,0:T(8,128)(2,1)S(1)} %shard_map.77.refs_8_), channel_id=1, source_target_pairs={{0,96},{1,97},{2,98},{3,99},{4,100},{5,101},{6,102},{7,103},{8,104... | collective-permute-start | bytes 786440 | tf_op jit(solution)/shard_map/ppermute | solution.py:41
  125.2 11.8 %collective-permute-start.25 = (bf16[256,128]{1,0:T(8,128)(2,1)S(1)}, bf16[256,128]{1,0:T(8,128)(2,1)S(1)}, u32[]{:S(2)}, u32[]{:S(2)}) collective-permute-start(bf16[256,128]{1,0:T(8,128)(2,1)S(1)} %collective-permute-done.24.refs_1_), channel_id=1, source_target_pairs={{0,2},{1,3},{2,4},{3,5},{4,6},{5,7},{6,0},{7,1},{8,10},{9,11},{10,... | collective-permute-start | bytes 196616 | tf_op jit(solution)/shard_map/ppermute | solution.py:41
  126.2 10.9 %collective-permute-start.26 = (bf16[256,128]{1,0:T(8,128)(2,1)S(1)}, bf16[256,128]{1,0:T(8,128)(2,1)S(1)}, u32[]{:S(2)}, u32[]{:S(2)}) collective-permute-start(bf16[256,128]{1,0:T(8,128)(2,1)S(1)} %collective-permute-done.24.refs_1_), channel_id=1, source_target_pairs={{0,6},{1,7},{2,0},{3,1},{4,2},{5,3},{6,4},{7,5},{8,14},{9,15},{10,... | collective-permute-start | bytes 196616 | tf_op jit(solution)/shard_map/ppermute | solution.py:41
  137.7 15.0 %collective-permute-start.30 = (bf16[2,256,256]{2,1,0:T(8,128)(2,1)S(1)}, bf16[2,256,256]{2,1,0:T(8,128)(2,1)S(1)}, u32[]{:S(2)}, u32[]{:S(2)}) collective-permute-start(bf16[2,256,256]{2,1,0:T(8,128)(2,1)S(1)} %shard_map.79.refs_0_), channel_id=1, source_target_pairs={{0,8},{1,9},{2,10},{3,11},{4,12},{5,13},{6,14},{7,15},{8,16},{9,17... | collective-permute-start | bytes 786440 | tf_op jit(solution)/shard_map/ppermute | solution.py:41
  139.5 16.0 %collective-permute-start.31 = (bf16[2,256,256]{2,1,0:T(8,128)(2,1)S(1)}, bf16[2,256,256]{2,1,0:T(8,128)(2,1)S(1)}, u32[]{:S(2)}, u32[]{:S(2)}) collective-permute-start(bf16[2,256,256]{2,1,0:T(8,128)(2,1)S(1)} %shard_map.79.refs_0_), channel_id=1, source_target_pairs={{0,24},{1,25},{2,26},{3,27},{4,28},{5,29},{6,30},{7,31},{8,0},{9,1... | collective-permute-start | bytes 786440 | tf_op jit(solution)/shard_map/ppermute | solution.py:41
  144.3 12.5 %collective-permute-start.32 = (bf16[2,256,256]{2,1,0:T(8,128)(2,1)S(1)}, bf16[2,256,256]{2,1,0:T(8,128)(2,1)S(1)}, u32[]{:S(2)}, u32[]{:S(2)}) collective-permute-start(bf16[2,256,256]{2,1,0:T(8,128)(2,1)S(1)} %shard_map.79.refs_0_), channel_id=1, source_target_pairs={{0,16},{1,17},{2,18},{3,19},{4,20},{5,21},{6,22},{7,23},{8,24},{9,... | collective-permute-start | bytes 786440 | tf_op jit(solution)/shard_map/ppermute | solution.py:41
  145.4 13.2 %collective-permute-start.37 = (bf16[256,512]{1,0:T(8,128)(2,1)S(1)}, bf16[256,512]{1,0:T(8,128)(2,1)S(1)}, u32[]{:S(2)}, u32[]{:S(2)}) collective-permute-start(bf16[256,512]{1,0:T(8,128)(2,1)S(1)} %shard_map.77.refs_8_), channel_id=1, source_target_pairs={{0,64},{1,65},{2,66},{3,67},{4,68},{5,69},{6,70},{7,71},{8,72},{9,... | collective-permute-start | bytes 786440 | tf_op jit(solution)/shard_map/ppermute | solution.py:41
  146.6 12.0 %collective-permute-start.33 = (bf16[2,256,256]{2,1,0:T(8,128)(2,1)S(1)}, bf16[2,256,256]{2,1,0:T(8,128)(2,1)S(1)}, u32[]{:S(2)}, u32[]{:S(2)}) collective-permute-start(bf16[2,256,256]{2,1,0:T(8,128)(2,1)S(1)} %shard_map.79.refs_0_), channel_id=1, source_target_pairs={{0,1},{1,0},{2,3},{3,2},{4,5},{5,4},{6,7},{7,6},{8,9},{9,8},{10,11... | collective-permute-start | bytes 786440 | tf_op jit(solution)/shard_map/ppermute | solution.py:41
  (20 other events, 114.6 us)

commit v5 on v4

--- a/solution.py
+++ b/solution.py
@@ -166,10 +166,10 @@
     rows = coded.shape[0] - 16
     power = coded[:rows, :].astype(jnp.float32)
     top = coded[rows:rows + 1, :].astype(jnp.float32) * (1.0 / 32768.0)
-    root = jnp.abs(power)
-    for _ in range(3):
-        root = jnp.sqrt(root)
-    return jnp.where(power < 0, -root, root) * top
+    size = jnp.abs(power)
+    root = lax.rsqrt(lax.rsqrt(size))
+    root = jnp.where(size < 1.1754944e-38, 0.0, root * lax.rsqrt(root) * top)
+    return jnp.where(power < 0, -root, root)
 
 
 def product(panel, basis, low, k):

time: 163 us -> 162 us (level)
  no operation moved by 1% of the time
where the time goes in v5:
time: 162 us
  starting transfers between devices  91.9 us (57%)
  waiting for transfers between devices  37.9 us (23%)
  Pallas kernels  29.3 us (18%)
  local copies, waits for them, and re-layouts  1.84 us (1%)
    ppermute x35, starting transfers between devices, shifted(): return lax.ppermute(value, AXES, permutation(target))  89 us
    ppermute x35, waiting for transfers between devices, shifted(): return lax.ppermute(value, AXES, permutation(target))  37.9 us
    pallas_call x1, Pallas kernels, covariance(): pl.pallas_call(covariance_kernel, out_shape=[jax.ShapeDtypeStruct((n, 4 *...  7.56 us
    pallas_call x1, Pallas kernels, rotate_some(): pl.pallas_call(rotate_some_kernel, out_shape=[jax.ShapeDtypeStruct((3, ro...  7.11 us
    pallas_call x1, Pallas kernels, rotate_last(): pl.pallas_call(rotate_last_kernel, out_shape=[jax.ShapeDtypeStruct((rows,...  3.88 us
  transfers between devices with their start and end apart: 38, of which 9 were waited for; matrix products, arithmetic and copies ran while one was open for 0% of the time, Pallas kernels for 11%

profile of v5, /device:TPU:1, one launch (start us, length us, event | category | flops | bytes accessed | tf_op | source)
XLA Modules:
  0.0 162.1 jit_solution(7510334902506930146)
XLA Ops:
  3.2 13.5 %collective-permute-start.1 = (bf16[768,128]{1,0:T(8,128)(2,1)S(1)}, bf16[768,128]{1,0:T(8,128)(2,1)S(1)}, u32[]{:S(2)}, u32[]{:S(2)}) collective-permute-start(bf16[768,128]{1,0:T(8,128)(2,1)S(1)} %get-tuple-element.32.refs_0_), channel_id=1, source_target_pairs={{0,32},{1,33},{2,34},{3,35},{4,36},{5,37},{6,38},{7,39},{8,40},{9,... | collective-permute-start | bytes 589832 | tf_op jit(solution)/shard_map/ppermute | solution.py:41
  22.7 3.5 %collective-permute-start.5 = (bf16[128,768]{1,0:T(8,128)(2,1)S(1)}, bf16[128,768]{1,0:T(8,128)(2,1)S(1)}, u32[]{:S(2)}, u32[]{:S(2)}) collective-permute-start(bf16[128,768]{1,0:T(8,128)(2,1)S(1)} %collective-permute-done.refs_1_), channel_id=1, source_target_pairs={{0,6},{1,7},{2,0},{3,1},{4,2},{5,3},{6,4},{7,5},{8,14},{9,15},{10,... | collective-permute-start | bytes 589832 | tf_op jit(solution)/shard_map/ppermute | solution.py:41
  26.2 2.7 %collective-permute-start.6 = (bf16[128,768]{1,0:T(8,128)(2,1)S(1)}, bf16[128,768]{1,0:T(8,128)(2,1)S(1)}, u32[]{:S(2)}, u32[]{:S(2)}) collective-permute-start(bf16[128,768]{1,0:T(8,128)(2,1)S(1)} %collective-permute-done.refs_1_), channel_id=1, source_target_pairs={{0,4},{1,5},{2,6},{3,7},{4,0},{5,1},{6,2},{7,3},{8,12},{9,13},{10,... | collective-permute-start | bytes 589832 | tf_op jit(solution)/shard_map/ppermute | solution.py:41
  30.6 10.7 %collective-permute-done.6.refs_4_ = bf16[128,768]{1,0:T(8,128)(2,1)S(1)} collective-permute-done((bf16[128,768]{1,0:T(8,128)(2,1)S(1)}, bf16[128,768]{1,0:T(8,128)(2,1)S(1)}, u32[]{:S(2)}, u32[]{:S(2)}) %collective-permute-start.6) | collective-permute-done | bytes 196640 | tf_op jit(solution)/shard_map/ppermute | solution.py:41
  43.0 3.2 %collective-permute-start.8 = (bf16[2,256,768]{2,1,0:T(8,128)(2,1)S(1)}, bf16[2,256,768]{2,1,0:T(8,128)(2,1)S(1)}, u32[]{:S(2)}, u32[]{:S(2)}) collective-permute-start(bf16[2,256,768]{2,1,0:T(8,128)(2,1)S(1)} %shard_map.69.refs_0_), channel_id=1, source_target_pairs={{0,24},{1,25},{2,26},{3,27},{4,28},{5,29},{6,30},{7,31},{8,0},{9,1... | collective-permute-start | bytes 2359304 | tf_op jit(solution)/shard_map/ppermute | solution.py:41
  46.2 5.2 %collective-permute-start.10 = (bf16[2,256,768]{2,1,0:T(8,128)(2,1)S(1)}, bf16[2,256,768]{2,1,0:T(8,128)(2,1)}, u32[]{:S(2)}, u32[]{:S(2)}) collective-permute-start(bf16[2,256,768]{2,1,0:T(8,128)(2,1)S(1)} %shard_map.69.refs_0_), channel_id=1, source_target_pairs={{0,1},{1,0},{2,3},{3,2},{4,5},{5,4},{6,7},{7,6},{8,9},{9,8},{10,11... | collective-permute-start | bytes 2359304 | tf_op jit(solution)/shard_map/ppermute | solution.py:41
  51.5 3.1 %collective-permute-start.13 = (bf16[4,768,128]{2,1,0:T(8,128)(2,1)S(1)}, bf16[4,768,128]{2,1,0:T(8,128)(2,1)}, u32[]{:S(2)}, u32[]{:S(2)}) collective-permute-start(bf16[4,768,128]{2,1,0:T(8,128)(2,1)S(1)} %shard_map.68.refs_8_), channel_id=1, source_target_pairs={{0,128},{1,129},{2,130},{3,131},{4,132},{5,133},{6,134},{7,135},{8... | collective-permute-start | bytes 2359304 | tf_op jit(solution)/shard_map/ppermute | solution.py:41
  54.5 4.5 %collective-permute-done.7.refs_1_ = bf16[2,256,768]{2,1,0:T(8,128)(2,1)S(1)} collective-permute-done((bf16[2,256,768]{2,1,0:T(8,128)(2,1)S(1)}, bf16[2,256,768]{2,1,0:T(8,128)(2,1)S(1)}, u32[]{:S(2)}, u32[]{:S(2)}) %collective-permute-start.7) | collective-permute-done | bytes 786464 | tf_op jit(solution)/shard_map/ppermute | solution.py:41
  59.1 5.6 %collective-permute-start.11 = (bf16[2,256,768]{2,1,0:T(8,128)(2,1)S(1)}, bf16[2,256,768]{2,1,0:T(8,128)(2,1)}, u32[]{:S(2)}, u32[]{:S(2)}) collective-permute-start(bf16[2,256,768]{2,1,0:T(8,128)(2,1)S(1)} %collective-permute-done.7.refs_1_), channel_id=1, source_target_pairs={{0,1},{1,0},{2,3},{3,2},{4,5},{5,4},{6,7},{7,6},{8,9},{9,8},{10,11... | collective-permute-start | bytes 2359304 | tf_op jit(solution)/shard_map/ppermute | solution.py:41
  68.4 4.2 %collective-permute-done.13.refs_8_.refs_9_ = bf16[4,768,128]{2,1,0:T(8,128)(2,1)} collective-permute-done((bf16[4,768,128]{2,1,0:T(8,128)(2,1)S(1)}, bf16[4,768,128]{2,1,0:T(8,128)(2,1)}, u32[]{:S(2)}, u32[]{:S(2)}) %collective-permute-start.13) | collective-permute-done | bytes 786464 | tf_op jit(solution)/shard_map/ppermute | solution.py:41
  72.6 7.1 %shard_map.70 = (f32[3,256,512]{2,1,0:T(8,128)}, bf16[3,272,512]{2,1,0:T(8,128)(2,1)}, f32[3,128,256]{2,1,0:T(8,128)S(1)}, bf16[3,144,256]{2,1,0:T(8,128)(2,1)S(1)}, f32[8,128]{1,0:T(8,128)S(1)}) custom-call(s32[5]{0:T(128)S(1)} %stack.23.where.refs_0_, bf16[2,256,768]{2,1,0:T(8,128)(2,1)S(1)} %shard_map.69.refs_0_, ...), custom_call_target="tpu_custom_call" | custom-call | flops 5000000000 | bytes 20000000 | tf_op jit(solution)/shard_map/pallas_call | solution.py:222
  82.6 3.9 %shard_map.73 = (f32[256,512]{1,0:T(8,128)S(1)}, bf16[272,512]{1,0:T(8,128)(2,1)S(1)}, bf16[272,512]{1,0:T(8,128)(2,1)S(1)}, bf16[272,512]{1,0:T(8,128)(2,1)S(1)...) custom-call(s32[5]{0:T(128)S(1)} %stack.23.where.refs_0_, ...), custom_call_target="tpu_custom_call" | custom-call | flops 1000 | bytes 1000 | tf_op jit(solution)/shard_map/pallas_call | solution.py:298
  86.5 3.2 %collective-permute-start.18 = (bf16[4,144,256]{2,1,0:T(8,128)(2,1)S(1)}, bf16[4,144,256]{2,1,0:T(8,128)(2,1)S(1)}, u32[]{:S(2)}, u32[]{:S(2)}) collective-permute-start(bf16[4,144,256]{2,1,0:T(8,128)(2,1)S(1)} %get-tuple-element.47), channel_id=1, source_target_pairs={{0,128},{1,129},{2,130},{3,131},{4,132},{5,133},{6,134},{7,135},{8... | collective-permute-start | bytes 884744 | tf_op jit(solution)/shard_map/ppermute | solution.py:41
  89.7 2.7 %collective-permute-start.16 = (bf16[272,512]{1,0:T(8,128)(2,1)S(1)}, bf16[272,512]{1,0:T(8,128)(2,1)S(1)}, u32[]{:S(2)}, u32[]{:S(2)}) collective-permute-start(bf16[272,512]{1,0:T(8,128)(2,1)S(1)} %get-tuple-element.44), channel_id=1, source_target_pairs={{0,96},{1,97},{2,98},{3,99},{4,100},{5,101},{6,102},{7,103},{8,104... | collective-permute-start | bytes 835592 | tf_op jit(solution)/shard_map/ppermute | solution.py:41
  92.4 4.4 %collective-permute-done.18.arrived = bf16[4,144,256]{2,1,0:T(8,128)(2,1)S(1)} collective-permute-done((bf16[4,144,256]{2,1,0:T(8,128)(2,1)S(1)}, bf16[4,144,256]{2,1,0:T(8,128)(2,1)S(1)}, u32[]{:S(2)}, u32[]{:S(2)}) %collective-permute-start.18) | collective-permute-done | bytes 294944 | tf_op jit(solution)/shard_map/ppermute | solution.py:41
  97.2 7.2 %collective-permute-done.15.refs_0_ = bf16[272,512]{1,0:T(8,128)(2,1)S(1)} collective-permute-done((bf16[272,512]{1,0:T(8,128)(2,1)S(1)}, bf16[272,512]{1,0:T(8,128)(2,1)S(1)}, u32[]{:S(2)}, u32[]{:S(2)}) %collective-permute-start.15) | collective-permute-done | bytes 278560 | tf_op jit(solution)/shard_map/ppermute | solution.py:41
  111.2 3.6 %collective-permute-done.23.refs_2_ = bf16[144,256]{1,0:T(8,128)(2,1)S(1)} collective-permute-done((bf16[144,256]{1,0:T(8,128)(2,1)S(1)}, bf16[144,256]{1,0:T(8,128)(2,1)S(1)}, u32[]{:S(2)}, u32[]{:S(2)}) %collective-permute-start.23) | collective-permute-done | bytes 73760 | tf_op jit(solution)/shard_map/ppermute | solution.py:41
  116.7 3.6 %collective-permute-start.28 = (bf16[256,512]{1,0:T(8,128)(2,1)S(1)}, bf16[256,512]{1,0:T(8,128)(2,1)S(1)}, u32[]{:S(2)}, u32[]{:S(2)}) collective-permute-start(bf16[256,512]{1,0:T(8,128)(2,1)S(1)} %shard_map.77.refs_8_), channel_id=1, source_target_pairs={{0,32},{1,33},{2,34},{3,35},{4,36},{5,37},{6,38},{7,39},{8,40},{9,... | collective-permute-start | bytes 786440 | tf_op jit(solution)/shard_map/ppermute | solution.py:41
  120.3 4.1 %collective-permute-start.29 = (bf16[256,512]{1,0:T(8,128)(2,1)S(1)}, bf16[256,512]{1,0:T(8,128)(2,1)S(1)}, u32[]{:S(2)}, u32[]{:S(2)}) collective-permute-start(bf16[256,512]{1,0:T(8,128)(2,1)S(1)} %shard_map.77.refs_8_), channel_id=1, source_target_pairs={{0,96},{1,97},{2,98},{3,99},{4,100},{5,101},{6,102},{7,103},{8,104... | collective-permute-start | bytes 786440 | tf_op jit(solution)/shard_map/ppermute | solution.py:41
  128.6 7.6 %shard_map.72 = (f32[256,1024]{1,0:T(8,128)}, f32[512,2048]{1,0:T(8,128)}, f32[8,128]{1,0:T(8,128)S(1)}) custom-call(s32[5]{0:T(128)S(1)} %stack.23.where.refs_0_, bf16[2,256,768]{2,1,0:T(8,128)(2,1)S(1)} %shard_map.69.refs_0_, bf16[2,256,768]{2,1,0:T(8,128)(2,1)S(1)} %collective-permute-done.7.refs_1_, ...), custom_call_target="tpu_custom_call" | custom-call | flops 5000000000 | bytes 20000000 | tf_op jit(solution)/shard_map/pallas_call | solution.py:371
  138.7 4.8 %collective-permute-start.31 = (bf16[2,256,256]{2,1,0:T(8,128)(2,1)S(1)}, bf16[2,256,256]{2,1,0:T(8,128)(2,1)S(1)}, u32[]{:S(2)}, u32[]{:S(2)}) collective-permute-start(bf16[2,256,256]{2,1,0:T(8,128)(2,1)S(1)} %shard_map.79.refs_0_), channel_id=1, source_target_pairs={{0,24},{1,25},{2,26},{3,27},{4,28},{5,29},{6,30},{7,31},{8,0},{9,1... | collective-permute-start | bytes 786440 | tf_op jit(solution)/shard_map/ppermute | solution.py:41
  145.7 6.2 %collective-permute-start.33 = (bf16[2,256,256]{2,1,0:T(8,128)(2,1)S(1)}, bf16[2,256,256]{2,1,0:T(8,128)(2,1)S(1)}, u32[]{:S(2)}, u32[]{:S(2)}) collective-permute-start(bf16[2,256,256]{2,1,0:T(8,128)(2,1)S(1)} %shard_map.79.refs_0_), channel_id=1, source_target_pairs={{0,1},{1,0},{2,3},{3,2},{4,5},{5,4},{6,7},{7,6},{8,9},{9,8},{10,11... | collective-permute-start | bytes 786440 | tf_op jit(solution)/shard_map/ppermute | solution.py:41
  151.9 2.7 %collective-permute-start.34 = (bf16[2,256,256]{2,1,0:T(8,128)(2,1)S(1)}, bf16[2,256,256]{2,1,0:T(8,128)(2,1)S(1)}, u32[]{:S(2)}, u32[]{:S(2)}) collective-permute-start(bf16[2,256,256]{2,1,0:T(8,128)(2,1)S(1)} %collective-permute-done.30.refs_1_), channel_id=1, source_target_pairs={{0,1},{1,0},{2,3},{3,2},{4,5},{5,4},{6,7},{7,6},{8,9},{9,8},{10,11... | collective-permute-start | bytes 786440 | tf_op jit(solution)/shard_map/ppermute | solution.py:41
  158.9 3.0 %shard_map.80 = f32[1024,512]{1,0:T(8,128)} custom-call(s32[5]{0:T(128)S(1)} %stack.23.where.refs_0_, bf16[2,256,256]{2,1,0:T(8,128)(2,1)S(1)} %shard_map.79.refs_0_, bf16[2,256,256]{2,1,0:T(8,128)(2,1)S(1)} %collective-permute-done.30.refs_1_, bf16[2,256,256]{2,1,0:T(8,128)(2,1)S(1)} %collective-permute-done.31.refs_2_, ...), custom_call_target="tpu_custom_call" | custom-call | flops 1000 | bytes 1000 | tf_op jit(solution)/shard_map/pallas_call | solution.py:430
  (80 shorter events, 40.8 us)
Async XLA Ops:
  3.2 23.0 %collective-permute-start.1 = (bf16[768,128]{1,0:T(8,128)(2,1)S(1)}, bf16[768,128]{1,0:T(8,128)(2,1)S(1)}, u32[]{:S(2)}, u32[]{:S(2)}) collective-permute-start(bf16[768,128]{1,0:T(8,128)(2,1)S(1)} %get-tuple-element.32.refs_0_), channel_id=1, source_target_pairs={{0,32},{1,33},{2,34},{3,35},{4,36},{5,37},{6,38},{7,39},{8,40},{9,... | collective-permute-start | bytes 589832 | tf_op jit(solution)/shard_map/ppermute | solution.py:41
  16.7 12.2 %collective-permute-start.2 = (bf16[768,128]{1,0:T(8,128)(2,1)S(1)}, bf16[768,128]{1,0:T(8,128)(2,1)S(1)}, u32[]{:S(2)}, u32[]{:S(2)}) collective-permute-start(bf16[768,128]{1,0:T(8,128)(2,1)S(1)} %get-tuple-element.32.refs_0_), channel_id=1, source_target_pairs={{0,96},{1,97},{2,98},{3,99},{4,100},{5,101},{6,102},{7,103},{8,104... | collective-permute-start | bytes 589832 | tf_op jit(solution)/shard_map/ppermute | solution.py:41
  19.3 9.7 %collective-permute-start.3 = (bf16[768,128]{1,0:T(8,128)(2,1)S(1)}, bf16[768,128]{1,0:T(8,128)(2,1)S(1)}, u32[]{:S(2)}, u32[]{:S(2)}) collective-permute-start(bf16[768,128]{1,0:T(8,128)(2,1)S(1)} %get-tuple-element.32.refs_0_), channel_id=1, source_target_pairs={{0,64},{1,65},{2,66},{3,67},{4,68},{5,69},{6,70},{7,71},{8,72},{9,... | collective-permute-start | bytes 589832 | tf_op jit(solution)/shard_map/ppermute | solution.py:41
  20.5 10.1 %collective-permute-start.4 = (bf16[128,768]{1,0:T(8,128)(2,1)S(1)}, bf16[128,768]{1,0:T(8,128)(2,1)S(1)}, u32[]{:S(2)}, u32[]{:S(2)}) collective-permute-start(bf16[128,768]{1,0:T(8,128)(2,1)S(1)} %collective-permute-done.refs_1_), channel_id=1, source_target_pairs={{0,2},{1,3},{2,4},{3,5},{4,6},{5,7},{6,0},{7,1},{8,10},{9,11},{10,... | collective-permute-start | bytes 589832 | tf_op jit(solution)/shard_map/ppermute | solution.py:41
  26.2 15.1 %collective-permute-start.6 = (bf16[128,768]{1,0:T(8,128)(2,1)S(1)}, bf16[128,768]{1,0:T(8,128)(2,1)S(1)}, u32[]{:S(2)}, u32[]{:S(2)}) collective-permute-start(bf16[128,768]{1,0:T(8,128)(2,1)S(1)} %collective-permute-done.refs_1_), channel_id=1, source_target_pairs={{0,4},{1,5},{2,6},{3,7},{4,0},{5,1},{6,2},{7,3},{8,12},{9,13},{10,... | collective-permute-start | bytes 589832 | tf_op jit(solution)/shard_map/ppermute | solution.py:41
  42.9 16.2 %collective-permute-start.7 = (bf16[2,256,768]{2,1,0:T(8,128)(2,1)S(1)}, bf16[2,256,768]{2,1,0:T(8,128)(2,1)S(1)}, u32[]{:S(2)}, u32[]{:S(2)}) collective-permute-start(bf16[2,256,768]{2,1,0:T(8,128)(2,1)S(1)} %shard_map.69.refs_0_), channel_id=1, source_target_pairs={{0,8},{1,9},{2,10},{3,11},{4,12},{5,13},{6,14},{7,15},{8,16},{9,17... | collective-permute-start | bytes 2359304 | tf_op jit(solution)/shard_map/ppermute | solution.py:41
  43.0 21.6 %collective-permute-start.8 = (bf16[2,256,768]{2,1,0:T(8,128)(2,1)S(1)}, bf16[2,256,768]{2,1,0:T(8,128)(2,1)S(1)}, u32[]{:S(2)}, u32[]{:S(2)}) collective-permute-start(bf16[2,256,768]{2,1,0:T(8,128)(2,1)S(1)} %shard_map.69.refs_0_), channel_id=1, source_target_pairs={{0,24},{1,25},{2,26},{3,27},{4,28},{5,29},{6,30},{7,31},{8,0},{9,1... | collective-permute-start | bytes 2359304 | tf_op jit(solution)/shard_map/ppermute | solution.py:41
  46.2 22.2 %collective-permute-start.10 = (bf16[2,256,768]{2,1,0:T(8,128)(2,1)S(1)}, bf16[2,256,768]{2,1,0:T(8,128)(2,1)}, u32[]{:S(2)}, u32[]{:S(2)}) collective-permute-start(bf16[2,256,768]{2,1,0:T(8,128)(2,1)S(1)} %shard_map.69.refs_0_), channel_id=1, source_target_pairs={{0,1},{1,0},{2,3},{3,2},{4,5},{5,4},{6,7},{7,6},{8,9},{9,8},{10,11... | collective-permute-start | bytes 2359304 | tf_op jit(solution)/shard_map/ppermute | solution.py:41
  51.5 21.1 %collective-permute-start.13 = (bf16[4,768,128]{2,1,0:T(8,128)(2,1)S(1)}, bf16[4,768,128]{2,1,0:T(8,128)(2,1)}, u32[]{:S(2)}, u32[]{:S(2)}) collective-permute-start(bf16[4,768,128]{2,1,0:T(8,128)(2,1)S(1)} %shard_map.68.refs_8_), channel_id=1, source_target_pairs={{0,128},{1,129},{2,130},{3,131},{4,132},{5,133},{6,134},{7,135},{8... | collective-permute-start | bytes 2359304 | tf_op jit(solution)/shard_map/ppermute | solution.py:41
  59.1 13.5 %collective-permute-start.11 = (bf16[2,256,768]{2,1,0:T(8,128)(2,1)S(1)}, bf16[2,256,768]{2,1,0:T(8,128)(2,1)}, u32[]{:S(2)}, u32[]{:S(2)}) collective-permute-start(bf16[2,256,768]{2,1,0:T(8,128)(2,1)S(1)} %collective-permute-done.7.refs_1_), channel_id=1, source_target_pairs={{0,1},{1,0},{2,3},{3,2},{4,5},{5,4},{6,7},{7,6},{8,9},{9,8},{10,11... | collective-permute-start | bytes 2359304 | tf_op jit(solution)/shard_map/ppermute | solution.py:41
  66.9 12.8 %collective-permute-start.9 = (bf16[2,256,768]{2,1,0:T(8,128)(2,1)S(1)}, bf16[2,256,768]{2,1,0:T(8,128)(2,1)S(1)}, u32[]{:S(2)}, u32[]{:S(2)}) collective-permute-start(bf16[2,256,768]{2,1,0:T(8,128)(2,1)S(1)} %broadcast_select_fusion), channel_id=1, source_target_pairs={{0,24},{1,9},{2,26},{3,11},{4,28},{5,13},{6,30},{7,15},{8,0},{9,17... | collective-permute-start | bytes 2359304 | tf_op jit(solution)/shard_map/ppermute | solution.py:52
  86.5 10.3 %collective-permute-start.18 = (bf16[4,144,256]{2,1,0:T(8,128)(2,1)S(1)}, bf16[4,144,256]{2,1,0:T(8,128)(2,1)S(1)}, u32[]{:S(2)}, u32[]{:S(2)}) collective-permute-start(bf16[4,144,256]{2,1,0:T(8,128)(2,1)S(1)} %get-tuple-element.47), channel_id=1, source_target_pairs={{0,128},{1,129},{2,130},{3,131},{4,132},{5,133},{6,134},{7,135},{8... | collective-permute-start | bytes 884744 | tf_op jit(solution)/shard_map/ppermute | solution.py:41
  89.7 14.7 %collective-permute-start.15 = (bf16[272,512]{1,0:T(8,128)(2,1)S(1)}, bf16[272,512]{1,0:T(8,128)(2,1)S(1)}, u32[]{:S(2)}, u32[]{:S(2)}) collective-permute-start(bf16[272,512]{1,0:T(8,128)(2,1)S(1)} %get-tuple-element.43), channel_id=1, source_target_pairs={{0,32},{1,33},{2,34},{3,35},{4,36},{5,37},{6,38},{7,39},{8,40},{9,... | collective-permute-start | bytes 835592 | tf_op jit(solution)/shard_map/ppermute | solution.py:41
  89.7 14.7 %collective-permute-start.16 = (bf16[272,512]{1,0:T(8,128)(2,1)S(1)}, bf16[272,512]{1,0:T(8,128)(2,1)S(1)}, u32[]{:S(2)}, u32[]{:S(2)}) collective-permute-start(bf16[272,512]{1,0:T(8,128)(2,1)S(1)} %get-tuple-element.44), channel_id=1, source_target_pairs={{0,96},{1,97},{2,98},{3,99},{4,100},{5,101},{6,102},{7,103},{8,104... | collective-permute-start | bytes 835592 | tf_op jit(solution)/shard_map/ppermute | solution.py:41
  92.4 12.1 %collective-permute-start.17 = (bf16[272,512]{1,0:T(8,128)(2,1)S(1)}, bf16[272,512]{1,0:T(8,128)(2,1)S(1)}, u32[]{:S(2)}, u32[]{:S(2)}) collective-permute-start(bf16[272,512]{1,0:T(8,128)(2,1)S(1)} %get-tuple-element.45), channel_id=1, source_target_pairs={{0,64},{1,65},{2,66},{3,67},{4,68},{5,69},{6,70},{7,71},{8,72},{9,... | collective-permute-start | bytes 835592 | tf_op jit(solution)/shard_map/ppermute | solution.py:41
  116.7 19.6 %collective-permute-start.28 = (bf16[256,512]{1,0:T(8,128)(2,1)S(1)}, bf16[256,512]{1,0:T(8,128)(2,1)S(1)}, u32[]{:S(2)}, u32[]{:S(2)}) collective-permute-start(bf16[256,512]{1,0:T(8,128)(2,1)S(1)} %shard_map.77.refs_8_), channel_id=1, source_target_pairs={{0,32},{1,33},{2,34},{3,35},{4,36},{5,37},{6,38},{7,39},{8,40},{9,... | collective-permute-start | bytes 786440 | tf_op jit(solution)/shard_map/ppermute | solution.py:41
  120.3 16.0 %collective-permute-start.29 = (bf16[256,512]{1,0:T(8,128)(2,1)S(1)}, bf16[256,512]{1,0:T(8,128)(2,1)S(1)}, u32[]{:S(2)}, u32[]{:S(2)}) collective-permute-start(bf16[256,512]{1,0:T(8,128)(2,1)S(1)} %shard_map.77.refs_8_), channel_id=1, source_target_pairs={{0,96},{1,97},{2,98},{3,99},{4,100},{5,101},{6,102},{7,103},{8,104... | collective-permute-start | bytes 786440 | tf_op jit(solution)/shard_map/ppermute | solution.py:41
  124.3 11.8 %collective-permute-start.25 = (bf16[256,128]{1,0:T(8,128)(2,1)S(1)}, bf16[256,128]{1,0:T(8,128)(2,1)S(1)}, u32[]{:S(2)}, u32[]{:S(2)}) collective-permute-start(bf16[256,128]{1,0:T(8,128)(2,1)S(1)} %collective-permute-done.24.refs_1_), channel_id=1, source_target_pairs={{0,2},{1,3},{2,4},{3,5},{4,6},{5,7},{6,0},{7,1},{8,10},{9,11},{10,... | collective-permute-start | bytes 196616 | tf_op jit(solution)/shard_map/ppermute | solution.py:41
  125.3 10.9 %collective-permute-start.26 = (bf16[256,128]{1,0:T(8,128)(2,1)S(1)}, bf16[256,128]{1,0:T(8,128)(2,1)S(1)}, u32[]{:S(2)}, u32[]{:S(2)}) collective-permute-start(bf16[256,128]{1,0:T(8,128)(2,1)S(1)} %collective-permute-done.24.refs_1_), channel_id=1, source_target_pairs={{0,6},{1,7},{2,0},{3,1},{4,2},{5,3},{6,4},{7,5},{8,14},{9,15},{10,... | collective-permute-start | bytes 196616 | tf_op jit(solution)/shard_map/ppermute | solution.py:41
  136.9 15.0 %collective-permute-start.30 = (bf16[2,256,256]{2,1,0:T(8,128)(2,1)S(1)}, bf16[2,256,256]{2,1,0:T(8,128)(2,1)S(1)}, u32[]{:S(2)}, u32[]{:S(2)}) collective-permute-start(bf16[2,256,256]{2,1,0:T(8,128)(2,1)S(1)} %shard_map.79.refs_0_), channel_id=1, source_target_pairs={{0,8},{1,9},{2,10},{3,11},{4,12},{5,13},{6,14},{7,15},{8,16},{9,17... | collective-permute-start | bytes 786440 | tf_op jit(solution)/shard_map/ppermute | solution.py:41
  138.7 16.0 %collective-permute-start.31 = (bf16[2,256,256]{2,1,0:T(8,128)(2,1)S(1)}, bf16[2,256,256]{2,1,0:T(8,128)(2,1)S(1)}, u32[]{:S(2)}, u32[]{:S(2)}) collective-permute-start(bf16[2,256,256]{2,1,0:T(8,128)(2,1)S(1)} %shard_map.79.refs_0_), channel_id=1, source_target_pairs={{0,24},{1,25},{2,26},{3,27},{4,28},{5,29},{6,30},{7,31},{8,0},{9,1... | collective-permute-start | bytes 786440 | tf_op jit(solution)/shard_map/ppermute | solution.py:41
  143.5 12.5 %collective-permute-start.32 = (bf16[2,256,256]{2,1,0:T(8,128)(2,1)S(1)}, bf16[2,256,256]{2,1,0:T(8,128)(2,1)S(1)}, u32[]{:S(2)}, u32[]{:S(2)}) collective-permute-start(bf16[2,256,256]{2,1,0:T(8,128)(2,1)S(1)} %shard_map.79.refs_0_), channel_id=1, source_target_pairs={{0,16},{1,17},{2,18},{3,19},{4,20},{5,21},{6,22},{7,23},{8,24},{9,... | collective-permute-start | bytes 786440 | tf_op jit(solution)/shard_map/ppermute | solution.py:41
  144.6 13.2 %collective-permute-start.37 = (bf16[256,512]{1,0:T(8,128)(2,1)S(1)}, bf16[256,512]{1,0:T(8,128)(2,1)S(1)}, u32[]{:S(2)}, u32[]{:S(2)}) collective-permute-start(bf16[256,512]{1,0:T(8,128)(2,1)S(1)} %shard_map.77.refs_8_), channel_id=1, source_target_pairs={{0,64},{1,65},{2,66},{3,67},{4,68},{5,69},{6,70},{7,71},{8,72},{9,... | collective-permute-start | bytes 786440 | tf_op jit(solution)/shard_map/ppermute | solution.py:41
  145.7 12.0 %collective-permute-start.33 = (bf16[2,256,256]{2,1,0:T(8,128)(2,1)S(1)}, bf16[2,256,256]{2,1,0:T(8,128)(2,1)S(1)}, u32[]{:S(2)}, u32[]{:S(2)}) collective-permute-start(bf16[2,256,256]{2,1,0:T(8,128)(2,1)S(1)} %shard_map.79.refs_0_), channel_id=1, source_target_pairs={{0,1},{1,0},{2,3},{3,2},{4,5},{5,4},{6,7},{7,6},{8,9},{9,8},{10,11... | collective-permute-start | bytes 786440 | tf_op jit(solution)/shard_map/ppermute | solution.py:41
  (20 other events, 114.5 us)
